TPU v7x, 32 devices: a whole 2x2x4 slice. The times are simulated.
32 devices in a mesh: dp: 4 (over y, x), strip: 2 (over core), tensor: 4 (over z).
Axes of the slice: x: 2, y: 2, z: 4, core: 2. Of those that a mesh axis runs over, the one named last changes fastest.
Arguments:
- res_code: int32 [12], P('dp'), may hold values from 768 to 1536, as said below
- vit_in: float32 [12, 24, 24, 1024], P('dp', 'strip'), may hold values from -6 to 6
- map_in: bfloat16 [12, 48, 48, 1536], P('dp', 'strip', 'tensor'), may hold values from -6 to 6
- dw_kernel: float32 [1536, 49], replicated, may hold values from -0.875 to 0.875
- conv_gain: float32 [1536], replicated, may hold values from 0.5 to 1.5
- conv_bias: float32 [1536], replicated, may hold values from -3 to 3
- w_expand: bfloat16 [1536, 6144], P(('strip', 'tensor')), may hold values from -0.15625 to 0.15625
- w_reduce: bfloat16 [1536, 6144], P(('strip', 'tensor')), may hold values from -0.078125 to 0.078125
- layer_scale: float32 [1536], replicated, may hold values from 0.5 to 1.5
- adapt_w: bfloat16 [1536, 1024], replicated, may hold values from -0.15625 to 0.15625
- mix_kernel: float32 [1024, 9], replicated, may hold values from -2 to 2
- gate_logit: float32 [1024], replicated, may hold values from -1.5 to 1.5
- gain_one: float32 [1024], replicated, may hold values from 0.5 to 1.5
- bias_one: float32 [1024], replicated, may hold values from -3 to 3
- w_qkv: bfloat16 [1024, 3, 1024], P(None, None, 'tensor'), may hold values from -0.1875 to 0.1875
- w_proj: bfloat16 [1024, 1024], P(None, 'tensor'), may hold values from -1.5 to 1.5
- gain_two: float32 [1024], replicated, may hold values from 0.5 to 1.5
- bias_two: float32 [1024], replicated, may hold values from -3 to 3
- w_up: bfloat16 [1024, 4096], P(None, 'tensor'), may hold values from -0.1875 to 0.1875
- w_down: bfloat16 [1024, 4096], P(None, 'tensor'), may hold values from -0.375 to 0.375
- d_vit: float32 [12, 24, 24, 1024], P('dp', 'strip'), may hold values from -6 to 6
- d_map: bfloat16 [12, 48, 48, 1536], P('dp', 'strip', 'tensor'), may hold values from -6 to 6
Outputs:
- vit_out: float32 [12, 24, 24, 1024], P('dp', 'strip')
- map_out: bfloat16 [12, 48, 48, 1536], P('dp', 'strip', 'tensor')
- grad_vit_in: float32 [12, 24, 24, 1024], P('dp', 'strip')
- grad_map_in: float32 [12, 48, 48, 1536], P('dp', 'strip', 'tensor')
- grad_dw_kernel: float32 [1536, 49], P(('strip', 'tensor'))
- grad_conv_gain: float32 [1536], P(('strip', 'tensor'))
- grad_conv_bias: float32 [1536], P(('strip', 'tensor'))
- grad_w_expand: float32 [1536, 6144], P(('strip', 'tensor'))
- grad_w_reduce: float32 [1536, 6144], P(('strip', 'tensor'))
- grad_layer_scale: float32 [1536], P(('strip', 'tensor'))
- grad_adapt_w: float32 [1536, 1024], P(('dp', 'strip'))
- grad_mix_kernel: float32 [1024, 9], P(('dp', 'strip'))
- grad_gate_logit: float32 [1024], P(('dp', 'strip'))
- grad_gain_one: float32 [1024], P(('dp', 'strip'))
- grad_bias_one: float32 [1024], P(('dp', 'strip'))
- grad_w_qkv: float32 [1024, 3, 1024], P(('dp', 'strip'), None, 'tensor')
- grad_w_proj: float32 [1024, 1024], P(('dp', 'strip'), 'tensor')
- grad_gain_two: float32 [1024], P(('dp', 'strip'))
- grad_bias_two: float32 [1024], P(('dp', 'strip'))
- grad_w_up: float32 [1024, 4096], P(('dp', 'strip'), 'tensor')
- grad_w_down: float32 [1024, 4096], P(('dp', 'strip'), 'tensor')
Inputs may be any that keep to these rules, and one draw needn't show every extreme that they name: `res_code`: each entry is 768, 1024 or 1536 (maps of 24, 32 or 48 cells a side); 1536 occurs in every draw.
All inputs are finite; a program needn't handle non-finite values.
Results may differ from a plain program's by a relative error of at most 0.024.
Values may be sent and summed in bfloat16 or wider, within the bound.
No kernel may reach another device: no remote copies, remote signals or barrier semaphores. Data moves between devices by JAX's collectives and lax.ppermute only.
A program may use at most 384 MiB of HBM per device.

v0:
```python
import jax
import jax.numpy as jnp
from jax import lax
from jax.sharding import PartitionSpec as P

HD = 64
G = 24
MAXS = 48
MB = 3


EPS = 1e-06
HIGH = lax.Precision.HIGHEST
DOWN_ROWS = (((0,), (0,)), ((), ()))
ACROSS = (((1,), (1,)), ((), ()))


def with_halo(cells, sides, width):
    for axis, dim in sides:
        count = lax.axis_size(axis)
        ends = count - 1
        head = lax.slice_in_dim(cells, 0, width, axis=dim)
        tail = lax.slice_in_dim(cells, cells.shape[dim] - width, cells.shape[dim], axis=dim)
        cells = jnp.concatenate(
            [
                lax.ppermute(tail, axis, [(i, (i + 1) % count) for i in range(ends)]),
                cells,
                lax.ppermute(head, axis, [((i + 1) % count, i) for i in range(ends)]),
            ],
            axis=dim,
        )
    return cells


def layer_norm(values, gain, bias):
    center = jnp.mean(values, axis=-1, keepdims=True)
    shifted = values - center
    spread_sq = jnp.mean(shifted * shifted, axis=-1, keepdims=True)
    return shifted * lax.rsqrt(spread_sq + EPS) * gain + bias


def depthwise(padded, kernel, reach, rows, cols):
    summed = jnp.zeros(padded.shape[:-3] + (rows, cols, padded.shape[-1]), jnp.float32)
    for row_off in range(reach):
        for col_off in range(reach):
            summed = (
                summed
                + padded[..., row_off : row_off + rows, col_off : col_off + cols, :]
                * kernel[:, row_off * reach + col_off]
            )
    return summed


def kernel_grad(padded, gradient, reach, rows, cols):
    columns = []
    for row_off in range(reach):
        for col_off in range(reach):
            window = padded[..., row_off : row_off + rows, col_off : col_off + cols, :]
            columns.append(jnp.sum(window * gradient, axis=(0, 1, 2)))
    return jnp.stack(columns, axis=1)


def gelu_exact(values):
    return jax.nn.gelu(values, approximate=False)


def pool_matrix(pooled_index, buffer_index, map_side, offset):
    map_place = buffer_index[None, :] - offset
    bin_start = pooled_index[:, None] * map_side // G
    bin_stop = ((pooled_index[:, None] + 1) * map_side + G - 1) // G
    inside = jnp.logical_and(map_place >= bin_start, map_place < bin_stop)
    return jnp.where(inside, 1.0, 0.0).astype(jnp.float32) / (bin_stop - bin_start).astype(
        jnp.float32
    )


def add_trees(first_tree, second_tree):
    return tuple(
        (first_part + second_part for first_part, second_part in zip(first_tree, second_tree))
    )


def shards(
    res_code,
    vit_in,
    map_in,
    dw_kernel,
    conv_gain,
    conv_bias,
    w_expand,
    w_reduce,
    layer_scale,
    adapt_w,
    mix_kernel,
    gate_logit,
    gain_one,
    bias_one,
    w_qkv,
    w_proj,
    gain_two,
    bias_two,
    w_up,
    w_down,
    d_vit,
    d_map,
):
    strip_at = lax.axis_index("strip")
    tensor_at = lax.axis_index("tensor")
    batch_items = vit_in.shape[0] // MB
    grid_rows = vit_in.shape[1]
    width = vit_in.shape[3]
    map_rows = map_in.shape[1]
    map_cols = map_in.shape[2]
    channels = map_in.shape[3]
    head_cols = w_qkv.shape[2]
    local_heads = head_cols // HD
    tokens = grid_rows * G
    score_scale = HD ** (-0.5)
    full_expand, full_reduce = (
        lax.all_gather(w_expand, ("strip", "tensor"), axis=0, tiled=True),
        lax.all_gather(w_reduce, ("strip", "tensor"), axis=0, tiled=True),
    )
    hidden_cols = full_expand.shape[1]
    row_cells = strip_at * map_rows + jnp.arange(map_rows, dtype=jnp.int32)
    col_cells = tensor_at * map_cols + jnp.arange(map_cols, dtype=jnp.int32)
    pooled_rows = strip_at * grid_rows + jnp.arange(grid_rows, dtype=jnp.int32)
    grid_cols = jnp.arange(G, dtype=jnp.int32)
    gate_scale = jnp.tanh(gate_logit)
    flipped_seven = dw_kernel[:, ::-1]
    flipped_three = mix_kernel[:, ::-1]
    many_pools = jax.vmap(pool_matrix, in_axes=(None, None, 0, 0))
    conv_totals = (
        jnp.zeros((channels, dw_kernel.shape[1]), jnp.float32),
        jnp.zeros((channels,), jnp.float32),
        jnp.zeros((channels,), jnp.float32),
        jnp.zeros((channels, hidden_cols), jnp.float32),
        jnp.zeros((channels, hidden_cols), jnp.float32),
        jnp.zeros((channels,), jnp.float32),
    )
    vit_totals = tuple(
        (
            jnp.zeros(shape_one, jnp.float32)
            for shape_one in (
                w_qkv.shape,
                w_proj.shape,
                w_up.shape,
                w_down.shape,
                adapt_w.shape,
                mix_kernel.shape,
                gate_logit.shape,
                gain_one.shape,
                bias_one.shape,
                gain_two.shape,
                bias_two.shape,
            )
        )
    )
    vit_parts = []
    map_parts = []
    grad_vit_parts = []
    grad_map_parts = []
    for batch_at in range(MB):
        first_item = batch_at * batch_items
        item_codes = res_code[first_item : first_item + batch_items]
        map_side = item_codes // 32
        offset = (MAXS - map_side) // 2
        row_ok = jnp.logical_and(
            row_cells[None, :] >= offset[:, None], row_cells[None, :] < (offset + map_side)[:, None]
        ).astype(jnp.float32)
        col_ok = jnp.logical_and(
            col_cells[None, :] >= offset[:, None], col_cells[None, :] < (offset + map_side)[:, None]
        ).astype(jnp.float32)
        cell_mask = row_ok[:, :, None, None] * col_ok[:, None, :, None]
        masked = map_in[first_item : first_item + batch_items] * cell_mask.astype(jnp.bfloat16)
        padded = with_halo(masked, (("strip", 1), ("tensor", 2)), 3)
        padded_full = padded.astype(jnp.float32)
        spread = depthwise(padded_full, dw_kernel, 7, map_rows, map_cols)
        normed, norm_pull = jax.vjp(layer_norm, spread, conv_gain, conv_bias)
        normed_low = normed.astype(jnp.bfloat16).reshape(-1, channels)
        hidden = jnp.dot(normed_low, full_expand, preferred_element_type=jnp.float32)
        active, gelu_pull = jax.vjp(gelu_exact, hidden)
        active_low = active.astype(jnp.bfloat16)
        branch = lax.dot_general(
            active_low, full_reduce, ACROSS, preferred_element_type=jnp.float32
        ).reshape(masked.shape)
        masked_full = masked.astype(jnp.float32)
        map_value = cell_mask * (masked_full + layer_scale * branch)
        map_parts.append(map_value.astype(jnp.bfloat16))
        row_pool = many_pools(pooled_rows, row_cells, map_side, offset)
        col_pool = many_pools(grid_cols, col_cells, map_side, offset)
        pooled_part = jnp.einsum("bir,brcd->bicd", row_pool, map_value, precision=HIGH)
        pooled_part = jnp.einsum("bjc,bicd->bijd", col_pool, pooled_part, precision=HIGH)
        pooled = lax.psum(pooled_part, "tensor")
        pooled_low = pooled.astype(jnp.bfloat16).reshape(-1, channels)
        adapted = jnp.dot(pooled_low, adapt_w, preferred_element_type=jnp.float32).reshape(
            batch_items, grid_rows, G, width
        )
        adapted_rim = with_halo(adapted, (("strip", 1),), 1)
        adapted_pad = jnp.pad(adapted_rim, ((0, 0), (0, 0), (1, 1), (0, 0)))
        local_mix = depthwise(adapted_pad, mix_kernel, 3, grid_rows, G)
        joined_rows = (
            vit_in[first_item : first_item + batch_items] + gate_scale * local_mix
        ).reshape(-1, width)
        normed_one, norm_one_pull = jax.vjp(layer_norm, joined_rows, gain_one, bias_one)
        normed_one_low = normed_one.astype(jnp.bfloat16)
        qkv_rows = jnp.einsum(
            "td,dkh->tkh", normed_one_low, w_qkv, preferred_element_type=jnp.float32
        ).astype(jnp.bfloat16)
        qkv_view = qkv_rows.reshape(batch_items, tokens, 3, local_heads, HD)
        queries = qkv_view[:, :, 0]
        keys_all, values_all = (
            lax.all_gather(qkv_view[:, :, 1], "strip", axis=1, tiled=True),
            lax.all_gather(qkv_view[:, :, 2], "strip", axis=1, tiled=True),
        )
        scores = (
            jnp.einsum("bqhe,bkhe->bhqk", queries, keys_all, preferred_element_type=jnp.float32)
            * score_scale
        )
        log_total = jax.nn.logsumexp(scores, axis=-1, keepdims=True)
        attn_probs = jnp.exp(scores - log_total)
        probs_low = attn_probs.astype(jnp.bfloat16)
        mixed_heads = (
            jnp.einsum("bhqk,bkhe->bqhe", probs_low, values_all, preferred_element_type=jnp.float32)
            .astype(jnp.bfloat16)
            .reshape(-1, head_cols)
        )
        attn_part = lax.dot_general(mixed_heads, w_proj, ACROSS, preferred_element_type=jnp.float32)
        attn_out = lax.psum(attn_part, "tensor")
        after_attn = joined_rows + attn_out
        normed_two, norm_two_pull = jax.vjp(layer_norm, after_attn, gain_two, bias_two)
        normed_two_low = normed_two.astype(jnp.bfloat16)
        hidden_two = jnp.dot(normed_two_low, w_up, preferred_element_type=jnp.float32)
        active_two, gelu_two_pull = jax.vjp(gelu_exact, hidden_two)
        active_two_low = active_two.astype(jnp.bfloat16)
        mlp_part = lax.dot_general(
            active_two_low, w_down, ACROSS, preferred_element_type=jnp.float32
        )
        mlp_out = lax.psum(mlp_part, "tensor")
        vit_parts.append((after_attn + mlp_out).reshape(batch_items, grid_rows, G, width))
        grad_out = d_vit[first_item : first_item + batch_items].reshape(-1, width)
        grad_mlp_low = grad_out.astype(jnp.bfloat16)
        grad_down = lax.dot_general(
            grad_mlp_low, active_two_low, DOWN_ROWS, preferred_element_type=jnp.float32
        )
        grad_active_two = jnp.dot(grad_mlp_low, w_down, preferred_element_type=jnp.float32)
        grad_hidden_two = gelu_two_pull(grad_active_two)[0].astype(jnp.bfloat16)
        grad_up = lax.dot_general(
            normed_two_low, grad_hidden_two, DOWN_ROWS, preferred_element_type=jnp.float32
        )
        grad_normed_part = lax.dot_general(
            grad_hidden_two, w_up, ACROSS, preferred_element_type=jnp.float32
        )
        grad_normed_two = lax.psum(grad_normed_part, "tensor")
        grad_after_norm, grad_gain_two, grad_bias_two = norm_two_pull(grad_normed_two)
        grad_after = grad_out + grad_after_norm
        grad_attn_low = grad_after.astype(jnp.bfloat16)
        grad_proj = lax.dot_general(
            grad_attn_low, mixed_heads, DOWN_ROWS, preferred_element_type=jnp.float32
        )
        grad_mixed = (
            jnp.dot(grad_attn_low, w_proj, preferred_element_type=jnp.float32)
            .astype(jnp.bfloat16)
            .reshape(batch_items, tokens, local_heads, HD)
        )
        grad_probs = jnp.einsum(
            "bqhe,bkhe->bhqk", grad_mixed, values_all, preferred_element_type=jnp.float32
        )
        row_dot = jnp.sum(attn_probs * grad_probs, axis=-1, keepdims=True)
        grad_scores = (attn_probs * (grad_probs - row_dot)).astype(jnp.bfloat16)
        grad_queries = (
            jnp.einsum("bhqk,bkhe->bqhe", grad_scores, keys_all, preferred_element_type=jnp.float32)
            * score_scale
        )
        grad_keys_part = (
            jnp.einsum("bhqk,bqhe->bkhe", grad_scores, queries, preferred_element_type=jnp.float32)
            * score_scale
        )
        grad_values_part = jnp.einsum(
            "bhqk,bqhe->bkhe", probs_low, grad_mixed, preferred_element_type=jnp.float32
        )
        grad_keys, grad_values = (
            lax.psum_scatter(grad_keys_part, "strip", scatter_dimension=1, tiled=True),
            lax.psum_scatter(grad_values_part, "strip", scatter_dimension=1, tiled=True),
        )
        grad_qkv_low = (
            jnp.stack((grad_queries, grad_keys, grad_values), axis=2)
            .astype(jnp.bfloat16)
            .reshape(-1, 3, head_cols)
        )
        grad_qkv = jnp.einsum(
            "td,tkh->dkh", normed_one_low, grad_qkv_low, preferred_element_type=jnp.float32
        )
        grad_normed_one_part = jnp.einsum(
            "tkh,dkh->td", grad_qkv_low, w_qkv, preferred_element_type=jnp.float32
        )
        grad_normed_one = lax.psum(grad_normed_one_part, "tensor")
        grad_joined_norm, grad_gain_one, grad_bias_one = norm_one_pull(grad_normed_one)
        grad_joined = (grad_after + grad_joined_norm).reshape(batch_items, grid_rows, G, width)
        grad_vit_parts.append(grad_joined)
        grad_gate = jnp.sum(grad_joined * local_mix, axis=(0, 1, 2)) * (
            1.0 - gate_scale * gate_scale
        )
        grad_mix = grad_joined * gate_scale
        mix_rim = with_halo(grad_mix, (("strip", 1),), 1)
        mix_pad = jnp.pad(mix_rim, ((0, 0), (0, 0), (1, 1), (0, 0)))
        grad_adapted = (
            depthwise(mix_pad, flipped_three, 3, grid_rows, G)
            .astype(jnp.bfloat16)
            .reshape(-1, width)
        )
        grad_mix_kernel = kernel_grad(adapted_pad, grad_mix, 3, grid_rows, G)
        grad_adapt = lax.dot_general(
            pooled_low, grad_adapted, DOWN_ROWS, preferred_element_type=jnp.float32
        )
        grad_pooled = lax.dot_general(
            grad_adapted, adapt_w, ACROSS, preferred_element_type=jnp.float32
        ).reshape(batch_items, grid_rows, G, channels)
        back_rows = jnp.einsum("bjc,bijd->bicd", col_pool, grad_pooled, precision=HIGH)
        grad_map_value = d_map[first_item : first_item + batch_items].astype(
            jnp.float32
        ) + jnp.einsum("bir,bicd->brcd", row_pool, back_rows, precision=HIGH)
        kept_grad = cell_mask * grad_map_value
        grad_scale = jnp.sum(kept_grad * branch, axis=(0, 1, 2))
        grad_branch = (kept_grad * layer_scale).astype(jnp.bfloat16).reshape(-1, channels)
        grad_reduce = lax.dot_general(
            grad_branch, active_low, DOWN_ROWS, preferred_element_type=jnp.float32
        )
        grad_active = jnp.dot(grad_branch, full_reduce, preferred_element_type=jnp.float32)
        grad_hidden = gelu_pull(grad_active)[0].astype(jnp.bfloat16)
        grad_expand = lax.dot_general(
            normed_low, grad_hidden, DOWN_ROWS, preferred_element_type=jnp.float32
        )
        grad_normed = lax.dot_general(
            grad_hidden, full_expand, ACROSS, preferred_element_type=jnp.float32
        ).reshape(masked.shape)
        grad_spread, grad_gain_conv, grad_bias_conv = norm_pull(grad_normed)
        spread_rim = with_halo(grad_spread, (("strip", 1), ("tensor", 2)), 3)
        grad_masked = kept_grad + depthwise(spread_rim, flipped_seven, 7, map_rows, map_cols)
        grad_map_parts.append(cell_mask * grad_masked)
        grad_dw = kernel_grad(padded_full, grad_spread, 7, map_rows, map_cols)
        vit_terms = (
            grad_qkv,
            grad_proj,
            grad_up,
            grad_down,
            grad_adapt,
            grad_mix_kernel,
            grad_gate,
            grad_gain_one,
            grad_bias_one,
            grad_gain_two,
            grad_bias_two,
        )
        vit_totals = add_trees(vit_totals, vit_terms)
        conv_terms = (grad_dw, grad_gain_conv, grad_bias_conv, grad_expand, grad_reduce, grad_scale)
        conv_totals = add_trees(conv_totals, conv_terms)
    conv_owned = lax.psum_scatter(conv_totals, ("strip", "tensor"), scatter_dimension=0, tiled=True)
    conv_shares = lax.psum(conv_owned, "dp")
    vit_shares = lax.psum_scatter(vit_totals, ("dp", "strip"), scatter_dimension=0, tiled=True)
    return (
        jnp.concatenate(vit_parts, axis=0),
        jnp.concatenate(map_parts, axis=0),
        jnp.concatenate(grad_vit_parts, axis=0),
        jnp.concatenate(grad_map_parts, axis=0),
        conv_shares[0],
        conv_shares[1],
        conv_shares[2],
        conv_shares[3],
        conv_shares[4],
        conv_shares[5],
        vit_shares[4],
        vit_shares[5],
        vit_shares[6],
        vit_shares[7],
        vit_shares[8],
        vit_shares[0],
        vit_shares[1],
        vit_shares[9],
        vit_shares[10],
        vit_shares[2],
        vit_shares[3],
    )


def solution(mesh):
    in_specs = (
        P("dp"),
        P("dp", "strip", None, None),
        P("dp", "strip", "tensor", None),
        P(),
        P(),
        P(),
        P(("strip", "tensor"), None),
        P(("strip", "tensor"), None),
        P(),
        P(),
        P(),
        P(),
        P(),
        P(),
        P(None, None, "tensor"),
        P(None, "tensor"),
        P(),
        P(),
        P(None, "tensor"),
        P(None, "tensor"),
        P("dp", "strip", None, None),
        P("dp", "strip", "tensor", None),
    )
    out_specs = (
        P("dp", "strip", None, None),
        P("dp", "strip", "tensor", None),
        P("dp", "strip", None, None),
        P("dp", "strip", "tensor", None),
        P(("strip", "tensor"), None),
        P(("strip", "tensor")),
        P(("strip", "tensor")),
        P(("strip", "tensor"), None),
        P(("strip", "tensor"), None),
        P(("strip", "tensor")),
        P(("dp", "strip"), None),
        P(("dp", "strip"), None),
        P(("dp", "strip")),
        P(("dp", "strip")),
        P(("dp", "strip")),
        P(("dp", "strip"), None, "tensor"),
        P(("dp", "strip"), "tensor"),
        P(("dp", "strip")),
        P(("dp", "strip")),
        P(("dp", "strip"), "tensor"),
        P(("dp", "strip"), "tensor"),
    )
    return jax.shard_map(shards, mesh=mesh, in_specs=in_specs, out_specs=out_specs, check_vma=False)
```

profile of v0, /device:TPU:0, one launch (start us, length us, event | category | flops | bytes accessed | tf_op | source)
XLA Modules:
  0.0 3737.0 jit_solution(730047679041999385)
XLA Ops:
  93.4 55.7 %fusion.490 = (f32[24,12]{0,1:T(8,128)}, f32[1,24,12,1536]{3,1,2,0:T(8,128)}) fusion(f32[1536]{0:T(1024)S(1)} %get-tuple-element.353, f32[1,30,18,1536]{3,1,2,0:T(8,128)} %maximum_convert_fusion, f32[1536]{0:T(1024)S(1)} %get-tuple-element.354, f32[1536]{0:T(1024)} %get-tuple-element.307, f32[1536]{0:T(1024)} %get-tuple-element.308, ...), kind=kLoop, calls=%fused_computation.1233 | loop fusion | flops 43351776 | bytes 88775808 | tf_op jit(solution)/shard_map/jvp()/reduce_sum | solution.py:36
  154.2 54.9 %fusion.494 = (f32[24,12]{0,1:T(8,128)S(1)}, f32[1,24,12,1536]{3,1,2,0:T(8,128)}) fusion(f32[1536]{0:T(1024)S(1)} %get-tuple-element.353, f32[1,30,18,1536]{3,1,2,0:T(8,128)} %maximum_convert_fusion.2, f32[1536]{0:T(1024)S(1)} %get-tuple-element.354, f32[1536]{0:T(1024)} %get-tuple-element.307, f32[1536]{0:T(1024)} %get-tuple-element.308, ...), kind=kLoop, calls=%fused_computation.1235 | loop fusion | flops 43351776 | bytes 88775808 | tf_op jit(solution)/shard_map/jvp()/reduce_sum | solution.py:36
  216.9 55.2 %fusion.492 = (f32[24,12]{0,1:T(8,128)S(1)}, f32[1,24,12,1536]{3,1,2,0:T(8,128)}) fusion(f32[1536]{0:T(1024)S(1)} %get-tuple-element.353, f32[1,30,18,1536]{3,1,2,0:T(8,128)} %maximum_convert_fusion.1, f32[1536]{0:T(1024)S(1)} %get-tuple-element.354, f32[1536]{0:T(1024)S(1)} %copy-done.275, f32[1536]{0:T(1024)} %get-tuple-element.308, ...), kind=kLoop, calls=%fused_computation.1234 | loop fusion | flops 43351776 | bytes 88775808 | tf_op jit(solution)/shard_map/jvp()/reduce_sum | solution.py:36
  291.7 26.0 multiply_convert_fusion
  317.7 50.0 %all-gather.11.cloned.1.call-done = bf16[1536,6144]{1,0:T(8,128)(2,1)} async-done(((bf16[192,6144]{1,0:T(8,128)(2,1)}), bf16[1536,6144]{1,0:T(8,128)(2,1)}) %all-gather.11.cloned.1.call-update) | async-done | bytes 18874384 | tf_op jit(solution)/shard_map/all_gather | solution.py:121
  390.0 24.2 multiply_convert_fusion.1
  437.8 24.2 multiply_convert_fusion.2
  485.3 183.1 %all-reduce.35 = (bf16[1,12,24,1536]{3,2,1,0:T(8,128)(2,1)}, bf16[1,12,24,1536]{3,2,1,0:T(8,128)(2,1)}, bf16[1,12,24,1536]{3,2,1,0:T(8,128)(2,1)}) all-reduce(f32[1,12,24,1536]{3,2,1,0:T(8,128)} %convolution_bitcast_fusion.3, ...), channel_id=1, replica_groups=mesh['dp'=4,'strip'=2,'tensor'=4] {'tensor'}, use_global_device_ids=true, to_apply=%region_24.25 | all-reduce | flops 1327104 | bytes 7962624 | tf_op jit(solution)/shard_map/psum | solution.py:193
  795.7 128.7 %all-reduce.32.cloned.1.call-done = (f32[288,1024]{1,0:T(8,128)}, f32[288,1024]{1,0:T(8,128)}, f32[288,1024]{1,0:T(8,128)}) async-done(((f32[288,1024]{1,0:T(8,128)}, f32[288,1024]{1,0:T(8,128)}, f32[288,1024]{1,0:T(8,128)}), (f32[288,1024]{1,0:T(8,128)}, f32[288,1024]{1,0:T(8,128)}, f32[288,1024]{1,0:T(8,128)})) %all-reduce.32.cloned.1.call-update) | async-done | bytes 3538960 | tf_op jit(solution)/shard_map/psum | solution.py:228
  953.3 133.4 %all-reduce.30.cloned.1.call-done = (f32[288,1024]{1,0:T(8,128)}, f32[288,1024]{1,0:T(8,128)}, f32[288,1024]{1,0:T(8,128)}) async-done(((f32[288,1024]{1,0:T(8,128)}, f32[288,1024]{1,0:T(8,128)}, f32[288,1024]{1,0:T(8,128)}), (f32[288,1024]{1,0:T(8,128)}, f32[288,1024]{1,0:T(8,128)}, f32[288,1024]{1,0:T(8,128)})) %all-reduce.30.cloned.1.call-update) | async-done | bytes 3538960 | tf_op jit(solution)/shard_map/psum | solution.py:253
  1234.2 241.6 %all-reduce.28.cloned.1.call-done = (f32[288,1024]{1,0:T(8,128)}, f32[288,1024]{1,0:T(8,128)}, f32[288,1024]{1,0:T(8,128)}, f32[288,1024]{1,0:T(8,128)}, f32[288,1024]{1,0:T(8,128)}, /*index=5*/f32[288,1024]{1,0:T(8,128)}) async-done(((f32[288,1024]{1,0:T(8,128)}, f32[288,1024]{1,0:T(8,128)}, f32[288,1024]{1,0:T(8,128)}, f32[288,1024]{1,0:T(8,128)}, f32[288,1024]{1,0:T(8,128)}, ...) | async-done | bytes 7077904 | tf_op jit(solution)/shard_map/psum | solution.py:238
  1554.0 18.2 add_convert_fusion.2
  1587.7 18.0 add_convert_fusion.1
  1618.8 17.9 add_convert_fusion
  1722.9 18.4 fusion.531
  1741.4 16.1 fusion.532
  1757.6 40.5 %add_add_fusion.1 = f32[1536,6144]{1,0:T(8,128)} fusion(f32[1536,6144]{1,0:T(8,128)} %fusion.531, f32[1536,6144]{1,0:T(8,128)} %fusion.532, bf16[288,1536]{1,0:T(8,128)(2,1)S(1)} %copy-done.109, bf16[288,6144]{1,0:T(8,128)(2,1)} %copy-done.114), kind=kOutput, calls=%fused_computation.1 | convolution fusion | flops 5454692352 | bytes 117669888 | tf_op jit(solution)/shard_map/dot_general | solution.py:330
  1799.2 18.2 fusion.533
  1817.4 16.2 fusion.534
  1833.6 40.5 %add_add_fusion = f32[1536,6144]{1,0:T(8,128)} fusion(f32[1536,6144]{1,0:T(8,128)} %fusion.533, f32[1536,6144]{1,0:T(8,128)} %fusion.534, bf16[288,1536]{1,0:T(8,128)(2,1)S(1)} %copy-done.111, bf16[288,6144]{1,0:T(8,128)(2,1)} %get-tuple-element.442), kind=kOutput, calls=%fused_computation | convolution fusion | flops 5454692352 | bytes 117669888 | tf_op jit(solution)/shard_map/dot_general | solution.py:325
  1913.1 26.6 all-reduce.15
  2003.1 100.9 %all-reduce.14 = (f32[1536]{0:T(1024)S(1)}, f32[1536]{0:T(1024)S(1)}, f32[1536]{0:T(1024)S(1)}) all-reduce(f32[1536]{0:T(1024)S(1)} %add_add_fusion.20, f32[1536]{0:T(1024)S(1)} %add_add_fusion.19, f32[1536]{0:T(1024)S(1)} %add_add_fusion.18), channel_id=15, replica_groups=mesh['dp'=4,'strip'=2,'tensor'=4] {'strip','tensor'}, use_global_device_ids=true, to_apply=%region_218.219.clone | all-reduce | flops 4608 | bytes 36864
  2107.0 17.9 all-reduce.20
  2139.3 31.2 fusion.104
  2170.5 385.0 %reduce-scatter.30.cloned.1.call-done = f32[192,6144]{1,0:T(8,128)} async-done(((f32[1536,6144]{1,0:T(8,128)}), f32[192,6144]{1,0:T(8,128)}) %reduce-scatter.30.cloned.1.call-update) | async-done | bytes 4718608 | tf_op jit(solution)/shard_map/reduce_scatter | solution.py:357
  2555.5 724.5 %reduce-scatter.32.cloned.1.call-done = f32[192,6144]{1,0:T(8,128)} async-done(((f32[1536,6144]{1,0:T(8,128)}), f32[192,6144]{1,0:T(8,128)}) %reduce-scatter.32.cloned.1.call-update) | async-done | bytes 4718608 | tf_op jit(solution)/shard_map/reduce_scatter | solution.py:357
  3284.1 44.2 %fusion.160 = f32[1,24,12,1536]{3,1,2,0:T(8,128)} fusion(f32[1,24,12,1536]{3,1,2,0:T(8,128)} %get-tuple-element.574, f32[1,24,12,1536]{3,1,2,0:T(8,128)} %copy-done.22, f32[1,3,12,1536]{3,1,2,0:T(4,128)} %copy-done.145, f32[1,3,12,1536]{3,1,2,0:T(4,128)} %copy-done.141, f32[1,30,15,1536]{3,1,2,0:T(8,128)} %get-tuple-element.459, ...), kind=kLoop, calls=%fused_computation.275 | loop fusion | flops 46448640 | bytes 80370816 | tf_op jit(solution)/shard_map/mul | solution.py:339
  3328.3 31.1 fusion.48
  3376.8 50.5 %reduce-scatter.38.cloned.1.call-done = f32[128,3,256]{2,0,1:T(8,128)} async-done(((f32[1024,3,256]{2,0,1:T(8,128)}), f32[128,3,256]{2,0,1:T(8,128)}) %reduce-scatter.38.cloned.1.call-update) | async-done | bytes 393232 | tf_op jit(solution)/shard_map/reduce_scatter | solution.py:359
  3427.3 35.0 reduce-scatter.36.cloned.1.call-done
  3462.3 66.0 %reduce-scatter.34.cloned.1.call-done = f32[192,1024]{1,0:T(8,128)} async-done(((f32[1536,1024]{1,0:T(8,128)}), f32[192,1024]{1,0:T(8,128)}) %reduce-scatter.34.cloned.1.call-update) | async-done | bytes 786448 | tf_op jit(solution)/shard_map/reduce_scatter | solution.py:359
  3528.3 192.9 %all-reduce.34.cloned.1.call-done = (f32[192,6144]{1,0:T(8,128)}, f32[192,6144]{1,0:T(8,128)}) async-done(((f32[192,6144]{1,0:T(8,128)}, f32[192,6144]{1,0:T(8,128)}), (f32[192,6144]{1,0:T(8,128)}, f32[192,6144]{1,0:T(8,128)})) %all-reduce.34.cloned.1.call-update) | async-done | bytes 9437200 | tf_op jit(solution)/shard_map/psum | solution.py:358
  (1613 shorter events, 818.6 us)
Async XLA Ops:
  7.2 284.5 %all-gather.9.cloned.1.call-start = ((), (), s32[]{:S(2)}) async-start(), calls=%async_computation.15 | async-start | bytes 21233664 | tf_op jit(solution)/shard_map/all_gather | solution.py:120
  8.0 359.8 %all-gather.11.cloned.1.call-start = ((), (), s32[]{:S(2)}) async-start(), calls=%async_computation.16 | async-start | bytes 21233664 | tf_op jit(solution)/shard_map/all_gather | solution.py:121
  8.7 915.8 %all-reduce.32.cloned.1.call-start = ((), (), s32[]{:S(2)}) async-start(), calls=%async_computation.34 | async-start | bytes 7077888 | tf_op jit(solution)/shard_map/psum | solution.py:228
  28.6 43.4 %collective-permute-start.12 = (bf16[1,3,12,1536]{3,1,2,0:T(4,128)(2,1)}, bf16[1,3,12,1536]{3,1,2,0:T(4,128)(2,1)S(1)}, u32[]{:S(2)}, u32[]{:S(2)}) collective-permute-start(bf16[1,3,12,1536]{3,1,2,0:T(4,128)(2,1)} %get-tuple-element.504), channel_id=1, source_target_pairs={{0,4},{1,5},{2,6},{3,7},{8,12},{9,13},{10,14},{11,15},{16,20},{17,... | collective-permute-start | bytes 331784 | tf_op jit(solution)/shard_map/ppermute | solution.py:26
  66.7 146.3 %collective-permute-start.8 = (bf16[1,30,3,1536]{3,1,2,0:T(8,128)(2,1)}, bf16[1,30,3,1536]{3,1,2,0:T(8,128)(2,1)}, u32[]{:S(2)}, u32[]{:S(2)}) collective-permute-start(bf16[1,30,3,1536]{3,1,2,0:T(8,128)(2,1)} %get-tuple-element.496), channel_id=1, source_target_pairs={{0,1},{1,2},{2,3},{4,5},{5,6},{6,7},{8,9},{9,10},{10,11},{12,13},{... | collective-permute-start | bytes 829448 | tf_op jit(solution)/shard_map/ppermute | solution.py:26
  72.0 141.1 %collective-permute-start.9 = (bf16[1,30,3,1536]{3,1,2,0:T(8,128)(2,1)}, bf16[1,30,3,1536]{3,1,2,0:T(8,128)(2,1)}, u32[]{:S(2)}, u32[]{:S(2)}) collective-permute-start(bf16[1,30,3,1536]{3,1,2,0:T(8,128)(2,1)} %get-tuple-element.497), channel_id=1, source_target_pairs={{1,0},{2,1},{3,2},{5,4},{6,5},{7,6},{9,8},{10,9},{11,10},{13,12},{... | collective-permute-start | bytes 829448 | tf_op jit(solution)/shard_map/ppermute | solution.py:28
  75.1 75.3 %collective-permute-start.14 = (bf16[1,30,3,1536]{3,1,2,0:T(8,128)(2,1)}, bf16[1,30,3,1536]{3,1,2,0:T(8,128)(2,1)}, u32[]{:S(2)}, u32[]{:S(2)}) collective-permute-start(bf16[1,30,3,1536]{3,1,2,0:T(8,128)(2,1)} %get-tuple-element.498), channel_id=1, source_target_pairs={{0,1},{1,2},{2,3},{4,5},{5,6},{6,7},{8,9},{9,10},{10,11},{12,13},{... | collective-permute-start | bytes 829448 | tf_op jit(solution)/shard_map/ppermute | solution.py:26
  80.4 70.0 %collective-permute-start.15 = (bf16[1,30,3,1536]{3,1,2,0:T(8,128)(2,1)}, bf16[1,30,3,1536]{3,1,2,0:T(8,128)(2,1)}, u32[]{:S(2)}, u32[]{:S(2)}) collective-permute-start(bf16[1,30,3,1536]{3,1,2,0:T(8,128)(2,1)} %get-tuple-element.499), channel_id=1, source_target_pairs={{1,0},{2,1},{3,2},{5,4},{6,5},{7,6},{9,8},{10,9},{11,10},{13,12},{... | collective-permute-start | bytes 829448 | tf_op jit(solution)/shard_map/ppermute | solution.py:28
  790.1 296.5 %all-reduce.30.cloned.1.call-start = ((), (), s32[]{:S(2)}) async-start(), calls=%async_computation.33 | async-start | bytes 7077888 | tf_op jit(solution)/shard_map/psum | solution.py:253
  953.0 244.0 %reduce-scatter.48.cloned.1.call-start = ((), (), s32[]{:S(2)}) async-start(), calls=%async_computation.26 | async-start | bytes 884736
  1107.7 93.0 %reduce-scatter.52.cloned.1.call-start = ((), (), s32[]{:S(2)}) async-start(), calls=%async_computation.28 | async-start | bytes 884736
  1122.2 82.3 %reduce-scatter.56.cloned.1.call-start = ((), (), s32[]{:S(2)}) async-start(), calls=%async_computation.30 | async-start | bytes 884736
  1137.8 70.4 %reduce-scatter.54.cloned.1.call-start = ((), (), s32[]{:S(2)}) async-start(), calls=%async_computation.29 | async-start | bytes 884736
  1152.4 59.5 %reduce-scatter.50.cloned.1.call-start = ((), (), s32[]{:S(2)}) async-start(), calls=%async_computation.27 | async-start | bytes 884736
  1166.6 49.0 %reduce-scatter.46.cloned.1.call-start = ((), (), s32[]{:S(2)}) async-start(), calls=%async_computation.25 | async-start | bytes 884736
  1180.8 294.9 %all-reduce.28.cloned.1.call-start = ((), (), s32[]{:S(2)}) async-start(), calls=%async_computation.32 | async-start | bytes 14155776 | tf_op jit(solution)/shard_map/psum | solution.py:238
  1226.4 669.9 %reduce-scatter.44.cloned.1.call-start = ((), (), s32[]{:S(2)}) async-start(), calls=%async_computation.24 | async-start | bytes 4718592 | tf_op jit(solution)/shard_map/reduce_scatter | solution.py:359
  1233.9 872.1 %reduce-scatter.58.cloned.1.call-start = ((), (), s32[]{:S(2)}) async-start(), calls=%async_computation.31 | async-start | bytes 884736
  1497.9 44.0 %collective-permute-start.18 = (f32[1,1,24,1024]{3,2,1,0:T(8,128)}, f32[1,1,24,1024]{3,2,1,0:T(8,128)S(1)}, u32[]{:S(2)}, u32[]{:S(2)}) collective-permute-start(f32[1,1,24,1024]{3,2,1,0:T(8,128)} %get-tuple-element.484), channel_id=1, source_target_pairs={{0,4},{1,5},{2,6},{3,7},{8,12},{9,13},{10,14},{11,15},{16,20},{17,... | collective-permute-start | bytes 294920 | tf_op jit(solution)/shard_map/ppermute | solution.py:26
  1757.5 797.9 %reduce-scatter.30.cloned.1.call-start = ((), (), s32[]{:S(2)}) async-start(), calls=%async_computation.17 | async-start | bytes 42467328 | tf_op jit(solution)/shard_map/reduce_scatter | solution.py:357
  1798.1 1481.9 %reduce-scatter.32.cloned.1.call-start = ((), (), s32[]{:S(2)}) async-start(), calls=%async_computation.18 | async-start | bytes 42467328 | tf_op jit(solution)/shard_map/reduce_scatter | solution.py:357
  1874.1 1490.8 %reduce-scatter.40.cloned.1.call-start = ((), (), s32[]{:S(2)}) async-start(), calls=%async_computation.22 | async-start | bytes 1179648 | tf_op jit(solution)/shard_map/reduce_scatter | solution.py:359
  1878.7 1498.1 %reduce-scatter.42.cloned.1.call-start = ((), (), s32[]{:S(2)}) async-start(), calls=%async_computation.23 | async-start | bytes 4718592 | tf_op jit(solution)/shard_map/reduce_scatter | solution.py:359
  1885.8 1541.5 %reduce-scatter.38.cloned.1.call-start = ((), (), s32[]{:S(2)}) async-start(), calls=%async_computation.21 | async-start | bytes 3538944 | tf_op jit(solution)/shard_map/reduce_scatter | solution.py:359
  1893.2 1569.1 %reduce-scatter.36.cloned.1.call-start = ((), (), s32[]{:S(2)}) async-start(), calls=%async_computation.20 | async-start | bytes 73728 | tf_op jit(solution)/shard_map/reduce_scatter | solution.py:359
  1902.3 1625.9 %reduce-scatter.34.cloned.1.call-start = ((), (), s32[]{:S(2)}) async-start(), calls=%async_computation.19 | async-start | bytes 7077888 | tf_op jit(solution)/shard_map/reduce_scatter | solution.py:359
  1912.5 1808.7 %all-reduce.34.cloned.1.call-start = ((), (), s32[]{:S(2)}) async-start(), calls=%async_computation.35 | async-start | bytes 18874368 | tf_op jit(solution)/shard_map/psum | solution.py:358
  1965.6 161.2 %collective-permute-start.34 = (f32[1,30,3,1536]{3,0,2,1:T(1,128)}, f32[1,30,3,1536]{3,0,2,1:T(1,128)}, u32[]{:S(2)}, u32[]{:S(2)}) collective-permute-start(f32[1,30,3,1536]{3,0,2,1:T(1,128)} %copy.231), channel_id=1, source_target_pairs={{0,1},{1,2},{2,3},{4,5},{5,6},{6,7},{8,9},{9,10},{10,11},{12,13},{... | collective-permute-start | bytes 1658888 | tf_op jit(solution)/shard_map/ppermute | solution.py:26
  1974.4 154.4 %collective-permute-start.23 = (f32[1,30,3,1536]{3,0,2,1:T(1,128)}, f32[1,30,3,1536]{3,0,2,1:T(1,128)}, u32[]{:S(2)}, u32[]{:S(2)}) collective-permute-start(f32[1,30,3,1536]{3,0,2,1:T(1,128)} %copy.219), channel_id=1, source_target_pairs={{1,0},{2,1},{3,2},{5,4},{6,5},{7,6},{9,8},{10,9},{11,10},{13,12},{... | collective-permute-start | bytes 1658888 | tf_op jit(solution)/shard_map/ppermute | solution.py:28
  1975.7 154.2 %collective-permute-start.22 = (f32[1,30,3,1536]{3,0,2,1:T(1,128)}, f32[1,30,3,1536]{3,0,2,1:T(1,128)}, u32[]{:S(2)}, u32[]{:S(2)}) collective-permute-start(f32[1,30,3,1536]{3,0,2,1:T(1,128)} %copy.217), channel_id=1, source_target_pairs={{0,1},{1,2},{2,3},{4,5},{5,6},{6,7},{8,9},{9,10},{10,11},{12,13},{... | collective-permute-start | bytes 1658888 | tf_op jit(solution)/shard_map/ppermute | solution.py:26
  1984.6 146.6 %collective-permute-start.29 = (f32[1,30,3,1536]{3,0,2,1:T(1,128)}, f32[1,30,3,1536]{3,0,2,1:T(1,128)}, u32[]{:S(2)}, u32[]{:S(2)}) collective-permute-start(f32[1,30,3,1536]{3,0,2,1:T(1,128)} %copy.226), channel_id=1, source_target_pairs={{1,0},{2,1},{3,2},{5,4},{6,5},{7,6},{9,8},{10,9},{11,10},{13,12},{... | collective-permute-start | bytes 1658888 | tf_op jit(solution)/shard_map/ppermute | solution.py:28
  2000.9 131.4 %collective-permute-start.28 = (f32[1,30,3,1536]{3,0,2,1:T(1,128)}, f32[1,30,3,1536]{3,0,2,1:T(1,128)}, u32[]{:S(2)}, u32[]{:S(2)}) collective-permute-start(f32[1,30,3,1536]{3,0,2,1:T(1,128)} %copy.224), channel_id=1, source_target_pairs={{0,1},{1,2},{2,3},{4,5},{5,6},{6,7},{8,9},{9,10},{10,11},{12,13},{... | collective-permute-start | bytes 1658888 | tf_op jit(solution)/shard_map/ppermute | solution.py:26
  (505 other events, 6918.7 us)
Sparse Core Ops, SparseCore 0:
  9.6 189.8 all-gather.8
  201.1 166.5 all-gather.10
  790.3 134.1 all-reduce.31
  953.1 133.4 all-reduce.29
  1107.8 6.9 reduce-scatter.47
  1122.3 6.9 reduce-scatter.51
  1137.9 7.0 reduce-scatter.55
  1152.5 7.0 reduce-scatter.53
  1166.8 7.0 reduce-scatter.49
  1180.9 7.0 reduce-scatter.45
  1226.5 249.1 all-reduce.27
  1479.5 50.1 reduce-scatter.43
  1757.7 34.1 reduce-scatter.57
  1798.2 757.2 reduce-scatter.29
  2557.8 722.0 reduce-scatter.31
  3283.5 37.5 reduce-scatter.39
  3325.5 51.2 reduce-scatter.41
  3381.0 46.2 reduce-scatter.37
  3430.9 31.3 reduce-scatter.35
  3466.5 61.7 reduce-scatter.33
  3532.0 189.1 all-reduce.33
where the time goes:
time: 3750 us; the launch traced here: 3740 us
  waiting for transfers between devices  2050 us (55%)
  matrix products  518 us (14%)
  other arithmetic  480 us (13%)
  blocking collectives  356 us (9%)
  local copies, waits for them, and re-layouts  219 us (6%)
  starting transfers between devices  86.8 us (2%)
    reduce_scatter x2, waiting for transfers between devices, shards(): lax.psum_scatter(conv_totals, ('strip', 'tensor'), scatter_dimension=0, t...  1110 us
    psum x1, waiting for transfers between devices, shards(): mlp_out = lax.psum(mlp_part, 'tensor')  242 us
    psum x1, waiting for transfers between devices, shards(): conv_shares = lax.psum(conv_owned, 'dp')  193 us
    psum x1, blocking collectives, shards(): pooled = lax.psum(pooled_part, 'tensor')  183 us
    reduce_sum x8, other arithmetic, layer_norm(): center = jnp.mean(values, axis=-1, keepdims=True)  178 us
    reduce_scatter x6, waiting for transfers between devices, shards(): lax.psum_scatter(vit_totals, ('dp', 'strip'), scatter_dimension=0, tiled=...  163 us
    psum x1, waiting for transfers between devices, shards(): grad_normed_two = lax.psum(grad_normed_part, 'tensor')  133 us
    psum x1, waiting for transfers between devices, shards(): attn_out = lax.psum(attn_part, 'tensor')  129 us
  transfers between devices with their start and end apart: 57, of which 14 were waited for; matrix products, arithmetic and copies ran while one was open for 25% of the time, Pallas kernels for 0%

commit v1 on v0

v1 whole, which is shorter than its diff:
```python
import functools

import jax
import jax.numpy as jnp
from jax import lax
from jax.experimental import pallas as pl
from jax.experimental.pallas import tpu as pltpu
from jax.sharding import PartitionSpec as P

HD = 64
G = 24
MAXS = 48
EPS = 1e-06
BF = jnp.bfloat16
F32 = jnp.float32
DOWN_ROWS = (((0,), (0,)), ((), ()))
ACROSS = (((1,), (1,)), ((), ()))
VMEM = 48 * 2**20
EDGE = 8


def core_swap(v):
    return lax.ppermute(v, "strip", [(0, 1), (1, 0)])


def dp_swap(v, bit):
    return lax.ppermute(v, "dp", [(i, i ^ bit) for i in range(lax.axis_size("dp"))])


def shift(v, axis, step):
    count = lax.axis_size(axis)
    pairs = [(i, i + step) for i in range(count) if 0 <= i + step < count]
    return lax.ppermute(v, axis, pairs)


def all_sum(v, axes):
    for axis in axes:
        count, bit = lax.axis_size(axis), 1
        while bit < count:
            v = v + lax.ppermute(v, axis, [(i, i ^ bit) for i in range(count)])
            bit *= 2
    return v


def quarters():
    return 4 if lax.axis_size("dp") == 4 else 1


def gather_dp(own):
    if quarters() == 1:
        return [own]
    half = own.shape[0] // 2
    beside_x, beside_y = dp_swap(own, 1), dp_swap(own, 2)
    far = jnp.concatenate([dp_swap(beside_x[:half], 2), dp_swap(beside_y[half:], 1)], axis=0)
    return [own, beside_x, beside_y, far]


def reduce_dp(pieces):
    if len(pieces) == 1:
        return pieces[0]
    own, beside_x, beside_y, far = pieces
    half = own.shape[0] // 2
    near_a = dp_swap(jnp.concatenate([beside_x[:half], far[:half]], axis=0), 1)
    near_b = dp_swap(jnp.concatenate([beside_y[half:], far[half:]], axis=0), 2)
    add = lambda *terms: functools.reduce(lambda a, b: a + b, [t.astype(F32) for t in terms])
    last_a = dp_swap(add(beside_y[:half], near_a[half:]).astype(BF), 2)
    last_b = dp_swap(add(beside_x[half:], near_b[half:]).astype(BF), 1)
    top = add(own[:half], near_a[:half], last_a)
    low = add(own[half:], near_b[:half], last_b)
    return jnp.concatenate([top, low], axis=0).astype(BF)


def in_order(mine, other, at):
    first = at == 0
    return jnp.stack([jnp.where(first, mine, other), jnp.where(first, other, mine)], axis=0)


def dp_order(pieces):
    at = lax.axis_index("dp")
    bit_x, bit_y = at % 2 == 1, at // 2 == 1
    row_own = [jnp.where(bit_x, pieces[1], pieces[0]), jnp.where(bit_x, pieces[0], pieces[1])]
    row_far = [jnp.where(bit_x, pieces[3], pieces[2]), jnp.where(bit_x, pieces[2], pieces[3])]
    return jnp.stack(
        [jnp.where(bit_y, f, o) for o, f in zip(row_own, row_far)]
        + [jnp.where(bit_y, o, f) for o, f in zip(row_own, row_far)],
        axis=0,
    )


def pick(view, first, second):
    rows, _, _, width = view.shape
    return lax.dynamic_slice(view, (0, first, second, 0), (rows, 1, 1, width)).reshape(rows, width)


def gather_conv_weight(block):
    rows, hidden = block.shape
    q = quarters()
    strip_at = lax.axis_index("strip")
    dp_at = lax.axis_index("dp") if q > 1 else 0
    view = block.reshape(rows, 2, q, hidden // (2 * q))
    mine = pick(view, strip_at, dp_at)
    other = core_swap(pick(view, 1 - strip_at, dp_at))
    both = in_order(mine, other, strip_at)
    whole = lax.all_gather(both, "tensor", axis=0)
    whole = jnp.swapaxes(whole, 0, 1).reshape(-1, mine.shape[1])
    return gather_dp(whole)


def return_conv_grad(pieces):
    strip_at = lax.axis_index("strip")
    zs = lax.axis_size("tensor")
    own = reduce_dp(pieces)
    channels, width = own.shape
    rows = channels // (2 * zs)
    view = jnp.swapaxes(own.reshape(2, zs, rows, width), 0, 1)
    part = lax.psum_scatter(view, "tensor", scatter_dimension=0)
    mine = lax.dynamic_index_in_dim(part, strip_at, 0, keepdims=False)
    other = core_swap(lax.dynamic_index_in_dim(part, 1 - strip_at, 0, keepdims=False))
    both = in_order(mine, other, strip_at)
    if len(pieces) == 1:
        total = lax.psum(both, "dp")
        return jnp.swapaxes(total, 0, 1).reshape(rows, -1).astype(F32)
    every = dp_order(gather_dp(jnp.swapaxes(both, 0, 1)))
    return jnp.transpose(every, (1, 2, 0, 3)).reshape(rows, -1).astype(F32)


def gather_mlp_weight(block):
    width, hidden = block.shape
    q = quarters()
    dp_at = lax.axis_index("dp") if q > 1 else 0
    mine = pick(block.reshape(width, 2, q, hidden // (2 * q)), lax.axis_index("strip"), dp_at)
    whole = lax.all_gather(mine, "tensor", axis=0)
    return gather_dp(jnp.swapaxes(whole, 0, 1).reshape(width, -1))


def return_mlp_grad(pieces):
    own = reduce_dp(pieces)
    width, all_cols = own.shape
    zs = lax.axis_size("tensor")
    cols = all_cols // zs
    dps = lax.axis_size("dp")
    rows = width // (2 * dps)
    view = jnp.swapaxes(own.reshape(width, zs, cols), 0, 1)
    part = lax.psum_scatter(view, "tensor", scatter_dimension=0)
    if len(pieces) > 1:
        parts = lax.all_to_all(part, ("dp", "strip"), 0, 0, tiled=True)
        parts = parts.reshape(dps, 2, rows, cols)
        return jnp.transpose(parts, (2, 1, 0, 3)).reshape(rows, -1).astype(F32)
    strip_at = lax.axis_index("strip")
    part = lax.psum_scatter(part.reshape(dps, 2, rows, cols), "dp", scatter_dimension=0)
    mine = lax.dynamic_index_in_dim(part, strip_at, 0, keepdims=False)
    other = core_swap(lax.dynamic_index_in_dim(part, 1 - strip_at, 0, keepdims=False))
    both = in_order(mine, other, strip_at)
    return jnp.swapaxes(both, 0, 1).reshape(rows, -1).astype(F32)


def gather_rows(block):
    width, cols = block.shape
    dps = lax.axis_size("dp")
    rows = width // (2 * dps)
    at = lax.axis_index("dp") * 2 + lax.axis_index("strip")
    mine = lax.dynamic_slice_in_dim(block, at * rows, rows, 0)
    whole = lax.all_gather(mine, ("tensor", "dp", "strip"), axis=0, tiled=True)
    return whole.reshape(-1, width, cols)


def params(limit=VMEM):
    return pltpu.CompilerParams(vmem_limit_bytes=limit)


def conv7_kernel(rows, cols, x_ref, k_ref, out_ref, wide):
    wide[...] = x_ref[0].astype(F32)

    def tap_row(i, sums):
        sums = list(sums)
        taps = k_ref[i]
        for m in range(cols + 6):
            x = wide[m, pl.ds(i + EDGE - 3, rows), :]
            for j in range(7):
                c = m - j
                if 0 <= c < cols:
                    sums[c] = sums[c] + x * taps[j : j + 1]
        return tuple(sums)

    sums = lax.fori_loop(0, 7, tap_row, tuple(jnp.zeros((rows, 128), F32) for _ in range(cols)))
    for c in range(cols):
        out_ref[0, c] = sums[c]


def conv7(padded, taps, rows, cols):
    items, _, _, channels = padded.shape
    return pl.pallas_call(
        functools.partial(conv7_kernel, rows, cols),
        grid=(items, channels // 128),
        in_specs=[
            pl.BlockSpec((1, cols + 6, rows + 2 * EDGE, 128), lambda b, c: (b, 0, 0, c)),
            pl.BlockSpec((7, 8, 128), lambda b, c: (0, 0, c)),
        ],
        out_specs=pl.BlockSpec((1, cols, rows, 128), lambda b, c: (b, 0, 0, c)),
        out_shape=jax.ShapeDtypeStruct((items, cols, rows, channels), F32),
        scratch_shapes=[pltpu.VMEM((cols + 6, rows + 2 * EDGE, 128), F32)],
        compiler_params=params(),
        cost_estimate=pl.CostEstimate(
            flops=items * cols * rows * channels * 98, bytes_accessed=padded.size * 2 + items * cols * rows * channels * 4, transcendentals=0
        ),
        name="depthwise",
    )(padded, taps)


def tap_grad_kernel(rows, cols, x_ref, g_ref, out_ref, wide):
    wide[...] = x_ref[0].astype(F32)

    @pl.when(pl.program_id(1) == 0)
    def _():
        out_ref[...] = jnp.zeros_like(out_ref)

    def tap_row(i, _):
        sums = [jnp.zeros((8, 128), F32) for _ in range(7)]
        grads = [g_ref[0, c] for c in range(cols)]
        for m in range(cols + 6):
            x = wide[m, pl.ds(i + EDGE - 3, rows), :]
            for j in range(7):
                c = m - j
                if 0 <= c < cols:
                    sums[j] = sums[j] + (x * grads[c]).reshape(rows // 8, 8, 128).sum(axis=0)
        lines = [jnp.sum(s, axis=0, keepdims=True) for s in sums]
        out_ref[i] += jnp.concatenate(lines + [jnp.zeros((1, 128), F32)], axis=0)
        return 0

    lax.fori_loop(0, 7, tap_row, 0)


def tap_grad(padded, grad, rows, cols):
    items, _, _, channels = padded.shape
    return pl.pallas_call(
        functools.partial(tap_grad_kernel, rows, cols),
        grid=(channels // 128, items),
        in_specs=[
            pl.BlockSpec((1, cols + 6, rows + 2 * EDGE, 128), lambda c, b: (b, 0, 0, c)),
            pl.BlockSpec((1, cols, rows, 128), lambda c, b: (b, 0, 0, c)),
        ],
        out_specs=pl.BlockSpec((7, 8, 128), lambda c, b: (0, 0, c)),
        out_shape=jax.ShapeDtypeStruct((7, 8, channels), F32),
        scratch_shapes=[pltpu.VMEM((cols + 6, rows + 2 * EDGE, 128), F32)],
        compiler_params=params(),
        cost_estimate=pl.CostEstimate(
            flops=items * cols * rows * channels * 98, bytes_accessed=padded.size * 2 + items * cols * rows * channels * 4, transcendentals=0
        ),
        name="tap_grad",
    )(padded, grad)


def gelu_pair(h):
    cdf = 0.5 * (1.0 + lax.erf(h * (0.5**0.5)))
    pdf = jnp.exp(h * h * -0.5) * 0.3989422804014327
    return h * cdf, cdf + h * pdf


def expand_kernel(step, x_ref, w_ref, act_ref, slope_ref):
    x = x_ref[...]
    for at in range(0, w_ref.shape[1], step):
        h = jnp.dot(x, w_ref[:, at : at + step], preferred_element_type=F32)
        act, slope = gelu_pair(h)
        act_ref[:, at : at + step] = act.astype(BF)
        slope_ref[:, at : at + step] = slope.astype(BF)


def row_block(rows, most):
    best = 16
    for block in range(16, most + 1, 16):
        if rows % block == 0:
            best = block
    return best


def expand(x, w):
    m, k = x.shape
    n = w.shape[1]
    bm = row_block(m, 432)
    bn = min(n, 768)
    spec = pl.BlockSpec((bm, bn), lambda j, i: (i, j))
    return pl.pallas_call(
        functools.partial(expand_kernel, 256),
        grid=(n // bn, m // bm),
        in_specs=[pl.BlockSpec((bm, k), lambda j, i: (i, 0)), pl.BlockSpec((k, bn), lambda j, i: (0, j))],
        out_specs=[spec, spec],
        out_shape=[jax.ShapeDtypeStruct((m, n), BF)] * 2,
        compiler_params=params(),
        cost_estimate=pl.CostEstimate(flops=2 * m * n * k + 40 * m * n, bytes_accessed=2 * (m * k + n * k + 2 * m * n), transcendentals=2 * m * n),
        name="expand_gelu",
    )(x, w)


def back_sum_kernel(count, *refs):
    out_ref = refs[-1]
    total = None
    for a_ref, w_ref in zip(refs[:count], refs[count : 2 * count]):
        term = lax.dot_general(a_ref[...], w_ref[...], ACROSS, preferred_element_type=F32)
        total = term if total is None else total + term
    out_ref[...] = total.astype(out_ref.dtype)


def back_sum(parts, weights, first, rows, dtype):
    n = weights[0].shape[0]
    ks = [w.shape[1] for w in weights]
    bm = row_block(rows, 432)
    bn = 512
    skip = first // bm
    return pl.pallas_call(
        functools.partial(back_sum_kernel, len(parts)),
        grid=(n // bn, rows // bm),
        in_specs=[pl.BlockSpec((bm, k), lambda j, i: (i + skip, 0)) for k in ks]
        + [pl.BlockSpec((bn, k), lambda j, i: (j, 0)) for k in ks],
        out_specs=pl.BlockSpec((bm, bn), lambda j, i: (i, j)),
        out_shape=jax.ShapeDtypeStruct((rows, n), dtype),
        compiler_params=params(),
        cost_estimate=pl.CostEstimate(flops=2 * rows * n * sum(ks), bytes_accessed=2 * sum(ks) * (rows + n) + 4 * rows * n, transcendentals=0),
        name="reduce_sum",
    )(*parts, *weights)


def normalise(v):
    center = jnp.mean(v, axis=-1, keepdims=True)
    shifted = v - center
    scale = lax.rsqrt(jnp.mean(shifted * shifted, axis=-1, keepdims=True) + EPS)
    return shifted * scale, scale


def normalise_back(g, unit, scale, gain):
    gg = g * gain
    along = jnp.mean(gg * unit, axis=-1, keepdims=True)
    return scale * (gg - jnp.mean(gg, axis=-1, keepdims=True) - unit * along)


def pool_matrix(pooled_index, buffer_index, map_side, offset):
    map_place = buffer_index[None, :] - offset
    bin_start = pooled_index[:, None] * map_side // G
    bin_stop = ((pooled_index[:, None] + 1) * map_side + G - 1) // G
    inside = jnp.logical_and(map_place >= bin_start, map_place < bin_stop)
    real = jnp.logical_and(pooled_index >= 0, pooled_index < G)[:, None]
    return jnp.where(jnp.logical_and(inside, real), 1.0, 0.0).astype(F32) / (bin_stop - bin_start).astype(F32)


def depthwise3(padded, kernel, rows, cols):
    total = None
    for i in range(3):
        for j in range(3):
            term = padded[:, i : i + rows, j : j + cols, :] * kernel[:, 3 * i + j]
            total = term if total is None else total + term
    return total


def rim(v):
    v = jnp.concatenate([shift(v[:, -1:], "strip", 1), v, shift(v[:, :1], "strip", -1)], axis=1)
    return jnp.concatenate([shift(v[:, :, -1:], "tensor", 1), v, shift(v[:, :, :1], "tensor", -1)], axis=2)


def wide_rim(v):
    v = jnp.concatenate([shift(v[:, -3:], "tensor", 1), v, shift(v[:, :3], "tensor", -1)], axis=1)
    return jnp.concatenate([shift(v[:, :, -EDGE:], "strip", 1), v, shift(v[:, :, :EDGE], "strip", -1)], axis=2)


def shards(
    res_code, vit_in, map_in, dw_kernel, conv_gain, conv_bias, w_expand, w_reduce, layer_scale, adapt_w, mix_kernel,
    gate_logit, gain_one, bias_one, w_qkv, w_proj, gain_two, bias_two, w_up, w_down, d_vit, d_map,
):
    strip_at, tensor_at, dp_at = (lax.axis_index(a) for a in ("strip", "tensor", "dp"))
    dps, zs = lax.axis_size("dp"), lax.axis_size("tensor")
    items, grid_rows, _, width = vit_in.shape
    _, map_rows, map_cols, channels = map_in.shape
    grid_cols = G // zs
    cells = items * map_rows * map_cols
    tokens = items * grid_rows * grid_cols
    head_cols = w_qkv.shape[2]
    score_scale = HD**-0.5

    expand_pieces = gather_conv_weight(w_expand)
    reduce_pieces = gather_conv_weight(w_reduce)
    qkv_whole = gather_rows(w_qkv.reshape(width, -1))
    proj_whole = gather_rows(w_proj)
    up_pieces = gather_mlp_weight(w_up)
    down_pieces = gather_mlp_weight(w_down)
    count = len(expand_pieces)

    side = res_code // 32
    offset = (MAXS - side) // 2
    row_cells = strip_at * map_rows + jnp.arange(map_rows, dtype=jnp.int32)
    col_cells = tensor_at * map_cols + jnp.arange(map_cols, dtype=jnp.int32)

    def inside(at):
        low, high = offset[:, None], (offset + side)[:, None]
        return jnp.logical_and(at[None] >= low, at[None] < high).astype(F32)

    row_ok, col_ok = inside(row_cells), inside(col_cells)
    cell_mask = col_ok[:, :, None, None] * row_ok[:, None, :, None]
    many_pools = jax.vmap(pool_matrix, in_axes=(None, None, 0, 0))
    pooled_rows = strip_at * grid_rows + jnp.arange(grid_rows, dtype=jnp.int32)
    pooled_cols = (tensor_at - 1) * grid_cols + jnp.arange(3 * grid_cols, dtype=jnp.int32)
    row_pool = many_pools(pooled_rows, row_cells, side, offset)
    col_pool = many_pools(pooled_cols, col_cells, side, offset).reshape(items, 3, grid_cols, map_cols)
    pool = jnp.einsum("bir,bgjc->bgijcr", row_pool, col_pool)
    pool = pool.reshape(items, 3 * grid_rows * grid_cols, map_cols * map_rows).astype(BF)

    masked = jnp.swapaxes(map_in, 1, 2) * cell_mask.astype(BF)
    padded = wide_rim(masked)
    taps = jnp.pad(dw_kernel.T.reshape(7, 7, channels), ((0, 0), (0, 1), (0, 0)))
    spread = conv7(padded, taps, map_rows, map_cols).reshape(cells, channels)
    conv_unit, conv_std = normalise(spread)
    conv_unit = conv_unit.astype(BF)
    normed = (conv_unit.astype(F32) * conv_gain + conv_bias).astype(BF)
    normed_both = jnp.concatenate([normed, core_swap(normed)], axis=0)
    acts, slopes = zip(*[expand(normed_both, w) for w in expand_pieces])
    branch_there = core_swap(back_sum(acts, reduce_pieces, cells, cells, BF))
    branch_here = back_sum(acts, reduce_pieces, 0, cells, F32)
    branch = (branch_here + branch_there.astype(F32)).reshape(masked.shape)
    map_value = cell_mask * (masked.astype(F32) + layer_scale * branch)
    map_low = map_value.astype(BF)
    map_out = jnp.swapaxes(map_low, 1, 2)

    pooled3 = lax.dot_general(
        pool, map_low.reshape(items, -1, channels), (((2,), (1,)), ((0,), (0,))), preferred_element_type=F32
    ).reshape(items, 3, -1, channels)
    pooled = (
        pooled3[:, 1]
        + shift(pooled3[:, 0].astype(BF), "tensor", -1).astype(F32)
        + shift(pooled3[:, 2].astype(BF), "tensor", 1).astype(F32)
    )
    pooled_low = pooled.astype(BF).reshape(tokens, channels)
    grid_shape = (items, grid_rows, grid_cols, width)
    adapted = jnp.dot(pooled_low, adapt_w, preferred_element_type=F32).reshape(grid_shape)
    adapted_pad = rim(adapted)
    local_mix = depthwise3(adapted_pad, mix_kernel, grid_rows, grid_cols)
    gate = jnp.tanh(gate_logit)
    mine = lambda v: lax.dynamic_slice_in_dim(v, tensor_at * grid_cols, grid_cols, 2)
    joined = (mine(vit_in) + gate * local_mix).reshape(tokens, width)

    unit_one, std_one = normalise(joined)
    normed_one = (unit_one * gain_one + bias_one).astype(BF)
    group = head_cols // 2
    heads = group // HD

    def to_heads(parts):
        a = parts[0].shape[1]
        out = jnp.stack(parts, axis=0).reshape(zs, items, -1, a, 2, group)
        out = jnp.transpose(out, (4, 0, 1, 2, 3, 5)).reshape(2 * zs, items, -1, a * group)
        out = lax.all_to_all(out, ("strip", "tensor"), 0, 0, tiled=True)
        return jnp.swapaxes(out, 0, 1).reshape(items, -1, a, heads, HD)

    def to_tokens(v):
        a = v.shape[2]
        out = jnp.swapaxes(v.reshape(items, 2 * zs, -1, a * group), 0, 1)
        out = lax.all_to_all(out, ("strip", "tensor"), 0, 0, tiled=True)
        out = jnp.transpose(out.reshape(2, zs, tokens, a, group), (1, 2, 3, 0, 4))
        return out.reshape(zs, tokens, a * 2 * group)

    qkv = [jnp.dot(normed_one, w, preferred_element_type=F32).astype(BF).reshape(tokens, 3, 2, group) for w in qkv_whole]
    qkv = to_heads(qkv)
    q, k, v = qkv[:, :, 0], qkv[:, :, 1], qkv[:, :, 2]
    scores = jnp.einsum("bqhe,bkhe->bhqk", q, k, preferred_element_type=F32) * score_scale
    top = jnp.max(scores, axis=-1, keepdims=True)
    powers = jnp.exp(scores - top)
    probs = powers / jnp.sum(powers, axis=-1, keepdims=True)
    probs_low = probs.astype(BF)
    mixed = jnp.einsum("bhqk,bkhe->bqhe", probs_low, v, preferred_element_type=F32).astype(BF)
    attention = to_tokens(mixed[:, :, None])
    attn_out = sum(
        lax.dot_general(attention[z], proj_whole[z], ACROSS, preferred_element_type=F32) for z in range(zs)
    )
    after_attn = joined + attn_out

    unit_two, std_two = normalise(after_attn)
    normed_two = (unit_two * gain_two + bias_two).astype(BF)
    two_both = jnp.concatenate([normed_two, core_swap(normed_two)], axis=0)
    ups = [gelu_pair(jnp.dot(two_both, w, preferred_element_type=F32)) for w in up_pieces]
    actives = [u[0].astype(BF) for u in ups]
    up_slopes = [u[1] for u in ups]
    mlp = sum(lax.dot_general(a, w, ACROSS, preferred_element_type=F32) for a, w in zip(actives, down_pieces))
    mlp_out = mlp[:tokens] + core_swap(mlp[tokens:].astype(BF)).astype(F32)

    def to_grid(v):
        every = lax.all_gather(v.astype(BF).reshape(grid_shape), "tensor", axis=0)
        return jnp.transpose(every, (1, 2, 0, 3, 4)).reshape(items, grid_rows, G, width).astype(F32)

    vit_out = to_grid(after_attn + mlp_out)

    grad_out = mine(d_vit).reshape(tokens, width)
    grad_mlp = grad_out.astype(BF)
    grad_mlp_both = jnp.concatenate([grad_mlp, core_swap(grad_mlp)], axis=0)
    grad_down = [
        lax.dot_general(grad_mlp_both, a, DOWN_ROWS, preferred_element_type=F32).astype(BF) for a in actives
    ]
    grad_ups = [
        (jnp.dot(grad_mlp_both, w, preferred_element_type=F32) * s).astype(BF) for w, s in zip(down_pieces, up_slopes)
    ]
    grad_up = [lax.dot_general(two_both, g, DOWN_ROWS, preferred_element_type=F32).astype(BF) for g in grad_ups]
    grad_two = sum(lax.dot_general(g, w, ACROSS, preferred_element_type=F32) for g, w in zip(grad_ups, up_pieces))
    grad_two = grad_two[:tokens] + core_swap(grad_two[tokens:].astype(BF)).astype(F32)
    grad_after = grad_out + normalise_back(grad_two, unit_two, std_two, gain_two)
    out_down = return_mlp_grad(grad_down)
    out_up = return_mlp_grad(grad_up)

    grad_att = grad_after.astype(BF)

    def return_rows(parts):
        whole = jnp.concatenate(parts, axis=0)
        return lax.psum_scatter(whole, ("tensor", "dp", "strip"), scatter_dimension=0, tiled=True).astype(F32)

    out_proj = return_rows(
        [lax.dot_general(grad_att, attention[z], DOWN_ROWS, preferred_element_type=F32).astype(BF) for z in range(zs)]
    )
    grad_mixed = [
        jnp.dot(grad_att, proj_whole[z], preferred_element_type=F32).astype(BF).reshape(tokens, 1, 2, group)
        for z in range(zs)
    ]
    grad_mixed = to_heads(grad_mixed)[:, :, 0]
    grad_probs = jnp.einsum("bqhe,bkhe->bhqk", grad_mixed, v, preferred_element_type=F32)
    row_dot = jnp.sum(probs * grad_probs, axis=-1, keepdims=True)
    grad_scores = (probs * (grad_probs - row_dot)).astype(BF)
    grad_q = jnp.einsum("bhqk,bkhe->bqhe", grad_scores, k, preferred_element_type=F32) * score_scale
    grad_k = jnp.einsum("bhqk,bqhe->bkhe", grad_scores, q, preferred_element_type=F32) * score_scale
    grad_v = jnp.einsum("bhqk,bqhe->bkhe", probs_low, grad_mixed, preferred_element_type=F32)
    grad_qkv = to_tokens(jnp.stack([grad_q, grad_k, grad_v], axis=2).astype(BF))
    out_qkv = return_rows(
        [lax.dot_general(normed_one, grad_qkv[z], DOWN_ROWS, preferred_element_type=F32).astype(BF) for z in range(zs)]
    )
    grad_one = sum(
        lax.dot_general(grad_qkv[z], qkv_whole[z], ACROSS, preferred_element_type=F32) for z in range(zs)
    )
    grad_joined = grad_after + normalise_back(grad_one, unit_one, std_one, gain_one)
    grad_vit = to_grid(grad_joined)

    grad_grid = grad_joined.reshape(grid_shape)
    over = (0, 1, 2)
    grad_gate = jnp.sum(grad_grid * local_mix, axis=over) * (1.0 - gate * gate)
    grad_mix = grad_grid * gate
    grad_adapted = depthwise3(rim(grad_mix), mix_kernel[:, ::-1], grid_rows, grid_cols)
    grad_adapted = grad_adapted.astype(BF).reshape(tokens, width)
    grad_taps = [
        jnp.sum(adapted_pad[:, i : i + grid_rows, j : j + grid_cols] * grad_mix, axis=over)
        for i in range(3)
        for j in range(3)
    ]
    small_vit = jnp.stack(
        grad_taps
        + [
            grad_gate,
            jnp.sum(grad_one * unit_one, axis=0),
            jnp.sum(grad_one, axis=0),
            jnp.sum(grad_two * unit_two, axis=0),
            jnp.sum(grad_two, axis=0),
        ],
        axis=0,
    )
    grad_adapt = lax.dot_general(pooled_low, grad_adapted, DOWN_ROWS, preferred_element_type=F32).astype(BF)
    grad_adapt = lax.psum_scatter(grad_adapt, ("dp", "strip"), scatter_dimension=0, tiled=True)
    out_adapt = all_sum(grad_adapt.astype(F32), ("tensor",))
    grad_pooled = lax.dot_general(grad_adapted, adapt_w, ACROSS, preferred_element_type=F32).astype(BF)
    grad_pooled = grad_pooled.reshape(items, -1, channels)
    grad_pooled = jnp.concatenate(
        [shift(grad_pooled, "tensor", 1), grad_pooled, shift(grad_pooled, "tensor", -1)], axis=1
    )
    grad_map = lax.dot_general(pool, grad_pooled, (((1,), (1,)), ((0,), (0,))), preferred_element_type=F32)
    grad_map = jnp.swapaxes(d_map, 1, 2).astype(F32) + grad_map.reshape(masked.shape)

    kept = cell_mask * grad_map
    grad_scale = jnp.sum(kept * branch, axis=over)
    grad_branch = (kept * layer_scale).astype(BF).reshape(cells, channels)
    grad_branch_both = jnp.concatenate([grad_branch, core_swap(grad_branch)], axis=0)
    grad_reduce = [
        lax.dot_general(grad_branch_both, a, DOWN_ROWS, preferred_element_type=F32).astype(BF) for a in acts
    ]
    out_reduce = return_conv_grad(grad_reduce)
    grad_hidden = [
        (jnp.dot(grad_branch_both, w, preferred_element_type=F32) * s.astype(F32)).astype(BF)
        for w, s in zip(reduce_pieces, slopes)
    ]
    grad_expand = [
        lax.dot_general(normed_both, g, DOWN_ROWS, preferred_element_type=F32).astype(BF) for g in grad_hidden
    ]
    out_expand = return_conv_grad(grad_expand)
    normed_there = core_swap(back_sum(grad_hidden, expand_pieces, cells, cells, BF))
    grad_normed = back_sum(grad_hidden, expand_pieces, 0, cells, F32) + normed_there.astype(F32)
    unit_full = conv_unit.astype(F32)
    grad_spread = normalise_back(grad_normed, unit_full, conv_std, conv_gain)
    grad_spread = grad_spread.astype(BF).reshape(masked.shape)
    grad_taps = tap_grad(padded, grad_spread.astype(F32), map_rows, map_cols)
    small_conv = jnp.concatenate(
        [
            grad_taps.reshape(56, channels),
            jnp.sum(grad_normed * unit_full, axis=0)[None],
            jnp.sum(grad_normed, axis=0)[None],
            grad_scale[None],
        ],
        axis=0,
    )
    grad_map_in = conv7(wide_rim(grad_spread), taps[::-1, [6, 5, 4, 3, 2, 1, 0, 7]], map_rows, map_cols)
    grad_map_in = jnp.swapaxes(cell_mask * (kept + grad_map_in), 1, 2)

    everywhere = ("strip", "tensor", "dp")
    small_vit = all_sum(small_vit, everywhere)
    small_conv = all_sum(small_conv, everywhere)
    vit_share = width // (2 * dps)
    small_vit = lax.dynamic_slice_in_dim(small_vit, (dp_at * 2 + strip_at) * vit_share, vit_share, 1)
    conv_share = channels // (2 * zs)
    small_conv = lax.dynamic_slice_in_dim(small_conv, (strip_at * zs + tensor_at) * conv_share, conv_share, 1)
    out_taps = small_conv[:56].reshape(7, 8, conv_share)[:, :7].reshape(49, conv_share).T
    return (
        vit_out,
        map_out,
        grad_vit,
        grad_map_in,
        out_taps,
        small_conv[56],
        small_conv[57],
        out_expand,
        out_reduce,
        small_conv[58],
        out_adapt,
        small_vit[:9].T,
        small_vit[9],
        small_vit[10],
        small_vit[11],
        out_qkv.reshape(-1, 3, head_cols),
        out_proj,
        small_vit[12],
        small_vit[13],
        out_up,
        out_down,
    )


def solution(mesh):
    rows = P("dp", "strip", None, None)
    maps = P("dp", "strip", "tensor", None)
    conv = ("strip", "tensor")
    vit = ("dp", "strip")
    in_specs = (
        P("dp"), rows, maps, P(), P(), P(), P(conv, None), P(conv, None), P(), P(), P(), P(), P(), P(),
        P(None, None, "tensor"), P(None, "tensor"), P(), P(), P(None, "tensor"), P(None, "tensor"), rows, maps,
    )
    out_specs = (
        rows, maps, rows, maps, P(conv, None), P(conv), P(conv), P(conv, None), P(conv, None), P(conv),
        P(vit, None), P(vit, None), P(vit), P(vit), P(vit), P(vit, None, "tensor"), P(vit, "tensor"), P(vit), P(vit),
        P(vit, "tensor"), P(vit, "tensor"),
    )
    return jax.shard_map(shards, mesh=mesh, in_specs=in_specs, out_specs=out_specs, check_vma=False)
```

time: 3750 us -> 1510 us (0.40)
  waiting for transfers between devices: 2050 us -> 537 us
  blocking collectives: 356 us -> 0 us
  other arithmetic: 480 us -> 170 us
  matrix products: 518 us -> 211 us
  Pallas kernels: 0 us -> 187 us
  starting transfers between devices: 86.8 us -> 142 us
    reduce_scatter x8 -> x5, waiting for transfers between devices: 1270 us -> 54.3 us  [the longest x2 54.2 us: return_rows(): lax.psum_scatter(whole, ('tensor', 'dp', 'strip'), scatter_dimension=0, t...]
    psum x4 -> x0, waiting for transfers between devices: 697 us -> none  [the longest x1 242 us: shards(): mlp_out = lax.psum(mlp_part, 'tensor')]
    ppermute x36 -> x84, waiting for transfers between devices: 23.9 us -> 435 us  [the longest x40 223 us: dp_swap(): lax.ppermute(v, 'dp', [(i, i ^ bit) for i in range(lax.axis_size('dp'))])]
    dot_general x87 -> x68, matrix products: 498 us -> 194 us  [the longest x4 34.9 us: shards(): jnp.dot(grad_branch_both, w, preferred_element_type=F32) * s.astype(F32)]
    reduce_sum x42 -> x9, other arithmetic: 286 us -> 30.6 us  [the longest x2 8.93 us: normalise(): center = jnp.mean(v, axis=-1, keepdims=True)]
    psum x2 -> x0, blocking collectives: 201 us -> none  [the longest x1 183 us: shards(): pooled = lax.psum(pooled_part, 'tensor')]
    pallas_call x0 -> x11, Pallas kernels: none -> 187 us  [the longest x4 65.8 us: back_sum(): pl.pallas_call(functools.partial(back_sum_kernel, len(parts)), grid=(n //...]
    unnamed x2 -> x0, blocking collectives: 127 us -> none
  transfers between devices with their start and end apart: 57 -> 104, of which waited for: 14 -> 44; matrix products, arithmetic and copies ran while one was open for 25% -> 37% of each run, Pallas kernels for 0% -> 12%
where the time goes in v1:
time: 1510 us; the launch traced here: 1500 us
  waiting for transfers between devices  537 us (36%)
  local copies, waits for them, and re-layouts  233 us (15%)
  matrix products  211 us (14%)
  Pallas kernels  187 us (12%)
  other arithmetic  170 us (11%)
  starting transfers between devices  142 us (9%)
  between operations  18.1 us (1%)
    ppermute x40, waiting for transfers between devices, dp_swap(): lax.ppermute(v, 'dp', [(i, i ^ bit) for i in range(lax.axis_size('dp'))])  223 us
    ppermute x20, waiting for transfers between devices, shift(): return lax.ppermute(v, axis, pairs)  130 us
    ppermute x12, waiting for transfers between devices, all_sum(): v = v + lax.ppermute(v, axis, [(i, i ^ bit) for i in range(count)])  77 us
    pallas_call x4, Pallas kernels, back_sum(): pl.pallas_call(functools.partial(back_sum_kernel, len(parts)), grid=(n //...  65.8 us
    pallas_call x2, Pallas kernels, conv7(): pl.pallas_call(functools.partial(conv7_kernel, rows, cols), grid=(items,...  56.6 us
    reduce_scatter x2, waiting for transfers between devices, return_rows(): lax.psum_scatter(whole, ('tensor', 'dp', 'strip'), scatter_dimension=0, t...  54.2 us
    ppermute x20, starting transfers between devices, shift(): return lax.ppermute(v, axis, pairs)  46.9 us
    ppermute x40, starting transfers between devices, dp_swap(): lax.ppermute(v, 'dp', [(i, i ^ bit) for i in range(lax.axis_size('dp'))])  44 us
  transfers between devices with their start and end apart: 104, of which 44 were waited for; matrix products, arithmetic and copies ran while one was open for 37% of the time, Pallas kernels for 12%

profile of v1, /device:TPU:0, one launch (start us, length us, event | category | flops | bytes accessed | tf_op | source)
XLA Modules:
  0.0 1498.2 jit_solution(16250208725213797608)
XLA Ops:
  43.2 27.8 %collective-permute-done = bf16[3,3,24,1536]{3,2,1,0:T(8,128)(2,1)S(1)} collective-permute-done((bf16[3,3,24,1536]{3,2,1,0:T(8,128)(2,1)S(1)}, bf16[3,3,24,1536]{3,2,1,0:T(8,128)(2,1)S(1)}, u32[]{:S(2)}, u32[]{:S(2)}) %collective-permute-start) | collective-permute-done | bytes 663584 | tf_op jit(solution)/shard_map/ppermute | solution.py:33
  71.1 18.9 %collective-permute-done.1 = bf16[3,3,24,1536]{3,2,1,0:T(8,128)(2,1)S(1)} collective-permute-done((bf16[3,3,24,1536]{3,2,1,0:T(8,128)(2,1)S(1)}, bf16[3,3,24,1536]{3,2,1,0:T(8,128)(2,1)S(1)}, u32[]{:S(2)}, u32[]{:S(2)}) %collective-permute-start.1) | collective-permute-done | bytes 663584 | tf_op jit(solution)/shard_map/ppermute | solution.py:33
  109.9 28.2 %depthwise.2 = f32[3,12,24,1536]{3,2,1,0:T(8,128)S(1)} custom-call(bf16[3,18,40,1536]{3,2,1,0:T(8,128)(2,1)} %pad_maximum_fusion.x_ref, f32[7,8,1536]{2,1,0:T(8,128)S(1)} %pad.4.k_ref), custom_call_target="tpu_custom_call" | custom-call | flops 130056192 | bytes 11943936 | tf_op jit(solution)/shard_map/depthwise/pallas_call | solution.py:192
  170.2 64.0 %collective-permute-done.6.w_ref.refs_5_ = bf16[1536,768]{1,0:T(8,128)(2,1)} collective-permute-done((bf16[1536,768]{1,0:T(8,128)(2,1)}, bf16[1536,768]{1,0:T(8,128)(2,1)}, u32[]{:S(2)}, u32[]{:S(2)}) %collective-permute-start.6) | collective-permute-done | bytes 2359328 | tf_op jit(solution)/shard_map/ppermute | solution.py:27
  245.4 39.4 %collective-permute-done.11.refs_5_ = bf16[1536,768]{1,0:T(8,128)(2,1)} collective-permute-done((bf16[1536,768]{1,0:T(8,128)(2,1)}, bf16[1536,768]{1,0:T(8,128)(2,1)}, u32[]{:S(2)}, u32[]{:S(2)}) %collective-permute-start.11) | collective-permute-done | bytes 2359328 | tf_op jit(solution)/shard_map/ppermute | solution.py:27
  288.7 9.0 expand_gelu.4
  302.1 9.0 expand_gelu.6
  312.6 9.0 expand_gelu.5
  345.2 15.7 %reduce_sum.345 = bf16[864,1536]{1,0:T(8,128)(2,1)} custom-call(bf16[1728,768]{1,0:T(8,128)(2,1)} %copy-done.6, bf16[1728,768]{1,0:T(8,128)(2,1)} %copy-done.8, bf16[1728,768]{1,0:T(8,128)(2,1)} %copy-done.10, bf16[1728,768]{1,0:T(8,128)(2,1)} %copy-done.12, bf16[1536,768]{1,0:T(8,128)(2,1)} %bitcast.13.refs_4_, ...), custom_call_target="tpu_custom_call" | custom-call | flops 8153726976 | bytes 20054016 | tf_op jit(solution)/shard_map/reduce_sum/pallas_call | solution.py:309
  370.3 16.6 %reduce_sum.344 = f32[864,1536]{1,0:T(8,128)} custom-call(bf16[1728,768]{1,0:T(8,128)(2,1)} %copy-done.6, bf16[1728,768]{1,0:T(8,128)(2,1)} %copy-done.8, bf16[1728,768]{1,0:T(8,128)(2,1)} %copy-done.10, bf16[1728,768]{1,0:T(8,128)(2,1)} %copy-done.12, bf16[1536,768]{1,0:T(8,128)(2,1)} %bitcast.13.refs_4_, ...), custom_call_target="tpu_custom_call" | custom-call | flops 8153726976 | bytes 20054016 | tf_op jit(solution)/shard_map/reduce_sum/pallas_call | solution.py:309
  448.4 10.3 collective-permute-done.21
  531.9 18.6 %all-to-all-done = bf16[8,3,72,384]{3,2,1,0:T(8,128)(2,1)} async-done(((bf16[8,3,72,384]{3,2,1,0:T(8,128)(2,1)}), bf16[8,3,72,384]{3,2,1,0:T(8,128)(2,1)}, u32[]{:S(2)}, u32[]{:S(2)}) %all-to-all-start) | async-done | bytes 1327136 | tf_op jit(solution)/shard_map/all_to_all | solution.py:446
  702.6 9.4 multiply_convert_fusion
  757.9 20.9 %all-to-all-done.3 = bf16[8,3,72,384]{3,2,1,0:T(8,128)(2,1)} async-done(((bf16[8,3,72,384]{3,2,1,0:T(8,128)(2,1)}), bf16[8,3,72,384]{3,2,1,0:T(8,128)(2,1)}, u32[]{:S(2)}, u32[]{:S(2)}) %all-to-all-start.3) | async-done | bytes 1327136 | tf_op jit(solution)/shard_map/all_to_all | solution.py:452
  840.0 12.0 collective-permute-done.38
  906.9 8.9 multiply_convert_fusion.1.refs_3_
  944.9 10.0 multiply_convert_fusion.4.refs_0_
  965.1 29.1 %collective-permute-done.53 = bf16[1536,768]{1,0:T(8,128)(2,1)S(1)} collective-permute-done((bf16[1536,768]{1,0:T(8,128)(2,1)S(1)}, bf16[1536,768]{1,0:T(8,128)(2,1)S(1)}, u32[]{:S(2)}, u32[]{:S(2)}) %collective-permute-start.53) | collective-permute-done | bytes 2359328 | tf_op jit(solution)/shard_map/ppermute | solution.py:27
  996.6 17.3 %collective-permute-done.51 = bf16[1536,768]{1,0:T(8,128)(2,1)S(1)} collective-permute-done((bf16[1536,768]{1,0:T(8,128)(2,1)S(1)}, bf16[1536,768]{1,0:T(8,128)(2,1)S(1)}, u32[]{:S(2)}, u32[]{:S(2)}) %collective-permute-start.51) | collective-permute-done | bytes 2359328 | tf_op jit(solution)/shard_map/ppermute | solution.py:27
  1022.1 17.0 %collective-permute-done.63 = bf16[768,768]{1,0:T(8,128)(2,1)S(1)} collective-permute-done((bf16[768,768]{1,0:T(8,128)(2,1)S(1)}, bf16[768,768]{1,0:T(8,128)(2,1)S(1)}, u32[]{:S(2)}, u32[]{:S(2)}) %collective-permute-start.63) | collective-permute-done | bytes 1179680 | tf_op jit(solution)/shard_map/ppermute | solution.py:27
  1041.8 22.3 %collective-permute-done.54 = bf16[768,768]{1,0:T(8,128)(2,1)S(1)} collective-permute-done((bf16[768,768]{1,0:T(8,128)(2,1)S(1)}, bf16[768,768]{1,0:T(8,128)(2,1)S(1)}, u32[]{:S(2)}, u32[]{:S(2)}) %collective-permute-start.54) | collective-permute-done | bytes 1179680 | tf_op jit(solution)/shard_map/ppermute | solution.py:27
  1069.0 16.7 %reduce_sum.347 = bf16[864,1536]{1,0:T(8,128)(2,1)} custom-call(bf16[1728,768]{1,0:T(8,128)(2,1)} %multiply_convert_fusion.4.refs_0_, bf16[1728,768]{1,0:T(8,128)(2,1)} %copy-done.135, bf16[1728,768]{1,0:T(8,128)(2,1)} %copy-done.133, bf16[1728,768]{1,0:T(8,128)(2,1)} %copy-done.134, bf16[1536,768]{1,0:T(8,128)(2,1)} %bitcast.8.w_ref.refs_4_, ...), custom_call_target="tpu_custom_call" | custom-call | flops 8153726976 | bytes 20054016 | tf_op jit(solution)/shard_map/reduce_sum/pallas_call | solution.py:309
  1093.4 16.8 %reduce_sum.346 = f32[864,1536]{1,0:T(8,128)} custom-call(bf16[1728,768]{1,0:T(8,128)(2,1)} %multiply_convert_fusion.4.refs_0_, bf16[1728,768]{1,0:T(8,128)(2,1)} %copy-done.135, bf16[1728,768]{1,0:T(8,128)(2,1)} %copy-done.133, bf16[1728,768]{1,0:T(8,128)(2,1)} %copy-done.134, bf16[1536,768]{1,0:T(8,128)(2,1)} %bitcast.8.w_ref.refs_4_, ...), custom_call_target="tpu_custom_call" | custom-call | flops 8153726976 | bytes 20054016 | tf_op jit(solution)/shard_map/reduce_sum/pallas_call | solution.py:309
  1122.5 27.6 %collective-permute-done.42 = bf16[3,3,24,1536]{3,2,1,0:T(8,128)(2,1)S(1)} collective-permute-done((bf16[3,3,24,1536]{3,2,1,0:T(8,128)(2,1)S(1)}, bf16[3,3,24,1536]{3,2,1,0:T(8,128)(2,1)S(1)}, u32[]{:S(2)}, u32[]{:S(2)}) %collective-permute-start.42) | collective-permute-done | bytes 663584 | tf_op jit(solution)/shard_map/ppermute | solution.py:33
  1150.1 11.6 collective-permute-done.43
  1183.3 10.3 collective-permute-done.73
  1201.6 28.9 %tap_grad.1 = f32[7,8,1536]{2,1,0:T(8,128)S(1)} custom-call(bf16[3,18,40,1536]{3,2,1,0:T(8,128)(2,1)} %pad_maximum_fusion.x_ref, f32[3,12,24,1536]{3,2,1,0:T(8,128)S(1)} %convert_element_type.601.g_ref), custom_call_target="tpu_custom_call" | custom-call | flops 130056192 | bytes 11943936 | tf_op jit(solution)/shard_map/tap_grad/pallas_call | solution.py:235
  1235.4 28.4 %depthwise.3 = f32[3,12,24,1536]{3,2,1,0:T(8,128)S(1)} custom-call(bf16[3,18,40,1536]{3,2,1,0:T(8,128)(2,1)} %pad_maximum_fusion.1.x_ref, f32[7,8,1536]{2,1,0:T(8,128)S(1)} %rev.8.k_ref), custom_call_target="tpu_custom_call" | custom-call | flops 130056192 | bytes 11943936 | tf_op jit(solution)/shard_map/depthwise/pallas_call | solution.py:192
  1291.9 19.2 %collective-permute-done.47 = f32[59,1536]{1,0:T(8,128)S(1)} collective-permute-done((f32[59,1536]{1,0:T(8,128)S(1)}, f32[59,1536]{1,0:T(8,128)S(1)}, u32[]{:S(2)}, u32[]{:S(2)}) %collective-permute-start.47) | collective-permute-done | bytes 362528 | tf_op jit(solution)/shard_map/ppermute | solution.py:40
  1325.0 9.3 collective-permute-done.48
  1354.4 25.3 %collective-permute-done.70 = f32[192,1024]{1,0:T(8,128)} collective-permute-done((f32[192,1024]{1,0:T(8,128)S(1)}, f32[192,1024]{1,0:T(8,128)}, u32[]{:S(2)}, u32[]{:S(2)}) %collective-permute-start.70) | collective-permute-done | bytes 786464 | tf_op jit(solution)/shard_map/ppermute | solution.py:40
  1392.7 54.2 %reduce-scatter.14.cloned.1.call-done = bf16[128,768]{1,0:T(8,128)(2,1)} async-done(((bf16[4096,768]{1,0:T(8,128)(2,1)}), bf16[128,768]{1,0:T(8,128)(2,1)}) %reduce-scatter.14.cloned.1.call-update) | async-done | bytes 196624 | tf_op jit(solution)/shard_map/reduce_scatter | solution.py:506
  (840 shorter events, 818.4 us)
Async XLA Ops:
  7.2 152.5 %all-gather.21.cloned.1.call-start = ((), (), s32[]{:S(2)}) async-start(), calls=%async_computation.20 | async-start | bytes 2949120 | tf_op jit(solution)/shard_map/all_gather | solution.py:104
  27.4 138.5 %all-gather.23.cloned.1.call-start = ((), (), s32[]{:S(2)}) async-start(), calls=%async_computation.21 | async-start | bytes 2949120 | tf_op jit(solution)/shard_map/all_gather | solution.py:104
  33.4 444.0 %all-gather.13.cloned.1.call-start = ((), (), s32[]{:S(2)}) async-start(), calls=%async_computation.11 | async-start | bytes 6488064 | tf_op jit(solution)/shard_map/all_gather | solution.py:163
  99.6 419.2 %all-gather.25.cloned.1.call-start = ((), (), s32[]{:S(2)}) async-start(), calls=%async_computation.22 | async-start | bytes 1310720 | tf_op jit(solution)/shard_map/all_gather | solution.py:132
  157.5 79.8 %collective-permute-start.4 = (bf16[864,1536]{1,0:T(8,128)(2,1)}, bf16[864,1536]{1,0:T(8,128)(2,1)}, u32[]{:S(2)}, u32[]{:S(2)}) collective-permute-start(bf16[864,1536]{1,0:T(8,128)(2,1)} %get-tuple-element.158), channel_id=1, source_target_pairs={{0,4},{4,0},{1,5},{5,1},{2,6},{6,2},{3,7},{7,3},{8,12},{12,8},{9,1... | collective-permute-start | bytes 7962632 | tf_op jit(solution)/shard_map/ppermute | solution.py:23
  164.4 78.1 %collective-permute-start.7 = (bf16[1536,768]{1,0:T(8,128)(2,1)}, bf16[1536,768]{1,0:T(8,128)(2,1)}, u32[]{:S(2)}, u32[]{:S(2)}) collective-permute-start(bf16[1536,768]{1,0:T(8,128)(2,1)} %bitcast.8.w_ref.refs_4_), channel_id=1, source_target_pairs={{0,16},{8,24},{16,0},{24,8},{1,17},{9,25},{17,1},{25,9},{2,18},{10... | collective-permute-start | bytes 7077896 | tf_op jit(solution)/shard_map/ppermute | solution.py:27
  169.2 115.6 %collective-permute-start.11 = (bf16[1536,768]{1,0:T(8,128)(2,1)}, bf16[1536,768]{1,0:T(8,128)(2,1)}, u32[]{:S(2)}, u32[]{:S(2)}) collective-permute-start(bf16[1536,768]{1,0:T(8,128)(2,1)} %bitcast.13.refs_4_), channel_id=1, source_target_pairs={{0,8},{8,0},{16,24},{24,16},{1,9},{9,1},{17,25},{25,17},{2,10},{10... | collective-permute-start | bytes 7077896 | tf_op jit(solution)/shard_map/ppermute | solution.py:27
  169.7 129.5 %collective-permute-start.12 = (bf16[1536,768]{1,0:T(8,128)(2,1)}, bf16[1536,768]{1,0:T(8,128)(2,1)}, u32[]{:S(2)}, u32[]{:S(2)}) collective-permute-start(bf16[1536,768]{1,0:T(8,128)(2,1)} %bitcast.13.refs_4_), channel_id=1, source_target_pairs={{0,16},{8,24},{16,0},{24,8},{1,17},{9,25},{17,1},{25,9},{2,18},{10... | collective-permute-start | bytes 7077896 | tf_op jit(solution)/shard_map/ppermute | solution.py:27
  235.6 86.0 %collective-permute-start.8 = (bf16[768,768]{1,0:T(8,128)(2,1)S(1)}, bf16[768,768]{1,0:T(8,128)(2,1)S(1)}, u32[]{:S(2)}, u32[]{:S(2)}) collective-permute-start(bf16[768,768]{1,0:T(8,128)(2,1)S(1)} %slice.618), channel_id=1, source_target_pairs={{0,16},{8,24},{16,0},{24,8},{1,17},{9,25},{17,1},{25,9},{2,18},{10... | collective-permute-start | bytes 3538952 | tf_op jit(solution)/shard_map/ppermute | solution.py:27
  243.8 81.6 %collective-permute-start.9 = (bf16[768,768]{1,0:T(8,128)(2,1)S(1)}, bf16[768,768]{1,0:T(8,128)(2,1)S(1)}, u32[]{:S(2)}, u32[]{:S(2)}) collective-permute-start(bf16[768,768]{1,0:T(8,128)(2,1)S(1)} %slice.619), channel_id=1, source_target_pairs={{0,8},{8,0},{16,24},{24,16},{1,9},{9,1},{17,25},{25,17},{2,10},{10... | collective-permute-start | bytes 3538952 | tf_op jit(solution)/shard_map/ppermute | solution.py:27
  410.7 115.7 %all-gather.27.cloned.1.call-start = ((), (), s32[]{:S(2)}) async-start(), calls=%async_computation.23 | async-start | bytes 1310720 | tf_op jit(solution)/shard_map/all_gather | solution.py:132
  516.9 83.9 %all-gather.15.cloned.1.call-start = ((), (), s32[]{:S(2)}) async-start(), calls=%async_computation.12 | async-start | bytes 2162688 | tf_op jit(solution)/shard_map/all_gather | solution.py:163
  641.3 95.0 %collective-permute-start.78 = (bf16[1024,512]{0,1:T(8,128)(2,1)}, bf16[1024,512]{0,1:T(8,128)(2,1)}, u32[]{:S(2)}, u32[]{:S(2)}) collective-permute-start(bf16[1024,512]{0,1:T(8,128)(2,1)} %pad_maximum_fusion.26), channel_id=1, source_target_pairs={{0,16},{8,24},{16,0},{24,8},{1,17},{9,25},{17,1},{25,9},{2,18},{10... | collective-permute-start | bytes 3145736 | tf_op jit(solution)/shard_map/ppermute | solution.py:27
  647.1 92.2 %collective-permute-start.76 = (bf16[1024,512]{0,1:T(8,128)(2,1)}, bf16[1024,512]{0,1:T(8,128)(2,1)}, u32[]{:S(2)}, u32[]{:S(2)}) collective-permute-start(bf16[1024,512]{0,1:T(8,128)(2,1)} %pad_maximum_fusion.25), channel_id=1, source_target_pairs={{0,8},{8,0},{16,24},{24,16},{1,9},{9,1},{17,25},{25,17},{2,10},{10... | collective-permute-start | bytes 3145736 | tf_op jit(solution)/shard_map/ppermute | solution.py:27
  675.0 594.5 %all-gather.17.cloned.1.call-start = ((), (), s32[]{:S(2)}) async-start(), calls=%async_computation.13 | async-start | bytes 2949120 | tf_op jit(solution)/shard_map/all_gather | solution.py:481
  732.8 546.0 %reduce-scatter.20.cloned.1.call-start = ((), (), s32[]{:S(2)}) async-start(), calls=%async_computation.19 | async-start | bytes 1310720 | tf_op jit(solution)/shard_map/reduce_scatter | solution.py:144
  736.3 547.8 %reduce-scatter.18.cloned.1.call-start = ((), (), s32[]{:S(2)}) async-start(), calls=%async_computation.18 | async-start | bytes 1310720 | tf_op jit(solution)/shard_map/reduce_scatter | solution.py:144
  757.4 529.9 %reduce-scatter.12.cloned.1.call-start = ((), (), s32[]{:S(2)}) async-start(), calls=%async_computation.15 | async-start | bytes 3538944 | tf_op jit(solution)/shard_map/reduce_scatter | solution.py:555
  831.6 491.9 %reduce-scatter.16.cloned.1.call-start = ((), (), s32[]{:S(2)}) async-start(), calls=%async_computation.17 | async-start | bytes 2162688 | tf_op jit(solution)/shard_map/reduce_scatter | solution.py:506
  863.3 472.8 %all-reduce.6.cloned.1.call-start = ((), (), s32[]{:S(2)}) async-start(), calls=%async_computation.24 | async-start | bytes 9437184
  880.3 81.8 %collective-permute-start.62 = (bf16[1536,768]{1,0:T(8,128)(2,1)S(1)}, bf16[1536,768]{1,0:T(8,128)(2,1)S(1)}, u32[]{:S(2)}, u32[]{:S(2)}) collective-permute-start(bf16[1536,768]{1,0:T(8,128)(2,1)S(1)} %pad_maximum_fusion.9), channel_id=1, source_target_pairs={{0,16},{8,24},{16,0},{24,8},{1,17},{9,25},{17,1},{25,9},{2,18},{10... | collective-permute-start | bytes 7077896 | tf_op jit(solution)/shard_map/ppermute | solution.py:27
  889.4 73.8 %collective-permute-start.60 = (bf16[1536,768]{1,0:T(8,128)(2,1)S(1)}, bf16[1536,768]{1,0:T(8,128)(2,1)S(1)}, u32[]{:S(2)}, u32[]{:S(2)}) collective-permute-start(bf16[1536,768]{1,0:T(8,128)(2,1)S(1)} %pad_maximum_fusion.8), channel_id=1, source_target_pairs={{0,8},{8,0},{16,24},{24,16},{1,9},{9,1},{17,25},{25,17},{2,10},{10... | collective-permute-start | bytes 7077896 | tf_op jit(solution)/shard_map/ppermute | solution.py:27
  962.4 76.7 %collective-permute-start.63 = (bf16[768,768]{1,0:T(8,128)(2,1)S(1)}, bf16[768,768]{1,0:T(8,128)(2,1)S(1)}, u32[]{:S(2)}, u32[]{:S(2)}) collective-permute-start(bf16[768,768]{1,0:T(8,128)(2,1)S(1)} %add_convert_fusion.1), channel_id=1, source_target_pairs={{0,8},{8,0},{16,24},{24,16},{1,9},{9,1},{17,25},{25,17},{2,10},{10... | collective-permute-start | bytes 3538952 | tf_op jit(solution)/shard_map/ppermute | solution.py:27
  963.5 75.7 %collective-permute-start.61 = (bf16[768,768]{1,0:T(8,128)(2,1)S(1)}, bf16[768,768]{1,0:T(8,128)(2,1)S(1)}, u32[]{:S(2)}, u32[]{:S(2)}) collective-permute-start(bf16[768,768]{1,0:T(8,128)(2,1)S(1)} %add_convert_fusion.3), channel_id=1, source_target_pairs={{0,16},{8,24},{16,0},{24,8},{1,17},{9,25},{17,1},{25,9},{2,18},{10... | collective-permute-start | bytes 3538952 | tf_op jit(solution)/shard_map/ppermute | solution.py:27
  1066.7 314.5 %all-gather.19.cloned.1.call-start = ((), (), s32[]{:S(2)}) async-start(), calls=%async_computation.14 | async-start | bytes 2949120 | tf_op jit(solution)/shard_map/all_gather | solution.py:481
  1068.7 378.3 %reduce-scatter.14.cloned.1.call-start = ((), (), s32[]{:S(2)}) async-start(), calls=%async_computation.16 | async-start | bytes 6488064 | tf_op jit(solution)/shard_map/reduce_scatter | solution.py:506
  1199.3 86.6 %collective-permute-start.75 = (f32[14,1024]{1,0:T(8,128)S(1)}, f32[14,1024]{1,0:T(8,128)}, u32[]{:S(2)}, u32[]{:S(2)}) collective-permute-start(f32[14,1024]{1,0:T(8,128)S(1)} %add.655), channel_id=1, source_target_pairs={{0,16},{8,24},{16,0},{24,8},{1,17},{9,25},{17,1},{25,9},{2,18},{10... | collective-permute-start | bytes 172040 | tf_op jit(solution)/shard_map/ppermute | solution.py:40
  1345.5 103.5 %collective-permute-start.50 = (f32[59,1536]{1,0:T(8,128)S(1)}, f32[59,1536]{1,0:T(8,128)}, u32[]{:S(2)}, u32[]{:S(2)}) collective-permute-start(f32[59,1536]{1,0:T(8,128)S(1)} %add.633), channel_id=1, source_target_pairs={{0,16},{8,24},{16,0},{24,8},{1,17},{9,25},{17,1},{25,9},{2,18},{10... | collective-permute-start | bytes 1087496 | tf_op jit(solution)/shard_map/ppermute | solution.py:40
  1350.1 99.8 %collective-permute-start.65 = (bf16[192,2,768]{2,0,1:T(8,128)(2,1)}, bf16[192,2,768]{2,0,1:T(8,128)(2,1)}, u32[]{:S(2)}, u32[]{:S(2)}) collective-permute-start(bf16[192,2,768]{2,0,1:T(8,128)(2,1)} %maximum_bitcast_fusion.4), channel_id=1, source_target_pairs={{0,8},{8,0},{16,24},{24,16},{1,9},{9,1},{17,25},{25,17},{2,10},{10... | collective-permute-start | bytes 1769480 | tf_op jit(solution)/shard_map/ppermute | solution.py:27
  1351.6 101.5 %collective-permute-start.67 = (bf16[192,2,768]{2,0,1:T(8,128)(2,1)}, bf16[192,2,768]{2,0,1:T(8,128)(2,1)}, u32[]{:S(2)}, u32[]{:S(2)}) collective-permute-start(bf16[192,2,768]{2,0,1:T(8,128)(2,1)} %maximum_bitcast_fusion.4), channel_id=1, source_target_pairs={{0,16},{8,24},{16,0},{24,8},{1,17},{9,25},{17,1},{25,9},{2,18},{10... | collective-permute-start | bytes 1769480 | tf_op jit(solution)/shard_map/ppermute | solution.py:27
  1354.0 102.0 %collective-permute-start.56 = (bf16[192,2,768]{2,0,1:T(8,128)(2,1)}, bf16[192,2,768]{2,0,1:T(8,128)(2,1)S(1)}, u32[]{:S(2)}, u32[]{:S(2)}) collective-permute-start(bf16[192,2,768]{2,0,1:T(8,128)(2,1)} %maximum_bitcast_fusion.3), channel_id=1, source_target_pairs={{0,8},{8,0},{16,24},{24,16},{1,9},{9,1},{17,25},{25,17},{2,10},{10... | collective-permute-start | bytes 1769480 | tf_op jit(solution)/shard_map/ppermute | solution.py:27
  1379.8 77.7 %collective-permute-start.58 = (bf16[192,2,768]{2,0,1:T(8,128)(2,1)}, bf16[192,2,768]{2,0,1:T(8,128)(2,1)S(1)}, u32[]{:S(2)}, u32[]{:S(2)}) collective-permute-start(bf16[192,2,768]{2,0,1:T(8,128)(2,1)} %maximum_bitcast_fusion.3), channel_id=1, source_target_pairs={{0,16},{8,24},{16,0},{24,8},{1,17},{9,25},{17,1},{25,9},{2,18},{10... | collective-permute-start | bytes 1769480 | tf_op jit(solution)/shard_map/ppermute | solution.py:27
  (217 other events, 4705.7 us)
Sparse Core Ops, SparseCore 0:
  27.5 66.9 all-gather.20
  96.1 49.4 all-gather.22
  149.0 99.6 all-gather.12
  410.8 26.1 all-gather.24
  438.4 34.2 all-gather.26
  520.3 68.9 all-gather.14
  679.3 50.9 all-gather.16
  736.5 45.9 reduce-scatter.19
  784.9 25.4 reduce-scatter.17
  831.7 44.6 reduce-scatter.11
  878.8 139.7 reduce-scatter.15
  1066.8 186.4 all-reduce.5
  1254.9 58.7 all-gather.18
  1319.2 127.6 reduce-scatter.13

commit v2 on v1

v2 whole, which is shorter than its diff:
```python
import functools

import jax
import jax.numpy as jnp
from jax import lax
from jax.experimental import pallas as pl
from jax.experimental.pallas import tpu as pltpu
from jax.sharding import PartitionSpec as P

HD = 64
G = 24
MAXS = 48
EPS = 1e-06
BF = jnp.bfloat16
F32 = jnp.float32
DOWN_ROWS = (((0,), (0,)), ((), ()))
ACROSS = (((1,), (1,)), ((), ()))
VMEM = 48 * 2**20
EDGE = 8
LIGHT = pl.CostEstimate(flops=1, bytes_accessed=1, transcendentals=0)


def core_swap(v):
    return lax.ppermute(v, "strip", [(0, 1), (1, 0)])


def dp_swap(v, bit):
    return lax.ppermute(v, "dp", [(i, i ^ bit) for i in range(lax.axis_size("dp"))])


def shift(v, axis, step):
    count = lax.axis_size(axis)
    pairs = [(i, i + step) for i in range(count) if 0 <= i + step < count]
    return lax.ppermute(v, axis, pairs)


def all_sum(v, axes):
    for axis in axes:
        count, bit = lax.axis_size(axis), 1
        while bit < count:
            v = v + lax.ppermute(v, axis, [(i, i ^ bit) for i in range(count)])
            bit *= 2
    return v


def gather_bits(v, axis="tensor"):
    count, at, bit = lax.axis_size(axis), lax.axis_index(axis), 1
    while bit < count:
        other = lax.ppermute(v, axis, [(i, i ^ bit) for i in range(count)])
        upper = (at // bit) % 2 == 1
        v = jnp.concatenate([jnp.where(upper, other, v), jnp.where(upper, v, other)], axis=1)
        bit *= 2
    return v


def quarters():
    return 4 if lax.axis_size("dp") == 4 else 1


def reduce_dp(near_a, near_b, keep_a, keep_b):
    near_a, near_b = dp_swap(near_a, 1), dp_swap(near_b, 2)

    def first(*waits):
        a, b = later(near_a, *waits), later(near_b, *waits)
        sent = add(keep_a[1], a[1]).astype(BF), add(keep_b[1], b[1]).astype(BF)
        last_a, last_b = dp_swap(sent[0], 2), dp_swap(sent[1], 1)

        def second(*waits):
            got_a, got_b = later(last_a, *waits), later(last_b, *waits)
            return add(keep_a[0], a[0], got_a).astype(BF), add(keep_b[0], b[0], got_b).astype(BF)

        return sent, second

    return first


def in_order(mine, other, at):
    first = at == 0
    return jnp.stack([jnp.where(first, mine, other), jnp.where(first, other, mine)], axis=0)


def dp_order(pieces):
    at = lax.axis_index("dp")
    bit_x, bit_y = at % 2 == 1, at // 2 == 1
    row_own = [jnp.where(bit_x, pieces[1], pieces[0]), jnp.where(bit_x, pieces[0], pieces[1])]
    row_far = [jnp.where(bit_x, pieces[3], pieces[2]), jnp.where(bit_x, pieces[2], pieces[3])]
    return jnp.stack(
        [jnp.where(bit_y, f, o) for o, f in zip(row_own, row_far)]
        + [jnp.where(bit_y, o, f) for o, f in zip(row_own, row_far)],
        axis=0,
    )


def later(v, *others):
    return lax.optimization_barrier((v, *others))[0]


def add(*terms):
    return functools.reduce(lambda a, b: a + b, [t.astype(F32) for t in terms])


def at_index(v, i, axis=0):
    return lax.dynamic_index_in_dim(v, i, axis, keepdims=False)


def hidden_share(block, strip_at, part, q):
    width = block.shape[1] // (2 * q)
    return lax.dynamic_slice_in_dim(block, (strip_at * q + part) * width, width, 1)


def gather_conv_weight(block):
    q = quarters()
    strip_at = lax.axis_index("strip")
    parts = [0] if q == 1 else [lax.axis_index("dp"), lax.axis_index("dp") ^ 3]
    mine = [hidden_share(block, strip_at, part, q) for part in parts]
    width = mine[0].shape[1]
    others = core_swap(jnp.concatenate([hidden_share(block, 1 - strip_at, part, q) for part in parts], axis=1))
    both = [in_order(own, others[:, i * width : (i + 1) * width], strip_at) for i, own in enumerate(mine)]

    def along_z(i, *waits):
        whole = lax.all_gather(both[i], "tensor", axis=0)
        whole = later(whole, *waits) if waits else whole
        return jnp.swapaxes(whole, 0, 1).reshape(-1, width)

    return along_z


def dp_neighbours(own):
    return [] if quarters() == 1 else [dp_swap(own, 1), dp_swap(own, 2)]


def conv_terms(left, rights, in_turn):
    if len(rights) == 1:
        return [lax.dot_general(left, rights[0], DOWN_ROWS, preferred_element_type=F32).astype(BF)]
    own, beside_x, beside_y, far = rights
    near = tall(in_turn(left), [beside_x, beside_y, far], [(0, 2), (1, 2)], "tall_near")
    keep = tall(later(left, near[0]), [own, beside_x, beside_y], [(0, 2), (0, 1)], "tall_keep")
    return [*near, *keep]


def conv_halves(halves):
    zs = lax.axis_size("tensor")
    rows = halves[0].shape[0] // zs
    view = jnp.concatenate([h[z * rows : (z + 1) * rows] for z in range(zs) for h in halves], axis=0)
    return lax.psum_scatter(view, "tensor", scatter_dimension=0, tiled=True).reshape(2, rows, -1)


def conv_rows(part, waits=()):
    strip_at = lax.axis_index("strip")
    mine = at_index(part, strip_at)
    other = core_swap(at_index(part, 1 - strip_at))
    both = in_order(mine, other, strip_at)
    if quarters() == 1:
        return jnp.concatenate(list(lax.psum(both, "dp")), axis=1).astype(F32)
    near = [dp_swap(both, k) for k in (1, 2, 3)]
    every = dp_order([both] + [later(n, *waits) if waits else n for n in near])
    return jnp.concatenate([every[d, c] for c in range(2) for d in range(4)], axis=1).astype(F32)


def gather_mlp_weights(up, down):
    q = quarters()
    strip_at, dp_at = lax.axis_index("strip"), lax.axis_index("dp") if q > 1 else 0
    mine = jnp.concatenate([hidden_share(w, strip_at, dp_at, q) for w in (up, down)], axis=0)
    whole = lax.all_gather(mine, "tensor", axis=0)
    return jnp.concatenate(list(whole), axis=1).reshape(2, up.shape[0], -1)


def mlp_far(near):
    return [dp_swap(near[0][0], 2), dp_swap(near[1][1], 1)] if near else []


def mlp_scatter(own, dps):
    width, all_cols = own[0].shape
    zs = lax.axis_size("tensor")
    cols = all_cols // zs
    view = jnp.concatenate([v[:, z * cols : (z + 1) * cols] for z in range(zs) for v in own], axis=0)
    part = lax.psum_scatter(view, "tensor", scatter_dimension=0, tiled=True)
    return part.reshape(2, dps * 2, -1, cols)


def mlp_rows(part, dps):
    rows, cols = part.shape[2:]
    if quarters() > 1:
        parts = lax.all_to_all(part, ("dp", "strip"), 0, 0).reshape(dps, 2, 2, rows, cols)
        return [
            jnp.concatenate([parts[d, c, i] for c in range(2) for d in range(dps)], axis=1).astype(F32) for i in range(2)
        ]
    strip_at = lax.axis_index("strip")
    part = lax.psum_scatter(part.reshape(dps, 2, 2, rows, cols), "dp", scatter_dimension=0)
    mine = at_index(part, strip_at)
    other = core_swap(at_index(part, 1 - strip_at))
    both = in_order(mine, other, strip_at)
    return [jnp.concatenate([both[0, i], both[1, i]], axis=1).astype(F32) for i in range(2)]


def rows_layout(whole):
    zs, dps = lax.axis_size("tensor"), lax.axis_size("dp")
    cut = min(w.shape[1] for w in whole) // zs
    return [w.reshape(dps, 2, -1, w.shape[1]) for w in whole], cut


def rows_scatter(whole):
    zs, dps, strip_at = lax.axis_size("tensor"), lax.axis_size("dp"), lax.axis_index("strip")
    view, cut = rows_layout(whole)

    def of_core(core):
        parts = [at_index(v, core, 1) for v in view]
        groups = []
        for z in range(zs):
            group = []
            for v in parts:
                share = v.shape[2] // zs
                group += [v[:, :, z * share + c : z * share + c + cut] for c in range(0, share, cut)]
            groups.append(jnp.concatenate(group, axis=1))
        return jnp.concatenate(groups, axis=0)

    sums = add(of_core(strip_at), core_swap(of_core(1 - strip_at))).astype(BF)
    part = lax.psum_scatter(sums.reshape(-1, cut), "tensor", scatter_dimension=0, tiled=True)
    return sums, part.reshape(dps, -1, cut)


def rows_sum(whole, part):
    zs, dp_at = lax.axis_size("tensor"), lax.axis_index("dp")
    view, cut = rows_layout(whole)
    if quarters() == 1:
        total = lax.psum_scatter(part, "dp", scatter_dimension=0).astype(F32)
    else:
        total = add(at_index(part, dp_at), *[dp_swap(at_index(part, dp_at ^ k), k) for k in (1, 2, 3)])
    outs, at = [], 0
    for v in view:
        rows = v.shape[2]
        count = v.shape[3] // zs // cut
        outs.append(jnp.concatenate([total[at + i * rows : at + (i + 1) * rows] for i in range(count)], axis=1))
        at += count * rows
    return outs


def scatter_small(v, order):
    for axis in order:
        count, bit, at = lax.axis_size(axis), lax.axis_size(axis) // 2, lax.axis_index(axis)
        while bit >= 1:
            half = v.shape[1] // 2
            upper = (at // bit) % 2
            mine = lax.dynamic_slice_in_dim(v, upper * half, half, 1)
            other = lax.dynamic_slice_in_dim(v, (1 - upper) * half, half, 1)
            v = mine + lax.ppermute(other, axis, [(i, i ^ bit) for i in range(count)])
            bit //= 2
    return all_sum(v, [a for a in ("strip", "tensor", "dp") if a not in order])


def gather_rows(block):
    width, cols = block.shape[-2:]
    dps, zs = lax.axis_size("dp"), lax.axis_size("tensor")
    rows = width // (2 * dps)
    at = lax.axis_index("dp") * 2 + lax.axis_index("strip")
    mine = lax.dynamic_slice_in_dim(block.reshape(-1, width, cols), at * rows, rows, 1)
    whole = lax.all_gather(mine, ("tensor", "dp", "strip"), axis=0).reshape(zs, 2 * dps, -1, rows, cols)
    return jnp.concatenate([whole[:, :, a].reshape(zs, width, cols) for a in range(whole.shape[2])], axis=2)


def params(limit=VMEM):
    return pltpu.CompilerParams(vmem_limit_bytes=limit)


def conv7_kernel(rows, cols, x_ref, k_ref, out_ref, wide):
    wide[...] = x_ref[0].astype(F32)

    def tap_row(i, sums):
        sums = list(sums)
        taps = k_ref[i]
        for m in range(cols + 6):
            x = wide[m, pl.ds(i + EDGE - 3, rows), :]
            for j in range(7):
                c = m - j
                if 0 <= c < cols:
                    sums[c] = sums[c] + x * taps[j : j + 1]
        return tuple(sums)

    sums = lax.fori_loop(0, 7, tap_row, tuple(jnp.zeros((rows, 128), F32) for _ in range(cols)))
    for c in range(cols):
        out_ref[0, c] = sums[c]


def conv7(padded, taps, rows, cols):
    items, _, _, channels = padded.shape
    return pl.pallas_call(
        functools.partial(conv7_kernel, rows, cols),
        grid=(items, channels // 128),
        in_specs=[
            pl.BlockSpec((1, cols + 6, rows + 2 * EDGE, 128), lambda b, c: (b, 0, 0, c)),
            pl.BlockSpec((7, 8, 128), lambda b, c: (0, 0, c)),
        ],
        out_specs=pl.BlockSpec((1, cols, rows, 128), lambda b, c: (b, 0, 0, c)),
        out_shape=jax.ShapeDtypeStruct((items, cols, rows, channels), F32),
        scratch_shapes=[pltpu.VMEM((cols + 6, rows + 2 * EDGE, 128), F32)],
        compiler_params=params(8 * 2**20),
        cost_estimate=LIGHT,
        name="depthwise",
    )(padded, taps)


def tap_grad_kernel(rows, cols, x_ref, g_ref, out_ref, wide, full):
    wide[...] = x_ref[0].astype(F32)
    full[...] = g_ref[0].astype(F32)

    @pl.when(pl.program_id(1) == 0)
    def _():
        out_ref[...] = jnp.zeros_like(out_ref)

    def tap_row(i, _):
        sums = [jnp.zeros((8, 128), F32) for _ in range(7)]
        grads = [full[c] for c in range(cols)]
        for m in range(cols + 6):
            x = wide[m, pl.ds(i + EDGE - 3, rows), :]
            for j in range(7):
                c = m - j
                if 0 <= c < cols:
                    sums[j] = sums[j] + (x * grads[c]).reshape(rows // 8, 8, 128).sum(axis=0)
        lines = [jnp.sum(s, axis=0, keepdims=True) for s in sums]
        out_ref[i] += jnp.concatenate(lines + [jnp.zeros((1, 128), F32)], axis=0)
        return 0

    lax.fori_loop(0, 7, tap_row, 0)


def tap_grad(padded, grad, rows, cols):
    items, _, _, channels = padded.shape
    return pl.pallas_call(
        functools.partial(tap_grad_kernel, rows, cols),
        grid=(channels // 128, items),
        in_specs=[
            pl.BlockSpec((1, cols + 6, rows + 2 * EDGE, 128), lambda c, b: (b, 0, 0, c)),
            pl.BlockSpec((1, cols, rows, 128), lambda c, b: (b, 0, 0, c)),
        ],
        out_specs=pl.BlockSpec((7, 8, 128), lambda c, b: (0, 0, c)),
        out_shape=jax.ShapeDtypeStruct((7, 8, channels), F32),
        scratch_shapes=[pltpu.VMEM((cols + 6, rows + 2 * EDGE, 128), F32), pltpu.VMEM((cols, rows, 128), F32)],
        compiler_params=params(8 * 2**20),
        cost_estimate=LIGHT,
        name="tap_grad",
    )(padded, grad)


def norm_kernel(v_ref, gain_ref, bias_ref, out_ref):
    unit, _ = normalise(v_ref[...])
    out_ref[...] = (unit * gain_ref[...] + bias_ref[...]).astype(BF)


def norm_rows(v, gain, bias):
    rows, width = v.shape
    block = row_block(rows, 144)
    tile, line = pl.BlockSpec((block, width), lambda i: (i, 0)), pl.BlockSpec((1, width), lambda i: (0, 0))
    return pl.pallas_call(
        norm_kernel,
        grid=(rows // block,),
        in_specs=[tile, line, line],
        out_specs=tile,
        out_shape=jax.ShapeDtypeStruct((rows, width), BF),
        compiler_params=params(16 * 2**20),
        cost_estimate=LIGHT,
        name="norm",
    )(v, gain.reshape(1, width), bias.reshape(1, width))


def norm_back_kernel(here_ref, there_ref, v_ref, gain_ref, out_ref, sums_ref):
    @pl.when(pl.program_id(0) == 0)
    def _():
        sums_ref[...] = jnp.zeros_like(sums_ref)

    grad = here_ref[...] + there_ref[...].astype(F32)
    unit, scale = normalise(v_ref[...])
    sums_ref[...] += lines(jnp.sum(grad * unit, axis=0, keepdims=True), jnp.sum(grad, axis=0, keepdims=True))
    out_ref[...] = normalise_back(grad, unit, scale, gain_ref[...]).astype(BF)


def norm_rows_back(here, there, v, gain):
    rows, width = v.shape
    block = row_block(rows, 144)
    tile, line = pl.BlockSpec((block, width), lambda i: (i, 0)), pl.BlockSpec((1, width), lambda i: (0, 0))
    return pl.pallas_call(
        norm_back_kernel,
        grid=(rows // block,),
        in_specs=[tile, tile, tile, line],
        out_specs=[tile, pl.BlockSpec((8, width), lambda i: (0, 0))],
        out_shape=[jax.ShapeDtypeStruct((rows, width), BF), jax.ShapeDtypeStruct((8, width), F32)],
        compiler_params=params(20 * 2**20),
        cost_estimate=LIGHT,
        name="norm_back",
    )(here, there, v, gain.reshape(1, width))


def gelu_pair(h):
    cdf = 0.5 * (1.0 + lax.erf(h * (0.5**0.5)))
    pdf = jnp.exp(h * h * -0.5) * 0.3989422804014327
    return h * cdf, cdf + h * pdf


def expand_kernel(step, x_ref, w_ref, act_ref, slope_ref):
    x = x_ref[...]
    for at in range(0, w_ref.shape[1], step):
        h = jnp.dot(x, w_ref[:, at : at + step], preferred_element_type=F32)
        act, slope = gelu_pair(h)
        act_ref[:, at : at + step] = act.astype(BF)
        slope_ref[:, at : at + step] = slope.astype(BF)


def row_block(rows, most):
    best = 16
    for block in range(16, most + 1, 16):
        if rows % block == 0:
            best = block
    return best


def expand(x, w):
    m, k = x.shape
    n = w.shape[1]
    bm = row_block(m, 432)
    bn = min(n, 768)
    spec = pl.BlockSpec((bm, bn), lambda j, i: (i, j))
    return pl.pallas_call(
        functools.partial(expand_kernel, 256),
        grid=(n // bn, m // bm),
        in_specs=[pl.BlockSpec((bm, k), lambda j, i: (i, 0)), pl.BlockSpec((k, bn), lambda j, i: (0, j))],
        out_specs=[spec, spec],
        out_shape=[jax.ShapeDtypeStruct((m, n), BF)] * 2,
        compiler_params=params(20 * 2**20),
        cost_estimate=LIGHT,
        name="expand_gelu",
    )(x, w)


def back_sum_kernel(count, *refs):
    out_ref = refs[-1]
    total = None
    for a_ref, w_ref in zip(refs[:count], refs[count : 2 * count]):
        term = lax.dot_general(a_ref[...], w_ref[...], ACROSS, preferred_element_type=F32)
        total = term if total is None else total + term
    out_ref[...] = total.astype(out_ref.dtype)


def back_sum(parts, weights, first, rows, dtype):
    n = weights[0].shape[0]
    ks = [w.shape[1] for w in weights]
    bm = row_block(rows, 432)
    bn = 512
    skip = first // bm
    return pl.pallas_call(
        functools.partial(back_sum_kernel, len(parts)),
        grid=(n // bn, rows // bm),
        in_specs=[pl.BlockSpec((bm, k), lambda j, i: (i + skip, 0)) for k in ks]
        + [pl.BlockSpec((bn, k), lambda j, i: (j, 0)) for k in ks],
        out_specs=pl.BlockSpec((bm, bn), lambda j, i: (i, j)),
        out_shape=jax.ShapeDtypeStruct((rows, n), dtype),
        compiler_params=params(24 * 2**20),
        cost_estimate=LIGHT,
        name="reduce_sum",
    )(*parts, *weights)


def tall(a, rights, uses, name):
    m, n = a.shape
    cols = rights[0].shape[1]
    bm = 256
    steps = n // 2 // bm

    def kernel(a_ref, *refs):
        outs = refs[-2:]
        for half in range(2):

            @pl.when(pl.program_id(0) // steps == half)
            def _():
                left = a_ref[...]
                for i, use in enumerate(uses[half]):
                    outs[half][i] = lax.dot_general(left, refs[use][...], DOWN_ROWS, preferred_element_type=F32).astype(BF)

    def out_spec(half):
        place = lambda i: (0, jnp.clip(i - half * steps, 0, steps - 1), 0)
        return pl.BlockSpec((len(uses[half]), bm, cols), place)

    return pl.pallas_call(
        kernel,
        grid=(2 * steps,),
        in_specs=[pl.BlockSpec((m, bm), lambda i: (0, i))] + [pl.BlockSpec((m, cols), lambda i: (0, 0)) for _ in rights],
        out_specs=[out_spec(0), out_spec(1)],
        out_shape=[jax.ShapeDtypeStruct((len(u), n // 2, cols), BF) for u in uses],
        compiler_params=params(28 * 2**20),
        cost_estimate=LIGHT,
        name=name,
    )(a, *rights)


def back_slope(a, w, slope):
    m, k = a.shape
    n = w.shape[1]
    bm, bn = row_block(m, 432), min(n, 768)

    def kernel(a_ref, w_ref, s_ref, out_ref):
        left = a_ref[...]
        for at in range(0, bn, 256):
            cut = slice(at, at + 256)
            grad = jnp.dot(left, w_ref[:, cut], preferred_element_type=F32)
            out_ref[:, cut] = (grad * s_ref[:, cut].astype(F32)).astype(BF)

    spec = pl.BlockSpec((bm, bn), lambda j, i: (i, j))
    return pl.pallas_call(
        kernel,
        grid=(n // bn, m // bm),
        in_specs=[pl.BlockSpec((bm, k), lambda j, i: (i, 0)), pl.BlockSpec((k, bn), lambda j, i: (0, j)), spec],
        out_specs=spec,
        out_shape=jax.ShapeDtypeStruct((m, n), BF),
        compiler_params=params(20 * 2**20),
        cost_estimate=LIGHT,
        name="back_slope",
    )(a, w, slope)


def whole_call(kernel, outs, args, flops, name):
    vmem = pl.BlockSpec(memory_space=pltpu.VMEM)
    bytes_accessed = sum(a.size * a.dtype.itemsize for a in args) + sum(o.size * o.dtype.itemsize for o in outs)
    return pl.pallas_call(
        kernel,
        in_specs=[vmem] * len(args),
        out_specs=[vmem] * len(outs),
        out_shape=outs,
        compiler_params=params(36 * 2**20),
        cost_estimate=LIGHT,
        name=name,
    )(*args)


def shape(dtype, *dims):
    return jax.ShapeDtypeStruct(dims, dtype)


def qkv_kernel(zs, group, joined_ref, gain_ref, bias_ref, w_ref, normed_ref, out_ref):
    unit, _ = normalise(joined_ref[...])
    normed = (unit * gain_ref[...] + bias_ref[...]).astype(BF)
    normed_ref[...] = normed
    for z in range(zs):
        part = jnp.dot(normed, w_ref[z], preferred_element_type=F32).astype(BF)
        for a in range(3):
            for core in range(2):
                at = (2 * a + core) * group
                out_ref[core * zs + z, :, a * group : (a + 1) * group] = part[:, at : at + group]


def tokens_of(ref):
    v = ref[:, 0].astype(F32)
    return v.reshape(v.shape[0] * v.shape[1], v.shape[2]).astype(BF)


def head_lanes(heads, lanes):
    lane = lax.broadcasted_iota(jnp.int32, (1, lanes), 1)
    return [jnp.logical_and(lane >= h * HD, lane < (h + 1) * HD) for h in range(heads)]


def only(lanes, v):
    return jnp.where(lanes, v, jnp.zeros((), v.dtype))


def head_probs(q, k):
    scores = lax.dot_general(q, k, ACROSS, preferred_element_type=F32) * HD**-0.5
    powers = jnp.exp(scores - jnp.max(scores, axis=-1, keepdims=True))
    return powers * (1.0 / jnp.sum(powers, axis=-1, keepdims=True))


def attention_kernel(group, qkv_ref, out_ref):
    qkv = tokens_of(qkv_ref)
    q, k, v = (qkv[:, a * group : (a + 1) * group] for a in range(3))
    mixed = jnp.zeros(v.shape, F32)
    for lanes in head_lanes(group // HD, group):
        probs = head_probs(only(lanes, q), k).astype(BF)
        mixed = jnp.where(lanes, jnp.dot(probs, v, preferred_element_type=F32), mixed)
    out_ref[:, 0] = mixed.reshape(out_ref.shape[0], out_ref.shape[2], group).astype(BF)


def attention_back_kernel(group, qkv_ref, grad_ref, out_ref):
    qkv = tokens_of(qkv_ref)
    grad = tokens_of(grad_ref)
    q, k, v = (qkv[:, a * group : (a + 1) * group] for a in range(3))
    sums = [jnp.zeros(v.shape, F32) for _ in range(3)]
    for lanes in head_lanes(group // HD, group):
        probs = head_probs(only(lanes, q), k)
        grad_h = only(lanes, grad)
        grad_probs = lax.dot_general(grad_h, v, ACROSS, preferred_element_type=F32)
        along = jnp.sum(probs * grad_probs, axis=-1, keepdims=True)
        grad_scores = (probs * (grad_probs - along)).astype(BF)
        terms = (
            jnp.dot(grad_scores, k, preferred_element_type=F32) * HD**-0.5,
            lax.dot_general(grad_scores, q, DOWN_ROWS, preferred_element_type=F32) * HD**-0.5,
            lax.dot_general(probs.astype(BF), grad, DOWN_ROWS, preferred_element_type=F32),
        )
        sums = [jnp.where(lanes, term, total) for term, total in zip(terms, sums)]
    for a, total in enumerate(sums):
        part = total.reshape(out_ref.shape[0], out_ref.shape[2], group).astype(BF)
        out_ref[:, 0, :, a * group : (a + 1) * group] = part


def by_item(kernel, arrays, lanes, flops, name):
    sources, items, tokens, _ = arrays[0].shape
    block = lambda n: pl.BlockSpec((sources, 1, tokens, n), lambda b: (0, b, 0, 0))
    return pl.pallas_call(
        kernel,
        grid=(items,),
        in_specs=[block(v.shape[3]) for v in arrays],
        out_specs=block(lanes),
        out_shape=shape(BF, sources, items, tokens, lanes),
        compiler_params=params(28 * 2**20),
        cost_estimate=LIGHT,
        name=name,
    )(*arrays)


def project_kernel(zs, group, heads_ref, w_ref, joined_ref, gain_ref, bias_ref, mixed_ref, after_ref, normed_ref):
    total = joined_ref[...]
    for z in range(zs):
        mixed = jnp.concatenate([heads_ref[z], heads_ref[zs + z]], axis=1)
        mixed_ref[:, z * 2 * group : (z + 1) * 2 * group] = mixed
        total = total + lax.dot_general(mixed, w_ref[z], ACROSS, preferred_element_type=F32)
    after_ref[...] = total
    unit, _ = normalise(total)
    normed_ref[...] = (unit * gain_ref[...] + bias_ref[...]).astype(BF)


def mlp_kernel(count, x_ref, g_ref, *refs):
    given = 1 if count == 1 else count + 1
    weights = [(r.at[0], r.at[1]) for r in refs[: count - 1 or 1]]
    if count > 1:
        weights.append((refs[count - 1], refs[count]))
    out_ref, back_ref = refs[given : given + 2]
    acts, grads = refs[given + 2 : given + 2 + count], refs[given + 2 + count :]
    x, g = x_ref[...], g_ref[...]
    for p, (up, down) in enumerate(weights):
        act, slope = gelu_pair(jnp.dot(x, up[...], preferred_element_type=F32))
        act = act.astype(BF)
        acts[p][...] = act
        grad = (jnp.dot(g, down[...], preferred_element_type=F32) * slope).astype(BF)
        grads[p][...] = grad
        out = lax.dot_general(act, down[...], ACROSS, preferred_element_type=F32)
        back = lax.dot_general(grad, up[...], ACROSS, preferred_element_type=F32)
        if p == 0:
            out_ref[...] = out
            back_ref[...] = back
        else:
            out_ref[...] += out
            back_ref[...] += back


def lines(*rows):
    width = rows[0].shape[1]
    return jnp.concatenate(list(rows) + [jnp.zeros((8 - len(rows), width), F32)], axis=0)


def norm_back_two_kernel(zs, group, here_ref, there_ref, after_ref, d_ref, gain_ref, w_ref, grad_ref, low_ref, sums_ref, out_ref):
    grad_two = here_ref[...] + there_ref[...].astype(F32)
    unit, scale = normalise(after_ref[...])
    sums_ref[...] = lines(jnp.sum(grad_two * unit, axis=0, keepdims=True), jnp.sum(grad_two, axis=0, keepdims=True))
    grad = d_ref[...] + normalise_back(grad_two, unit, scale, gain_ref[...])
    grad_ref[...] = grad
    low = grad.astype(BF)
    low_ref[...] = low
    for z in range(zs):
        part = jnp.dot(low, w_ref[z], preferred_element_type=F32).astype(BF)
        for core in range(2):
            out_ref[core * zs + z] = part[:, core * group : (core + 1) * group]


def norm_back_one_kernel(zs, group, g_ref, w_ref, joined_ref, after_ref, gain_ref, all_ref, grad_ref, sums_ref):
    grad_one = jnp.zeros(joined_ref.shape, F32)
    for z in range(zs):
        part = jnp.concatenate(
            [g_ref[core * zs + z, :, a * group : (a + 1) * group] for a in range(3) for core in range(2)], axis=1
        )
        all_ref[:, z * 6 * group : (z + 1) * 6 * group] = part
        grad_one = grad_one + lax.dot_general(part, w_ref[z], ACROSS, preferred_element_type=F32)
    unit, scale = normalise(joined_ref[...])
    sums_ref[...] = lines(jnp.sum(grad_one * unit, axis=0, keepdims=True), jnp.sum(grad_one, axis=0, keepdims=True))
    grad_ref[...] = after_ref[...] + normalise_back(grad_one, unit, scale, gain_ref[...])


def normalise(v):
    center = jnp.mean(v, axis=-1, keepdims=True)
    shifted = v - center
    scale = lax.rsqrt(jnp.mean(shifted * shifted, axis=-1, keepdims=True) + EPS)
    return shifted * scale, scale


def normalise_back(g, unit, scale, gain):
    gg = g * gain
    along = jnp.mean(gg * unit, axis=-1, keepdims=True)
    return scale * (gg - jnp.mean(gg, axis=-1, keepdims=True) - unit * along)


def pool_matrix(pooled_index, buffer_index, map_side, offset):
    map_place = buffer_index[None, :] - offset
    bin_start = pooled_index[:, None] * map_side // G
    bin_stop = ((pooled_index[:, None] + 1) * map_side + G - 1) // G
    inside = jnp.logical_and(map_place >= bin_start, map_place < bin_stop)
    real = jnp.logical_and(pooled_index >= 0, pooled_index < G)[:, None]
    return jnp.where(jnp.logical_and(inside, real), 1.0, 0.0).astype(F32) / (bin_stop - bin_start).astype(F32)


def depthwise3(padded, kernel, rows, cols):
    total = None
    for i in range(3):
        for j in range(3):
            term = padded[:, i : i + rows, j : j + cols, :] * kernel[:, 3 * i + j]
            total = term if total is None else total + term
    return total


def rim(v):
    v = jnp.concatenate([shift(v[:, -1:], "strip", 1), v, shift(v[:, :1], "strip", -1)], axis=1)
    return jnp.concatenate([shift(v[:, :, -1:], "tensor", 1), v, shift(v[:, :, :1], "tensor", -1)], axis=2)


def wide_rim(v):
    v = jnp.concatenate([shift(v[:, -3:], "tensor", 1), v, shift(v[:, :3], "tensor", -1)], axis=1)
    return jnp.concatenate([shift(v[:, :, -EDGE:], "strip", 1), v, shift(v[:, :, :EDGE], "strip", -1)], axis=2)


def shards(
    res_code, vit_in, map_in, dw_kernel, conv_gain, conv_bias, w_expand, w_reduce, layer_scale, adapt_w, mix_kernel,
    gate_logit, gain_one, bias_one, w_qkv, w_proj, gain_two, bias_two, w_up, w_down, d_vit, d_map,
):
    strip_at, tensor_at, dp_at = (lax.axis_index(a) for a in ("strip", "tensor", "dp"))
    dps, zs = lax.axis_size("dp"), lax.axis_size("tensor")
    items, grid_rows, _, width = vit_in.shape
    _, map_rows, map_cols, channels = map_in.shape
    grid_cols = G // zs
    cells = items * map_rows * map_cols
    tokens = items * grid_rows * grid_cols
    head_cols = w_qkv.shape[2]
    score_scale = HD**-0.5

    expand_z, reduce_z = gather_conv_weight(w_expand), gather_conv_weight(w_reduce)
    expand_own, reduce_own = expand_z(0), reduce_z(0)
    expand_near = dp_neighbours(expand_own)
    qkv_whole = gather_rows(jnp.swapaxes(w_qkv, 0, 1))
    mlp_own = gather_mlp_weights(w_up, w_down)
    proj_whole = gather_rows(w_proj)
    count = quarters()

    side = res_code // 32
    offset = (MAXS - side) // 2
    row_cells = strip_at * map_rows + jnp.arange(map_rows, dtype=jnp.int32)
    col_cells = tensor_at * map_cols + jnp.arange(map_cols, dtype=jnp.int32)

    def inside(at):
        low, high = offset[:, None], (offset + side)[:, None]
        return jnp.logical_and(at[None] >= low, at[None] < high).astype(F32)

    row_ok, col_ok = inside(row_cells), inside(col_cells)
    cell_mask = col_ok[:, :, None, None] * row_ok[:, None, :, None]
    many_pools = jax.vmap(pool_matrix, in_axes=(None, None, 0, 0))
    pooled_rows = strip_at * grid_rows + jnp.arange(grid_rows, dtype=jnp.int32)
    pooled_cols = (tensor_at - 1) * grid_cols + jnp.arange(3 * grid_cols, dtype=jnp.int32)
    row_pool = many_pools(pooled_rows, row_cells, side, offset)
    col_pool = many_pools(pooled_cols, col_cells, side, offset).reshape(items, 3, grid_cols, map_cols)
    pool = jnp.einsum("bir,bgjc->bgijcr", row_pool, col_pool)
    pool = pool.reshape(items, 3 * grid_rows * grid_cols, map_cols * map_rows).astype(BF)

    masked = jnp.swapaxes(map_in, 1, 2) * cell_mask.astype(BF)
    padded = later(wide_rim(masked), expand_own)
    taps = jnp.pad(dw_kernel.T.reshape(7, 7, channels), ((0, 0), (0, 1), (0, 0)))
    spread = conv7(padded, taps, map_rows, map_cols).reshape(cells, channels)
    reduce_near = dp_neighbours(later(reduce_own, spread))
    normed = norm_rows(spread, conv_gain, conv_bias)
    normed_both = jnp.concatenate([normed, core_swap(normed)], axis=0)
    expand_pieces, reduce_pieces, pairs = [expand_own, *expand_near], [reduce_own, *reduce_near], []
    x = later(normed_both, *expand_near)
    for k in range(count):
        if k == 3:
            expand_pieces.append(expand_z(1, pairs[2][0]))
        pairs.append(expand(x, expand_pieces[k]))
        x = later(normed_both, pairs[k][0])
    acts, slopes = zip(*pairs)
    if count > 1:
        reduce_pieces.append(reduce_z(1, acts[3]))
    branch_there = core_swap(back_sum(acts, reduce_pieces, cells, cells, BF))
    branch_here = back_sum(acts, reduce_pieces, 0, cells, F32)
    branch = (branch_here + branch_there.astype(F32)).reshape(masked.shape)
    map_value = cell_mask * (masked.astype(F32) + layer_scale * branch)
    map_low = map_value.astype(BF)
    map_out = jnp.swapaxes(map_low, 1, 2)

    pooled3 = lax.dot_general(
        pool, map_low.reshape(items, -1, channels), (((2,), (1,)), ((0,), (0,))), preferred_element_type=F32
    ).reshape(items, 3, -1, channels)
    pooled = (
        pooled3[:, 1]
        + shift(pooled3[:, 0].astype(BF), "tensor", -1).astype(F32)
        + shift(pooled3[:, 2].astype(BF), "tensor", 1).astype(F32)
    )
    pooled_low = pooled.astype(BF).reshape(tokens, channels)
    grid_shape = (items, grid_rows, grid_cols, width)
    adapted = jnp.dot(pooled_low, adapt_w, preferred_element_type=F32).reshape(grid_shape)
    adapted_pad = rim(adapted)
    local_mix = depthwise3(adapted_pad, mix_kernel, grid_rows, grid_cols)
    gate = jnp.tanh(gate_logit)
    mine = lambda v: lax.dynamic_slice_in_dim(v, tensor_at * grid_cols, grid_cols, 2)
    grad_out = mine(d_vit).reshape(tokens, width)
    grad_mlp = grad_out.astype(BF)
    grad_mlp_both = jnp.concatenate([grad_mlp, core_swap(grad_mlp)], axis=0)
    joined = (mine(vit_in) + gate * local_mix).reshape(tokens, width)

    group = head_cols // 2
    line = lambda v: v.reshape(1, width)
    dots = lambda m, n, k: 2 * m * n * k
    spread_heads = lambda v: lax.all_to_all(v, ("strip", "tensor"), 0, 0, tiled=True)
    by_source = lambda v: v.reshape(2 * zs, items, -1, v.shape[-1])
    normed_one, qkv = whole_call(
        functools.partial(qkv_kernel, zs, group),
        [shape(BF, tokens, width), shape(BF, 2 * zs, tokens, 3 * group)],
        [joined, line(gain_one), line(bias_one), qkv_whole],
        dots(tokens, width, 3 * zs * head_cols),
        "qkv",
    )
    mlp_near = dp_neighbours(mlp_own)
    if mlp_near:
        qkv = later(qkv, *mlp_near)
    qkv = by_source(spread_heads(qkv))
    mlp_weights = [mlp_own, *mlp_near, *mlp_far(mlp_near)]
    attention_flops = items * 2 * dots(24 * 24, 24 * 24, group)
    heads = by_item(functools.partial(attention_kernel, group), [qkv], group, 2 * attention_flops, "attention")
    heads = later(heads, *mlp_weights)
    heads = spread_heads(heads).reshape(2 * zs, tokens, group)
    mixed, after_attn, normed_two = whole_call(
        functools.partial(project_kernel, zs, group),
        [shape(BF, tokens, width), shape(F32, tokens, width), shape(BF, tokens, width)],
        [heads, proj_whole, joined, line(gain_two), line(bias_two)],
        dots(tokens, width, width),
        "project",
    )

    two_both = jnp.concatenate([normed_two, core_swap(normed_two)], axis=0)
    some = mlp_own.shape[2]
    mlp, back, *halves = whole_call(
        functools.partial(mlp_kernel, count),
        [shape(F32, 2 * tokens, width)] * 2 + [shape(BF, 2 * tokens, some)] * (2 * count),
        [two_both, grad_mlp_both, *mlp_weights],
        4 * count * dots(2 * tokens, width, some),
        "mlp",
    )
    actives, grad_ups = halves[:count], halves[count:]
    back_there = core_swap(back[tokens:].astype(BF))
    grad_after, grad_att, sums_two, grad_heads = whole_call(
        functools.partial(norm_back_two_kernel, zs, group),
        [shape(F32, tokens, width), shape(BF, tokens, width), shape(F32, 8, width), shape(BF, 2 * zs, tokens, group)],
        [back[:tokens], back_there, after_attn, grad_out, line(gain_two), proj_whole],
        dots(tokens, width, width),
        "norm_back_two",
    )
    grad_heads = by_source(spread_heads(grad_heads))
    mlp_there = core_swap(mlp[tokens:].astype(BF))
    every = lambda v: lax.all_gather(v.astype(BF).reshape(grid_shape), "tensor", axis=0)
    to_grid = lambda v: jnp.concatenate(list(v), axis=2).astype(F32)
    down_terms = lambda left, rights: [
        lax.dot_general(left, r, DOWN_ROWS, preferred_element_type=F32).astype(BF) for r in rights
    ]
    grad_down = down_terms(grad_mlp_both, actives)
    grad_up = down_terms(two_both, grad_ups)

    grad_qkv = by_item(
        functools.partial(attention_back_kernel, group), [qkv, grad_heads], 3 * group, 5 * attention_flops, "attention_back"
    )
    vit_every = every(after_attn + mlp[:tokens] + later(mlp_there, grad_qkv).astype(F32))
    grad_qkv = later(spread_heads(grad_qkv).reshape(2 * zs, tokens, 3 * group), *grad_down, *grad_up)
    grad_qkv, grad_joined, sums_one = whole_call(
        functools.partial(norm_back_one_kernel, zs, group),
        [shape(BF, tokens, 3 * width), shape(F32, tokens, width), shape(F32, 8, width)],
        [grad_qkv, qkv_whole, joined, grad_after, line(gain_one)],
        dots(tokens, width, 3 * width),
        "norm_back_one",
    )
    grad_vit_every = every(grad_joined)

    grad_grid = grad_joined.reshape(grid_shape)
    over = (0, 1, 2)
    grad_gate = jnp.sum(grad_grid * local_mix, axis=over) * (1.0 - gate * gate)
    grad_mix = grad_grid * gate
    grad_adapted = depthwise3(rim(grad_mix), mix_kernel[:, ::-1], grid_rows, grid_cols)
    grad_adapted = grad_adapted.astype(BF).reshape(tokens, width)
    grad_taps = [
        jnp.sum(adapted_pad[:, i : i + grid_rows, j : j + grid_cols] * grad_mix, axis=over)
        for i in range(3)
        for j in range(3)
    ]
    small_vit = jnp.stack(
        grad_taps
        + [
            grad_gate,
            sums_one[0],
            sums_one[1],
            sums_two[0],
            sums_two[1],
        ],
        axis=0,
    )
    row_terms = down_terms(normed_one, [grad_qkv]) + down_terms(grad_att, [mixed]) + down_terms(pooled_low, [grad_adapted])
    grad_pooled = lax.dot_general(grad_adapted, adapt_w, ACROSS, preferred_element_type=F32).astype(BF)
    grad_pooled = grad_pooled.reshape(items, -1, channels)
    grad_pooled = jnp.concatenate(
        [later(shift(grad_pooled, "tensor", 1), *row_terms), grad_pooled, shift(grad_pooled, "tensor", -1)], axis=1
    )
    grad_map = lax.dot_general(pool, grad_pooled, (((1,), (1,)), ((0,), (0,))), preferred_element_type=F32)
    grad_map = jnp.swapaxes(d_map, 1, 2).astype(F32) + grad_map.reshape(masked.shape)

    kept = cell_mask * grad_map
    grad_scale = jnp.sum(kept * branch, axis=over)
    grad_branch = (kept * layer_scale).astype(BF).reshape(cells, channels)
    grad_branch_both = jnp.concatenate([grad_branch, core_swap(grad_branch)], axis=0)
    pair = lambda a, b: jnp.stack([a, b], axis=0)
    own_up, own_down = grad_up[0], grad_down[0]
    four = count > 1
    if four:
        mlp_first = reduce_dp(
            pair(grad_up[1], grad_up[3]), pair(grad_down[2], grad_down[3]), [own_up, grad_up[2]], [own_down, grad_down[1]]
        )
    rows_sums, rows_part = rows_scatter(row_terms)
    reduce_terms = conv_terms(grad_branch_both, acts, lambda v: later(v, rows_sums))
    grad_hidden, last = [], [reduce_terms[-1]]
    if four:
        reduce_first = reduce_dp(*reduce_terms)
    for k in range(count):
        if four and k == 2:
            mlp_sent, mlp_second = mlp_first(last[0])
            last += [*mlp_sent]
        last = [back_slope(later(grad_branch_both, *last), reduce_pieces[k], slopes[k])]
        grad_hidden += last
    reduce_halves = jnp.split(reduce_terms[0], 2, axis=0)
    if four:
        reduce_sent, reduce_second = reduce_first(last[0])
        last += [*reduce_sent]
    expand_terms = conv_terms(normed_both, grad_hidden, lambda v: later(v, *last))
    expand_halves = jnp.split(expand_terms[0], 2, axis=0)
    last = [expand_terms[-1], rows_part]
    if four:
        expand_first = reduce_dp(*expand_terms)
        own_up, own_down = mlp_second(expand_terms[-1])
        last += [own_up, own_down]
    mlp_part = mlp_scatter([own_up, own_down], dps)
    sent = later(grad_hidden[0], *last)
    normed_sent = back_sum([sent] + grad_hidden[1:], expand_pieces, cells, cells, BF)
    last = [normed_sent]
    if four:
        reduce_halves = reduce_second(normed_sent)
        last += [*reduce_halves]
    reduce_part = conv_halves(reduce_halves)
    normed_there = core_swap(normed_sent)
    kept_here = later(grad_hidden[0], *last)
    normed_here = back_sum([kept_here] + grad_hidden[1:], expand_pieces, 0, cells, F32)
    last = [normed_here]
    if four:
        expand_sent, expand_second = expand_first(normed_here)
        last += [*expand_sent]
    grad_spread, sums_conv = norm_rows_back(later(normed_here, *last), normed_there, spread, conv_gain)
    grad_spread = grad_spread.reshape(masked.shape)
    mlp_part = later(mlp_part, grad_spread)
    mlp_turned = jnp.swapaxes(mlp_part, 0, 1)
    grad_taps = tap_grad(padded, later(grad_spread, mlp_turned), map_rows, map_cols)
    if four:
        expand_halves = expand_second(grad_taps)
    expand_part = conv_halves(expand_halves)
    out_qkv, out_proj, out_adapt = rows_sum(row_terms, later(rows_part, grad_taps))
    out_reduce = conv_rows(later(reduce_part, grad_taps))
    grad_map_in = conv7(
        later(wide_rim(grad_spread), *expand_halves, out_reduce, out_qkv), taps[::-1, [6, 5, 4, 3, 2, 1, 0, 7]], map_rows, map_cols
    )
    grad_map_in = jnp.swapaxes(cell_mask * (kept + grad_map_in), 1, 2)
    small_conv = jnp.concatenate(
        [
            grad_taps.reshape(56, channels),
            sums_conv[:2],
            grad_scale[None],
        ],
        axis=0,
    )
    out_up, out_down = mlp_rows(later(mlp_turned, grad_map_in), dps)
    out_adapt = gather_bits(later(out_adapt.astype(BF), grad_map_in)).astype(F32)
    vit_out = to_grid(later(vit_every, normed_here))
    grad_vit = to_grid(later(grad_vit_every, grad_taps))
    out_expand = conv_rows(expand_part)
    small_vit, small_conv = later(small_vit, grad_map_in), later(small_conv, grad_map_in)
    small_vit = scatter_small(small_vit, ("dp", "strip"))
    small_conv = scatter_small(small_conv, ("strip", "tensor"))
    conv_share = channels // (2 * zs)
    out_taps = small_conv[:56].reshape(7, 8, conv_share)[:, :7].reshape(49, conv_share).T
    return (
        vit_out,
        map_out,
        grad_vit,
        grad_map_in,
        out_taps,
        small_conv[56],
        small_conv[57],
        out_expand,
        out_reduce,
        small_conv[58],
        out_adapt,
        small_vit[:9].T,
        small_vit[9],
        small_vit[10],
        small_vit[11],
        out_qkv.reshape(-1, 3, head_cols),
        out_proj,
        small_vit[12],
        small_vit[13],
        out_up,
        out_down,
    )


def solution(mesh):
    rows = P("dp", "strip", None, None)
    maps = P("dp", "strip", "tensor", None)
    conv = ("strip", "tensor")
    vit = ("dp", "strip")
    in_specs = (
        P("dp"), rows, maps, P(), P(), P(), P(conv, None), P(conv, None), P(), P(), P(), P(), P(), P(),
        P(None, None, "tensor"), P(None, "tensor"), P(), P(), P(None, "tensor"), P(None, "tensor"), rows, maps,
    )
    out_specs = (
        rows, maps, rows, maps, P(conv, None), P(conv), P(conv), P(conv, None), P(conv, None), P(conv),
        P(vit, None), P(vit, None), P(vit), P(vit), P(vit), P(vit, None, "tensor"), P(vit, "tensor"), P(vit), P(vit),
        P(vit, "tensor"), P(vit, "tensor"),
    )
    return jax.shard_map(shards, mesh=mesh, in_specs=in_specs, out_specs=out_specs, check_vma=False)
```

time: 1510 us -> 1150 us (0.76)
  matrix products: 211 us -> 32.5 us
  waiting for transfers between devices: 537 us -> 381 us
  Pallas kernels: 187 us -> 266 us
  other arithmetic: 170 us -> 127 us
  local copies, waits for them, and re-layouts: 233 us -> 192 us
  starting transfers between devices: 142 us -> 126 us
    dot_general x66 -> x11, matrix products: 194 us -> 23.6 us  [shards(): lax.dot_general(left, r, DOWN_ROWS, preferred_element_type=F32).astype(BF)]
    pallas_call x0 -> x17, Pallas kernels: none -> 119 us  [the longest x4 43.8 us: tall(): pl.pallas_call(kernel, grid=(2 * steps,), in_specs=[pl.BlockSpec((m, bm),...]
    ppermute x40 -> x29, waiting for transfers between devices: 223 us -> 145 us  [dp_swap(): lax.ppermute(v, 'dp', [(i, i ^ bit) for i in range(lax.axis_size('dp'))])]
    ppermute x12 -> x4, waiting for transfers between devices: 77 us -> 3.59 us  [all_sum(): v = v + lax.ppermute(v, axis, [(i, i ^ bit) for i in range(count)])]
    unnamed x301 -> x492, local copies, waits for them, and re-layouts: 39 us -> 111 us
    reduce_scatter x5 -> x4, waiting for transfers between devices: 54.3 us -> 0.04 us  [the longest x2 0.02 us: conv_halves(): lax.psum_scatter(view, 'tensor', scatter_dimension=0, tiled=True)]
    convert_element_type x10 -> x0, local copies, waits for them, and re-layouts: 38.3 us -> none  [the longest x4 23.1 us: return_conv_grad(): return jnp.transpose(every, (1, 2, 0, 3)).reshape(rows, -1).astype(F32)]
    ppermute x0 -> x8, waiting for transfers between devices: none -> 31 us  [the longest x6 16.7 us: scatter_small(): v = mine + lax.ppermute(other, axis, [(i, i ^ bit) for i in range(count)])]
  transfers between devices with their start and end apart: 104 -> 92, of which waited for: 44 -> 43; matrix products, arithmetic and copies ran while one was open for 37% -> 20% of each run, Pallas kernels for 12% -> 21%
where the time goes in v2:
time: 1150 us; the launch traced here: 1140 us
  waiting for transfers between devices  381 us (33%)
  Pallas kernels  266 us (23%)
  local copies, waits for them, and re-layouts  192 us (17%)
  other arithmetic  127 us (11%)
  starting transfers between devices  126 us (11%)
  matrix products  32.5 us (3%)
  between operations  17.4 us (2%)
    ppermute x29, waiting for transfers between devices, dp_swap(): lax.ppermute(v, 'dp', [(i, i ^ bit) for i in range(lax.axis_size('dp'))])  145 us
    ppermute x20, waiting for transfers between devices, shift(): return lax.ppermute(v, axis, pairs)  118 us
    unnamed x492, local copies, waits for them, and re-layouts  111 us
    ppermute x20, starting transfers between devices, shift(): return lax.ppermute(v, axis, pairs)  53.8 us
    all_to_all x4, waiting for transfers between devices, shards(): lax.all_to_all(v, ('strip', 'tensor'), 0, 0, tiled=True)  52 us
    pallas_call x4, Pallas kernels, back_sum(): pl.pallas_call(functools.partial(back_sum_kernel, len(parts)), grid=(n //...  47.1 us
    pallas_call x2, Pallas kernels, conv7(): pl.pallas_call(functools.partial(conv7_kernel, rows, cols), grid=(items,...  45.9 us
    pallas_call x4, Pallas kernels, tall(): pl.pallas_call(kernel, grid=(2 * steps,), in_specs=[pl.BlockSpec((m, bm),...  43.8 us
  transfers between devices with their start and end apart: 92, of which 43 were waited for; matrix products, arithmetic and copies ran while one was open for 20% of the time, Pallas kernels for 21%

profile of v2, /device:TPU:0, one launch (start us, length us, event | category | flops | bytes accessed | tf_op | source)
XLA Modules:
  0.0 1141.4 jit_solution(17226107973488081992)
XLA Ops:
  37.1 42.2 %collective-permute-done.1 = bf16[3,3,24,1536]{3,2,1,0:T(8,128)(2,1)S(1)} collective-permute-done((bf16[3,3,24,1536]{3,2,1,0:T(8,128)(2,1)S(1)}, bf16[3,3,24,1536]{3,2,1,0:T(8,128)(2,1)S(1)}, u32[]{:S(2)}, u32[]{:S(2)}) %collective-permute-start.1) | collective-permute-done | bytes 663584 | tf_op jit(solution)/shard_map/ppermute | solution.py:34
  106.9 22.9 %depthwise.2 = f32[3,12,24,1536]{3,2,1,0:T(8,128)S(1)} custom-call(bf16[3,18,40,1536]{3,2,1,0:T(8,128)(2,1)S(1)} %copy-done.9, f32[7,8,1536]{2,1,0:T(8,128)S(1)} %copy-done.35), custom_call_target="tpu_custom_call" | custom-call | flops 1 | bytes 1 | tf_op jit(solution)/shard_map/depthwise/pallas_call | solution.py:286
  146.2 42.4 %collective-permute-done.6.w_ref.refs_5_ = bf16[1536,768]{1,0:T(8,128)(2,1)} collective-permute-done((bf16[1536,768]{1,0:T(8,128)(2,1)}, bf16[1536,768]{1,0:T(8,128)(2,1)}, u32[]{:S(2)}, u32[]{:S(2)}) %collective-permute-start.6) | collective-permute-done | bytes 2359328 | tf_op jit(solution)/shard_map/ppermute | solution.py:28
  190.6 7.7 expand_gelu.4
  201.3 7.7 expand_gelu.5
  212.0 7.7 expand_gelu.6
  246.8 12.4 %reduce_sum.126 = bf16[864,1536]{1,0:T(8,128)(2,1)} custom-call(bf16[1728,768]{1,0:T(8,128)(2,1)S(1)} %copy-done.38, bf16[1728,768]{1,0:T(8,128)(2,1)S(1)} %copy-done.15, bf16[1728,768]{1,0:T(8,128)(2,1)S(1)} %copy-done.19, bf16[1728,768]{1,0:T(8,128)(2,1)S(1)} %copy-done.42, bf16[1536,768]{1,0:T(8,128)(2,1)} %bitcast.19.refs_4_.w_ref, ...), custom_call_target="tpu_custom_call" | custom-call | flops 1 | bytes 1 | tf_op jit(solution)/shard_map/reduce_sum/pallas_call | solution.py:448
  276.2 11.9 %reduce_sum.125 = f32[864,1536]{1,0:T(8,128)S(1)} custom-call(bf16[1728,768]{1,0:T(8,128)(2,1)S(1)} %copy-done.39, bf16[1728,768]{1,0:T(8,128)(2,1)S(1)} %copy-done.16, bf16[1728,768]{1,0:T(8,128)(2,1)S(1)} %copy-done.20, bf16[1728,768]{1,0:T(8,128)(2,1)S(1)} %copy-done.43, bf16[1536,768]{1,0:T(8,128)(2,1)} %bitcast.19.refs_4_.w_ref, ...), custom_call_target="tpu_custom_call" | custom-call | flops 1 | bytes 1 | tf_op jit(solution)/shard_map/reduce_sum/pallas_call | solution.py:448
  308.4 13.2 %collective-permute-done.13 = bf16[3,72,1536]{2,1,0:T(8,128)(2,1)} collective-permute-done((bf16[3,72,1536]{2,1,0:T(8,128)(2,1)}, bf16[3,72,1536]{2,1,0:T(8,128)(2,1)}, u32[]{:S(2)}, u32[]{:S(2)}) %collective-permute-start.13) | collective-permute-done | bytes 663584 | tf_op jit(solution)/shard_map/ppermute | solution.py:34
  393.2 28.1 %all-to-all-done = bf16[8,216,384]{2,1,0:T(8,128)(2,1)} async-done(((bf16[8,216,384]{2,1,0:T(8,128)(2,1)}), bf16[8,216,384]{2,1,0:T(8,128)(2,1)}, u32[]{:S(2)}, u32[]{:S(2)}) %all-to-all-start) | async-done | bytes 1327136 | tf_op jit(solution)/shard_map/all_to_all | solution.py:811
  437.3 12.9 %all-gather.33.cloned.1.call-done = bf16[4096,256]{1,0:T(8,128)(2,1)} async-done(((bf16[128,256]{1,0:T(8,128)(2,1)}), bf16[4096,256]{1,0:T(8,128)(2,1)}) %all-gather.33.cloned.1.call-update) | async-done | bytes 2097168 | tf_op jit(solution)/shard_map/all_gather | solution.py:257
  457.1 11.9 %mlp.1 = (f32[432,1024]{1,0:T(8,128)S(1)}, f32[432,1024]{1,0:T(8,128)S(1)}, bf16[432,512]{1,0:T(8,128)(2,1)S(1)}, bf16[432,512]{1,0:T(8,128)(2,1)S(1)}, bf16[432...) custom-call(bf16[432,1024]{1,0:T(8,128)(2,1)S(1)} %constant_dynamic-, ...), custom_call_target="tpu_custom_call" | custom-call | flops 1 | bytes 1 | tf_op jit(solution)/shard_map/mlp/pallas_call | solution.py:521
  483.4 10.0 all-to-all-done.2
  495.2 11.6 %attention_back.1 = bf16[8,3,72,384]{3,2,1,0:T(8,128)(2,1)} custom-call(bf16[8,3,72,384]{3,2,1,0:T(8,128)(2,1)} %bitcast.55.qkv_ref, bf16[8,3,72,128]{3,2,1,0:T(8,128)(2,1)S(1)} %bitcast.458), custom_call_target="tpu_custom_call" | custom-call | flops 1 | bytes 1 | tf_op jit(solution)/shard_map/attention_back/pallas_call | solution.py:603
  528.6 13.9 %all-to-all-done.3 = bf16[8,3,72,384]{3,2,1,0:T(8,128)(2,1)S(1)} async-done(((bf16[8,3,72,384]{3,2,1,0:T(8,128)(2,1)}), bf16[8,3,72,384]{3,2,1,0:T(8,128)(2,1)S(1)}, u32[]{:S(2)}, u32[]{:S(2)}) %all-to-all-start.3) | async-done | bytes 1327136 | tf_op jit(solution)/shard_map/all_to_all | solution.py:811
  607.8 27.7 %collective-permute-done.30 = bf16[3,72,1536]{2,1,0:T(8,128)(2,1)S(1)} collective-permute-done((bf16[3,72,1536]{2,1,0:T(8,128)(2,1)S(1)}, bf16[3,72,1536]{2,1,0:T(8,128)(2,1)S(1)}, u32[]{:S(2)}, u32[]{:S(2)}) %collective-permute-start.30) | collective-permute-done | bytes 663584 | tf_op jit(solution)/shard_map/ppermute | solution.py:34
  635.5 16.0 %collective-permute-done.31 = bf16[3,72,1536]{2,1,0:T(8,128)(2,1)S(1)} collective-permute-done((bf16[3,72,1536]{2,1,0:T(8,128)(2,1)S(1)}, bf16[3,72,1536]{2,1,0:T(8,128)(2,1)S(1)}, u32[]{:S(2)}, u32[]{:S(2)}) %collective-permute-start.31) | collective-permute-done | bytes 663584 | tf_op jit(solution)/shard_map/ppermute | solution.py:34
  664.3 11.7 %tall_near.2 = (bf16[2,768,768]{2,1,0:T(8,128)(2,1)}, bf16[2,768,768]{2,1,0:T(8,128)(2,1)}) custom-call(bf16[1728,1536]{1,0:T(8,128)(2,1)S(1)} %pad_maximum_fusion.5.a_ref, bf16[1728,768]{1,0:T(8,128)(2,1)S(1)} %copy-done.17, bf16[1728,768]{1,0:T(8,128)(2,1)S(1)} %copy-done.21, bf16[1728,768]{1,0:T(8,128)(2,1)S(1)} %copy-done.44), custom_call_target="tpu_custom_call" | custom-call | flops 1 | bytes 1 | tf_op jit(solution)/shard_map/tall_near/pallas_call | solution.py:481
  678.3 10.8 tall_keep.2
  689.1 8.2 back_slope.4.refs_0_
  732.7 23.8 %collective-permute-done.36 = bf16[2,768,768]{2,1,0:T(8,128)(2,1)} collective-permute-done((bf16[2,768,768]{2,1,0:T(8,128)(2,1)}, bf16[2,768,768]{2,1,0:T(8,128)(2,1)}, u32[]{:S(2)}, u32[]{:S(2)}) %collective-permute-start.36) | collective-permute-done | bytes 2359328 | tf_op jit(solution)/shard_map/ppermute | solution.py:28
  764.9 10.7 tall_near.3
  776.9 10.7 tall_keep.3
  808.8 11.4 %reduce_sum.127 = bf16[864,1536]{1,0:T(8,128)(2,1)S(1)} custom-call(bf16[1728,768]{1,0:T(8,128)(2,1)S(1)} %copy-done.24, bf16[1728,768]{1,0:T(8,128)(2,1)S(1)} %back_slope.5.refs_0_.refs_1_, bf16[1728,768]{1,0:T(8,128)(2,1)S(1)} %copy-done.7, bf16[1728,768]{1,0:T(8,128)(2,1)S(1)} %copy-done.27, bf16[1536,768]{1,0:T(8,128)(2,1)} %bitcast.6.w_ref.refs_4_, ...), custom_call_target="tpu_custom_call" | custom-call | flops 1 | bytes 1 | tf_op jit(solution)/shard_map/reduce_sum/pallas_call | solution.py:448
  856.4 11.4 %reduce_sum.128.here_ref = f32[864,1536]{1,0:T(8,128)S(1)} custom-call(bf16[1728,768]{1,0:T(8,128)(2,1)S(1)} %copy-done.25, bf16[1728,768]{1,0:T(8,128)(2,1)S(1)} %back_slope.5.refs_0_.refs_1_, bf16[1728,768]{1,0:T(8,128)(2,1)S(1)} %copy-done.8, bf16[1728,768]{1,0:T(8,128)(2,1)S(1)} %copy-done.28, bf16[1536,768]{1,0:T(8,128)(2,1)} %bitcast.6.w_ref.refs_4_, ...), custom_call_target="tpu_custom_call" | custom-call | flops 1 | bytes 1 | tf_op jit(solution)/shard_map/reduce_sum/pallas_call | solution.py:448
  870.2 16.2 %collective-permute-done.42 = bf16[2,768,768]{2,1,0:T(8,128)(2,1)} collective-permute-done((bf16[2,768,768]{2,1,0:T(8,128)(2,1)}, bf16[2,768,768]{2,1,0:T(8,128)(2,1)}, u32[]{:S(2)}, u32[]{:S(2)}) %collective-permute-start.42) | collective-permute-done | bytes 2359328 | tf_op jit(solution)/shard_map/ppermute | solution.py:28
  910.6 24.0 %tap_grad.1 = f32[7,8,1536]{2,1,0:T(8,128)S(1)} custom-call(bf16[3,18,40,1536]{3,2,1,0:T(8,128)(2,1)S(1)} %copy-done.10, bf16[3,12,24,1536]{3,2,1,0:T(8,128)(2,1)S(1)} %bitcast.449), custom_call_target="tpu_custom_call" | custom-call | flops 1 | bytes 1 | tf_op jit(solution)/shard_map/tap_grad/pallas_call | solution.py:328
  975.8 22.1 %collective-permute-done.53 = bf16[2,192,768]{2,1,0:T(8,128)(2,1)S(1)} collective-permute-done((bf16[2,192,768]{2,1,0:T(8,128)(2,1)S(1)}, bf16[2,192,768]{2,1,0:T(8,128)(2,1)S(1)}, u32[]{:S(2)}, u32[]{:S(2)}) %collective-permute-start.53) | collective-permute-done | bytes 589856 | tf_op jit(solution)/shard_map/ppermute | solution.py:28
  1002.6 23.0 %depthwise.3 = f32[3,12,24,1536]{3,2,1,0:T(8,128)S(1)} custom-call(bf16[3,18,40,1536]{3,2,1,0:T(8,128)(2,1)S(1)} %pad_maximum_fusion.1.x_ref, f32[7,8,1536]{2,1,0:T(8,128)S(1)} %rev.8.k_ref), custom_call_target="tpu_custom_call" | custom-call | flops 1 | bytes 1 | tf_op jit(solution)/shard_map/depthwise/pallas_call | solution.py:286
  1059.8 9.3 collective-permute-done.59
  1080.2 11.7 %collective-permute-done.68 = bf16[192,512]{1,0:T(8,128)(2,1)S(1)} collective-permute-done((bf16[192,512]{1,0:T(8,128)(2,1)S(1)}, bf16[192,512]{1,0:T(8,128)(2,1)S(1)}, u32[]{:S(2)}, u32[]{:S(2)}) %collective-permute-start.68) | collective-permute-done | bytes 196640 | tf_op jit(solution)/shard_map/ppermute | solution.py:49
  1106.8 23.0 %collective-permute-done.65 = bf16[2,192,768]{2,1,0:T(8,128)(2,1)S(1)} collective-permute-done((bf16[2,192,768]{2,1,0:T(8,128)(2,1)S(1)}, bf16[2,192,768]{2,1,0:T(8,128)(2,1)S(1)}, u32[]{:S(2)}, u32[]{:S(2)}) %collective-permute-start.65) | collective-permute-done | bytes 589856 | tf_op jit(solution)/shard_map/ppermute | solution.py:28
  (882 shorter events, 596.1 us)
Async XLA Ops:
  7.2 93.5 %all-gather.21.cloned.1.call-start = ((), (), s32[]{:S(2)}) async-start(), calls=%async_computation.15 | async-start | bytes 2949120 | tf_op jit(solution)/shard_map/all_gather | solution.py:121
  18.3 119.4 %all-gather.25.cloned.1.call-start = ((), (), s32[]{:S(2)}) async-start(), calls=%async_computation.17 | async-start | bytes 2949120 | tf_op jit(solution)/shard_map/all_gather | solution.py:121
  20.3 202.4 %all-gather.23.cloned.1.call-start = ((), (), s32[]{:S(2)}) async-start(), calls=%async_computation.16 | async-start | bytes 2949120 | tf_op jit(solution)/shard_map/all_gather | solution.py:121
  22.3 216.3 %all-gather.27.cloned.1.call-start = ((), (), s32[]{:S(2)}) async-start(), calls=%async_computation.18 | async-start | bytes 2949120 | tf_op jit(solution)/shard_map/all_gather | solution.py:121
  24.3 278.8 %all-gather.31.cloned.1.call-start = ((), (), s32[]{:S(2)}) async-start(), calls=%async_computation.20 | async-start | bytes 2621440 | tf_op jit(solution)/shard_map/all_gather | solution.py:164
  26.3 347.1 %all-gather.29.cloned.1.call-start = ((), (), s32[]{:S(2)}) async-start(), calls=%async_computation.19 | async-start | bytes 6488064 | tf_op jit(solution)/shard_map/all_gather | solution.py:257
  30.5 48.8 %collective-permute-start.1 = (bf16[3,3,24,1536]{3,2,1,0:T(8,128)(2,1)S(1)}, bf16[3,3,24,1536]{3,2,1,0:T(8,128)(2,1)S(1)}, u32[]{:S(2)}, u32[]{:S(2)}) collective-permute-start(bf16[3,3,24,1536]{3,2,1,0:T(8,128)(2,1)S(1)} %get-tuple-element.327), channel_id=1, source_target_pairs={{1,0},{2,1},{3,2},{5,4},{6,5},{7,6},{9,8},{10,9},{11,10},{13,12},{... | collective-permute-start | bytes 1990664 | tf_op jit(solution)/shard_map/ppermute | solution.py:34
  89.4 360.7 %all-gather.33.cloned.1.call-start = ((), (), s32[]{:S(2)}) async-start(), calls=%async_computation.21 | async-start | bytes 2162688 | tf_op jit(solution)/shard_map/all_gather | solution.py:257
  134.2 54.4 %collective-permute-start.6 = (bf16[1536,768]{1,0:T(8,128)(2,1)}, bf16[1536,768]{1,0:T(8,128)(2,1)}, u32[]{:S(2)}, u32[]{:S(2)}) collective-permute-start(bf16[1536,768]{1,0:T(8,128)(2,1)} %bitcast.6.w_ref.refs_4_), channel_id=1, source_target_pairs={{0,8},{8,0},{16,24},{24,16},{1,9},{9,1},{17,25},{25,17},{2,10},{10... | collective-permute-start | bytes 7077896 | tf_op jit(solution)/shard_map/ppermute | solution.py:28
  136.2 54.4 %collective-permute-start.7 = (bf16[1536,768]{1,0:T(8,128)(2,1)}, bf16[1536,768]{1,0:T(8,128)(2,1)}, u32[]{:S(2)}, u32[]{:S(2)}) collective-permute-start(bf16[1536,768]{1,0:T(8,128)(2,1)} %bitcast.6.w_ref.refs_4_), channel_id=1, source_target_pairs={{0,16},{8,24},{16,0},{24,8},{1,17},{9,25},{17,1},{25,9},{2,18},{10... | collective-permute-start | bytes 7077896 | tf_op jit(solution)/shard_map/ppermute | solution.py:28
  140.9 99.7 %collective-permute-start.9 = (bf16[1536,768]{1,0:T(8,128)(2,1)}, bf16[1536,768]{1,0:T(8,128)(2,1)}, u32[]{:S(2)}, u32[]{:S(2)}) collective-permute-start(bf16[1536,768]{1,0:T(8,128)(2,1)} %bitcast.19.refs_4_.w_ref), channel_id=1, source_target_pairs={{0,8},{8,0},{16,24},{24,16},{1,9},{9,1},{17,25},{25,17},{2,10},{10... | collective-permute-start | bytes 7077896 | tf_op jit(solution)/shard_map/ppermute | solution.py:28
  141.5 99.0 %collective-permute-start.10 = (bf16[1536,768]{1,0:T(8,128)(2,1)}, bf16[1536,768]{1,0:T(8,128)(2,1)}, u32[]{:S(2)}, u32[]{:S(2)}) collective-permute-start(bf16[1536,768]{1,0:T(8,128)(2,1)} %bitcast.19.refs_4_.w_ref), channel_id=1, source_target_pairs={{0,16},{8,24},{16,0},{24,8},{1,17},{9,25},{17,1},{25,9},{2,18},{10... | collective-permute-start | bytes 7077896 | tf_op jit(solution)/shard_map/ppermute | solution.py:28
  306.4 75.7 %collective-permute-start.18 = (bf16[2,1024,512]{2,1,0:T(8,128)(2,1)}, bf16[2,1024,512]{2,1,0:T(8,128)(2,1)}, u32[]{:S(2)}, u32[]{:S(2)}) collective-permute-start(bf16[2,1024,512]{2,1,0:T(8,128)(2,1)} %pad_maximum_fusion.6.refs_0_), channel_id=1, source_target_pairs={{0,8},{8,0},{16,24},{24,16},{1,9},{9,1},{17,25},{25,17},{2,10},{10... | collective-permute-start | bytes 6291464 | tf_op jit(solution)/shard_map/ppermute | solution.py:28
  306.8 75.2 %collective-permute-start.19 = (bf16[2,1024,512]{2,1,0:T(8,128)(2,1)}, bf16[2,1024,512]{2,1,0:T(8,128)(2,1)}, u32[]{:S(2)}, u32[]{:S(2)}) collective-permute-start(bf16[2,1024,512]{2,1,0:T(8,128)(2,1)} %pad_maximum_fusion.6.refs_0_), channel_id=1, source_target_pairs={{0,16},{8,24},{16,0},{24,8},{1,17},{9,25},{17,1},{25,9},{2,18},{10... | collective-permute-start | bytes 6291464 | tf_op jit(solution)/shard_map/ppermute | solution.py:28
  510.5 291.2 %reduce-scatter.5.cloned.1.call-start = ((), (), s32[]{:S(2)}) async-start(), calls=%async_computation.10 | async-start | bytes 7208960 | tf_op jit(solution)/shard_map/reduce_scatter | solution.py:218
  598.4 271.9 %all-gather.17.cloned.1.call-start = ((), (), s32[]{:S(2)}) async-start(), calls=%async_computation.9 | async-start | bytes 2949120 | tf_op jit(solution)/shard_map/all_gather | solution.py:857
  657.1 48.7 %collective-permute-start.34 = (bf16[2,1024,512]{2,1,0:T(8,128)(2,1)}, bf16[2,1024,512]{2,1,0:T(8,128)(2,1)S(1)}, u32[]{:S(2)}, u32[]{:S(2)}) collective-permute-start(bf16[2,1024,512]{2,1,0:T(8,128)(2,1)} %pad_maximum_fusion.7), channel_id=1, source_target_pairs={{0,8},{8,0},{16,24},{24,16},{1,9},{9,1},{17,25},{25,17},{2,10},{10... | collective-permute-start | bytes 6291464 | tf_op jit(solution)/shard_map/ppermute | solution.py:28
  660.2 48.9 %collective-permute-start.35 = (bf16[2,1024,512]{2,1,0:T(8,128)(2,1)}, bf16[2,1024,512]{2,1,0:T(8,128)(2,1)}, u32[]{:S(2)}, u32[]{:S(2)}) collective-permute-start(bf16[2,1024,512]{2,1,0:T(8,128)(2,1)} %pad_maximum_fusion.8), channel_id=1, source_target_pairs={{0,16},{8,24},{16,0},{24,8},{1,17},{9,25},{17,1},{25,9},{2,18},{10... | collective-permute-start | bytes 6291464 | tf_op jit(solution)/shard_map/ppermute | solution.py:28
  676.0 80.5 %collective-permute-start.36 = (bf16[2,768,768]{2,1,0:T(8,128)(2,1)}, bf16[2,768,768]{2,1,0:T(8,128)(2,1)}, u32[]{:S(2)}, u32[]{:S(2)}) collective-permute-start(bf16[2,768,768]{2,1,0:T(8,128)(2,1)} %get-tuple-element.146), channel_id=1, source_target_pairs={{0,8},{8,0},{16,24},{24,16},{1,9},{9,1},{17,25},{25,17},{2,10},{10... | collective-permute-start | bytes 7077896 | tf_op jit(solution)/shard_map/ppermute | solution.py:28
  676.9 82.7 %collective-permute-start.37 = (bf16[2,768,768]{2,1,0:T(8,128)(2,1)}, bf16[2,768,768]{2,1,0:T(8,128)(2,1)}, u32[]{:S(2)}, u32[]{:S(2)}) collective-permute-start(bf16[2,768,768]{2,1,0:T(8,128)(2,1)} %get-tuple-element.161), channel_id=1, source_target_pairs={{0,16},{8,24},{16,0},{24,8},{1,17},{9,25},{17,1},{25,9},{2,18},{10... | collective-permute-start | bytes 7077896 | tf_op jit(solution)/shard_map/ppermute | solution.py:28
  709.0 80.0 %collective-permute-start.38 = (bf16[1024,512]{1,0:T(8,128)(2,1)}, bf16[1024,512]{1,0:T(8,128)(2,1)}, u32[]{:S(2)}, u32[]{:S(2)}) collective-permute-start(bf16[1024,512]{1,0:T(8,128)(2,1)} %fusion.13), channel_id=1, source_target_pairs={{0,16},{8,24},{16,0},{24,8},{1,17},{9,25},{17,1},{25,9},{2,18},{10... | collective-permute-start | bytes 3145736 | tf_op jit(solution)/shard_map/ppermute | solution.py:28
  712.7 76.3 %collective-permute-start.39 = (bf16[1024,512]{1,0:T(8,128)(2,1)}, bf16[1024,512]{1,0:T(8,128)(2,1)}, u32[]{:S(2)}, u32[]{:S(2)}) collective-permute-start(bf16[1024,512]{1,0:T(8,128)(2,1)} %fusion.12), channel_id=1, source_target_pairs={{0,8},{8,0},{16,24},{24,16},{1,9},{9,1},{17,25},{25,17},{2,10},{10... | collective-permute-start | bytes 3145736 | tf_op jit(solution)/shard_map/ppermute | solution.py:28
  716.5 189.3 %reduce-scatter.7.cloned.1.call-start = ((), (), s32[]{:S(2)}) async-start(), calls=%async_computation.12 | async-start | bytes 2621440 | tf_op jit(solution)/shard_map/reduce_scatter | solution.py:177
  799.6 166.1 %reduce-scatter.9.cloned.1.call-start = ((), (), s32[]{:S(2)}) async-start(), calls=%async_computation.13 | async-start | bytes 2949120 | tf_op jit(solution)/shard_map/reduce_scatter | solution.py:145
  836.3 196.3 %all-gather.19.cloned.1.call-start = ((), (), s32[]{:S(2)}) async-start(), calls=%async_computation.11 | async-start | bytes 2949120 | tf_op jit(solution)/shard_map/all_gather | solution.py:857
  836.4 50.0 %collective-permute-start.42 = (bf16[2,768,768]{2,1,0:T(8,128)(2,1)}, bf16[2,768,768]{2,1,0:T(8,128)(2,1)}, u32[]{:S(2)}, u32[]{:S(2)}) collective-permute-start(bf16[2,768,768]{2,1,0:T(8,128)(2,1)} %copy-done.97), channel_id=1, source_target_pairs={{0,8},{8,0},{16,24},{24,16},{1,9},{9,1},{17,25},{25,17},{2,10},{10... | collective-permute-start | bytes 7077896 | tf_op jit(solution)/shard_map/ppermute | solution.py:28
  837.8 50.0 %collective-permute-start.43 = (bf16[2,768,768]{2,1,0:T(8,128)(2,1)}, bf16[2,768,768]{2,1,0:T(8,128)(2,1)}, u32[]{:S(2)}, u32[]{:S(2)}) collective-permute-start(bf16[2,768,768]{2,1,0:T(8,128)(2,1)} %copy-done.96), channel_id=1, source_target_pairs={{0,16},{8,24},{16,0},{24,8},{1,17},{9,25},{17,1},{25,9},{2,18},{10... | collective-permute-start | bytes 7077896 | tf_op jit(solution)/shard_map/ppermute | solution.py:28
  838.6 61.0 %collective-permute-start.44 = (bf16[864,1536]{1,0:T(8,128)(2,1)}, bf16[864,1536]{1,0:T(8,128)(2,1)}, u32[]{:S(2)}, u32[]{:S(2)}) collective-permute-start(bf16[864,1536]{1,0:T(8,128)(2,1)} %copy-done.61), channel_id=1, source_target_pairs={{0,4},{4,0},{1,5},{5,1},{2,6},{6,2},{3,7},{7,3},{8,12},{12,8},{9,1... | collective-permute-start | bytes 7962632 | tf_op jit(solution)/shard_map/ppermute | solution.py:24
  847.5 250.2 %reduce-scatter.11.cloned.1.call-start = ((), (), s32[]{:S(2)}) async-start(), calls=%async_computation.14 | async-start | bytes 2949120 | tf_op jit(solution)/shard_map/reduce_scatter | solution.py:145
  890.9 50.0 %collective-permute-start.49 = (bf16[768,768]{1,0:T(8,128)(2,1)}, bf16[768,768]{1,0:T(8,128)(2,1)}, u32[]{:S(2)}, u32[]{:S(2)}) collective-permute-start(bf16[768,768]{1,0:T(8,128)(2,1)} %fusion.25), channel_id=1, source_target_pairs={{0,16},{8,24},{16,0},{24,8},{1,17},{9,25},{17,1},{25,9},{2,18},{10... | collective-permute-start | bytes 3538952 | tf_op jit(solution)/shard_map/ppermute | solution.py:28
  894.4 48.6 %collective-permute-start.50 = (bf16[768,768]{1,0:T(8,128)(2,1)}, bf16[768,768]{1,0:T(8,128)(2,1)}, u32[]{:S(2)}, u32[]{:S(2)}) collective-permute-start(bf16[768,768]{1,0:T(8,128)(2,1)} %fusion.26), channel_id=1, source_target_pairs={{0,8},{8,0},{16,24},{24,16},{1,9},{9,1},{17,25},{25,17},{2,10},{10... | collective-permute-start | bytes 3538952 | tf_op jit(solution)/shard_map/ppermute | solution.py:28
  1050.0 47.6 %all-to-all-start.4 = ((bf16[8,2,128,128]{3,2,1,0:T(8,128)(2,1)}), bf16[8,2,128,128]{3,2,1,0:T(8,128)(2,1)S(1)}, u32[]{:S(2)}, u32[]{:S(2)}) async-start(bf16[8,2,128,128]{3,2,1,0:T(8,128)(2,1)} %bitcast.435), calls=%async_computation.8 | async-start | bytes 1048576 | tf_op jit(solution)/shard_map/all_to_all | solution.py:184
  (280 other events, 3177.6 us)
Sparse Core Ops, SparseCore 0:
  18.4 66.7 all-gather.20
  87.4 49.4 all-gather.24
  138.4 49.2 all-gather.22
  189.2 49.3 all-gather.26
  240.6 44.7 all-gather.30
  288.1 85.2 all-gather.28
  376.3 73.8 all-gather.32
  598.5 115.0 reduce-scatter.4
  716.6 49.9 all-gather.16
  799.7 42.0 reduce-scatter.6
  844.3 47.3 reduce-scatter.8
  893.2 53.0 all-gather.18
  1032.8 57.4 reduce-scatter.10

commit v3 on v2

--- a/solution.py
+++ b/solution.py
@@ -57,17 +57,17 @@
     return 4 if lax.axis_size("dp") == 4 else 1
 
 
-def reduce_dp(near_a, near_b, keep_a, keep_b):
+def reduce_dp(near_a, near_b, keep_a, keep_b, arrange):
     near_a, near_b = dp_swap(near_a, 1), dp_swap(near_b, 2)
 
     def first(*waits):
         a, b = later(near_a, *waits), later(near_b, *waits)
-        sent = add(keep_a[1], a[1]).astype(BF), add(keep_b[1], b[1]).astype(BF)
+        sent = sum_pairs([keep_a[1], (a, 1)], [keep_b[1], (b, 1)])
         last_a, last_b = dp_swap(sent[0], 2), dp_swap(sent[1], 1)
 
         def second(*waits):
             got_a, got_b = later(last_a, *waits), later(last_b, *waits)
-            return add(keep_a[0], a[0], got_a).astype(BF), add(keep_b[0], b[0], got_b).astype(BF)
+            return arrange([keep_a[0], (a, 0), (got_a, None)], [keep_b[0], (b, 0), (got_b, None)])
 
         return sent, second
 
@@ -99,6 +99,12 @@
     return functools.reduce(lambda a, b: a + b, [t.astype(F32) for t in terms])
 
 
+def sum_dp(v, before, after):
+    count = lax.axis_size("dp")
+    v = later(v, before)
+    return functools.reduce(lambda a, b: a + b, [v] + [later(dp_swap(v, k), after) for k in range(1, count)])
+
+
 def at_index(v, i, axis=0):
     return lax.dynamic_index_in_dim(v, i, axis, keepdims=False)
 
@@ -108,21 +114,30 @@
     return lax.dynamic_slice_in_dim(block, (strip_at * q + part) * width, width, 1)
 
 
-def gather_conv_weight(block):
+def gather_conv_weight(block, across):
     q = quarters()
     strip_at = lax.axis_index("strip")
-    parts = [0] if q == 1 else [lax.axis_index("dp"), lax.axis_index("dp") ^ 3]
-    mine = [hidden_share(block, strip_at, part, q) for part in parts]
-    width = mine[0].shape[1]
-    others = core_swap(jnp.concatenate([hidden_share(block, 1 - strip_at, part, q) for part in parts], axis=1))
-    both = [in_order(own, others[:, i * width : (i + 1) * width], strip_at) for i, own in enumerate(mine)]
+    width = block.shape[1] // (2 * q)
+    parts = [(0, width)] if q == 1 else [(lax.axis_index("dp"), width), (lax.axis_index("dp") ^ 3, int(width * across))]
+    cut = lambda core: [hidden_share(block, core, part, q)[:, :cols] for part, cols in parts]
+    mine = cut(strip_at)
+    others = core_swap(jnp.concatenate(cut(1 - strip_at), axis=1))
+    ends = [0, width, others.shape[1]]
+    both = [in_order(own, others[:, ends[i] : ends[i + 1]], strip_at) for i, own in enumerate(mine)]
 
     def along_z(i, *waits):
         whole = lax.all_gather(both[i], "tensor", axis=0)
         whole = later(whole, *waits) if waits else whole
-        return jnp.swapaxes(whole, 0, 1).reshape(-1, width)
+        return jnp.swapaxes(whole, 0, 1).reshape(-1, both[i].shape[2])
 
     return along_z
+
+
+def dp_across(near, first, *waits):
+    half, skip = near[0].shape[0] // 2, first.shape[1]
+    near = [later(n, *waits)[:, skip:] for n in near]
+    rest = jnp.concatenate([dp_swap(near[0][:half], 2), dp_swap(near[1][half:], 1)], axis=0)
+    return jnp.concatenate([first, rest], axis=1)
 
 
 def dp_neighbours(own):
@@ -138,29 +153,35 @@
     return [*near, *keep]
 
 
-def conv_halves(halves):
-    zs = lax.axis_size("tensor")
-    rows = halves[0].shape[0] // zs
-    view = jnp.concatenate([h[z * rows : (z + 1) * rows] for z in range(zs) for h in halves], axis=0)
-    return lax.psum_scatter(view, "tensor", scatter_dimension=0, tiled=True).reshape(2, rows, -1)
-
-
-def conv_rows(part, waits=()):
+def conv_dp(terms):
+    near_a, near_b, keep_a, keep_b = terms
+    return reduce_dp(near_a, near_b, [(keep_a, 0), (keep_a, 1)], [(keep_b, 0), (keep_b, 1)], sum_rows)
+
+
+def conv_scatter(view):
+    _, _, rows, width = view.shape
+    return lax.psum_scatter(view.reshape(-1, width), "tensor", scatter_dimension=0, tiled=True).reshape(2, rows, width)
+
+
+def conv_cores(part):
     strip_at = lax.axis_index("strip")
     mine = at_index(part, strip_at)
     other = core_swap(at_index(part, 1 - strip_at))
-    both = in_order(mine, other, strip_at)
+    return in_order(mine, other, strip_at)
+
+
+def conv_rows(both, *waits):
     if quarters() == 1:
         return jnp.concatenate(list(lax.psum(both, "dp")), axis=1).astype(F32)
     near = [dp_swap(both, k) for k in (1, 2, 3)]
-    every = dp_order([both] + [later(n, *waits) if waits else n for n in near])
+    every = dp_order([both] + [later(n, *waits) for n in near])
     return jnp.concatenate([every[d, c] for c in range(2) for d in range(4)], axis=1).astype(F32)
 
 
-def gather_mlp_weights(up, down):
+def gather_mlp_weights(up, down, *waits):
     q = quarters()
     strip_at, dp_at = lax.axis_index("strip"), lax.axis_index("dp") if q > 1 else 0
-    mine = jnp.concatenate([hidden_share(w, strip_at, dp_at, q) for w in (up, down)], axis=0)
+    mine = later(jnp.concatenate([hidden_share(w, strip_at, dp_at, q) for w in (up, down)], axis=0), *waits)
     whole = lax.all_gather(mine, "tensor", axis=0)
     return jnp.concatenate(list(whole), axis=1).reshape(2, up.shape[0], -1)
 
@@ -169,13 +190,15 @@
     return [dp_swap(near[0][0], 2), dp_swap(near[1][1], 1)] if near else []
 
 
-def mlp_scatter(own, dps):
-    width, all_cols = own[0].shape
-    zs = lax.axis_size("tensor")
-    cols = all_cols // zs
-    view = jnp.concatenate([v[:, z * cols : (z + 1) * cols] for z in range(zs) for v in own], axis=0)
-    part = lax.psum_scatter(view, "tensor", scatter_dimension=0, tiled=True)
-    return part.reshape(2, dps * 2, -1, cols)
+def mlp_scatter(terms, dps):
+    _, _, width, cols = terms.shape
+    if quarters() > 1:
+        terms = lax.psum_scatter(terms.reshape(-1, cols), "dp", scatter_dimension=0, tiled=True)
+    terms = terms.reshape(2, width, cols)
+    view = sum_cols([(terms, 0)], [(terms, 1)])
+    cols = view.shape[3]
+    part = lax.psum_scatter(view.reshape(-1, cols), "tensor", scatter_dimension=0, tiled=True)
+    return view, part.reshape(2, dps * 2, -1, cols)
 
 
 def mlp_rows(part, dps):
@@ -215,17 +238,22 @@
         return jnp.concatenate(groups, axis=0)
 
     sums = add(of_core(strip_at), core_swap(of_core(1 - strip_at))).astype(BF)
-    part = lax.psum_scatter(sums.reshape(-1, cut), "tensor", scatter_dimension=0, tiled=True)
-    return sums, part.reshape(dps, -1, cut)
-
-
-def rows_sum(whole, part):
+
+    def over_z(*waits):
+        part = lax.psum_scatter(later(sums, *waits).reshape(-1, cut), "tensor", scatter_dimension=0, tiled=True)
+        return part.reshape(dps, -1, cut)
+
+    return sums, over_z
+
+
+def rows_sum(whole, part, *waits):
     zs, dp_at = lax.axis_size("tensor"), lax.axis_index("dp")
     view, cut = rows_layout(whole)
     if quarters() == 1:
         total = lax.psum_scatter(part, "dp", scatter_dimension=0).astype(F32)
     else:
-        total = add(at_index(part, dp_at), *[dp_swap(at_index(part, dp_at ^ k), k) for k in (1, 2, 3)])
+        near = [dp_swap(at_index(part, dp_at ^ k), k) for k in (1, 2, 3)]
+        total = add(at_index(part, dp_at), *[later(n, *waits) for n in near])
     outs, at = [], 0
     for v in view:
         rows = v.shape[2]
@@ -235,17 +263,16 @@
     return outs
 
 
-def scatter_small(v, order):
-    for axis in order:
-        count, bit, at = lax.axis_size(axis), lax.axis_size(axis) // 2, lax.axis_index(axis)
-        while bit >= 1:
-            half = v.shape[1] // 2
-            upper = (at // bit) % 2
-            mine = lax.dynamic_slice_in_dim(v, upper * half, half, 1)
-            other = lax.dynamic_slice_in_dim(v, (1 - upper) * half, half, 1)
-            v = mine + lax.ppermute(other, axis, [(i, i ^ bit) for i in range(count)])
-            bit //= 2
-    return all_sum(v, [a for a in ("strip", "tensor", "dp") if a not in order])
+def scatter_steps(v, axis):
+    count, bit, at = lax.axis_size(axis), lax.axis_size(axis) // 2, lax.axis_index(axis)
+    while bit >= 1:
+        half = v.shape[1] // 2
+        upper = (at // bit) % 2
+        mine = lax.dynamic_slice_in_dim(v, upper * half, half, 1)
+        other = lax.dynamic_slice_in_dim(v, (1 - upper) * half, half, 1)
+        v = mine + lax.ppermute(other, axis, [(i, i ^ bit) for i in range(count)])
+        bit //= 2
+    return v
 
 
 def gather_rows(block):
@@ -262,18 +289,94 @@
     return pltpu.CompilerParams(vmem_limit_bytes=limit)
 
 
-def conv7_kernel(rows, cols, x_ref, k_ref, out_ref, wide):
+def add_kernel(counts, *refs):
+    outs = refs[sum(counts) :]
+    at = 0
+    for i, count in enumerate(counts):
+        total = add(*[r[0] if len(r.shape) == 3 else r[...] for r in refs[at : at + count]]).astype(BF)
+        if len(outs) == 1:
+            outs[0][0, i] = total
+        else:
+            outs[i][...] = total
+        at += count
+
+
+def sum_call(groups, grid, block, place, out_specs, out_shape, name):
+    specs = []
+    for array, lead in [term for group in groups for term in group]:
+        if lead is None:
+            specs.append(pl.BlockSpec(block, place))
+        else:
+            specs.append(pl.BlockSpec((1, *block), lambda i, lead=lead: (lead, *place(i))))
+    return pl.pallas_call(
+        functools.partial(add_kernel, [len(g) for g in groups]),
+        grid=(grid,),
+        in_specs=specs,
+        out_specs=out_specs,
+        out_shape=out_shape,
+        compiler_params=params(20 * 2**20),
+        cost_estimate=LIGHT,
+        name=name,
+    )(*[array for group in groups for array, _ in group])
+
+
+def sum_pairs(*groups):
+    rows, cols = groups[0][0][0].shape[-2:]
+    block, place = (256, cols), lambda i: (i, 0)
+    return sum_call(
+        groups,
+        rows // 256,
+        block,
+        place,
+        [pl.BlockSpec(block, place)] * len(groups),
+        [jax.ShapeDtypeStruct((rows, cols), BF)] * len(groups),
+        "sum_pairs",
+    )
+
+
+def sum_rows(*groups):
+    zs = lax.axis_size("tensor")
+    rows, cols = groups[0][0][0].shape[-2:]
+    rows = rows // zs
+    return sum_call(
+        groups,
+        zs,
+        (rows, cols),
+        lambda i: (i, 0),
+        pl.BlockSpec((1, 2, rows, cols), lambda i: (i, 0, 0, 0)),
+        jax.ShapeDtypeStruct((zs, 2, rows, cols), BF),
+        "sum_rows",
+    )
+
+
+def sum_cols(*groups):
+    zs = lax.axis_size("tensor")
+    rows, cols = groups[0][0][0].shape[-2:]
+    cols = cols // zs
+    return sum_call(
+        groups,
+        zs,
+        (rows, cols),
+        lambda i: (0, i),
+        pl.BlockSpec((1, 2, rows, cols), lambda i: (i, 0, 0, 0)),
+        jax.ShapeDtypeStruct((zs, 2, rows, cols), BF),
+        "sum_cols",
+    )
+
+
+def conv7_kernel(rows, cols, back, x_ref, k_ref, out_ref, wide):
     wide[...] = x_ref[0].astype(F32)
 
     def tap_row(i, sums):
         sums = list(sums)
-        taps = k_ref[i]
+        taps = k_ref[6 - i if back else i]
         for m in range(cols + 6):
             x = wide[m, pl.ds(i + EDGE - 3, rows), :]
             for j in range(7):
                 c = m - j
                 if 0 <= c < cols:
-                    sums[c] = sums[c] + x * taps[j : j + 1]
+                    tap = 6 - j if back else j
+                    sums[c] = sums[c] + x * taps[tap : tap + 1]
         return tuple(sums)
 
     sums = lax.fori_loop(0, 7, tap_row, tuple(jnp.zeros((rows, 128), F32) for _ in range(cols)))
@@ -281,10 +384,10 @@
         out_ref[0, c] = sums[c]
 
 
-def conv7(padded, taps, rows, cols):
+def conv7(padded, taps, rows, cols, back=False):
     items, _, _, channels = padded.shape
     return pl.pallas_call(
-        functools.partial(conv7_kernel, rows, cols),
+        functools.partial(conv7_kernel, rows, cols, back),
         grid=(items, channels // 128),
         in_specs=[
             pl.BlockSpec((1, cols + 6, rows + 2 * EDGE, 128), lambda b, c: (b, 0, 0, c)),
@@ -452,7 +555,7 @@
         + [pl.BlockSpec((bn, k), lambda j, i: (j, 0)) for k in ks],
         out_specs=pl.BlockSpec((bm, bn), lambda j, i: (i, j)),
         out_shape=jax.ShapeDtypeStruct((rows, n), dtype),
-        compiler_params=params(24 * 2**20),
+        compiler_params=params(52 * 2**20),
         cost_estimate=LIGHT,
         name="reduce_sum",
     )(*parts, *weights)
@@ -621,6 +724,11 @@
     after_ref[...] = total
     unit, _ = normalise(total)
     normed_ref[...] = (unit * gain_ref[...] + bias_ref[...]).astype(BF)
+
+
+def pair_kernel(after_ref, here_ref, there_ref, grad_ref, out_ref):
+    out_ref[0] = (after_ref[...] + here_ref[...] + there_ref[...].astype(F32)).astype(BF)
+    out_ref[1] = grad_ref[...].astype(BF)
 
 
 def mlp_kernel(count, x_ref, g_ref, *refs):
@@ -647,6 +755,37 @@
             back_ref[...] += back
 
 
+def mlp_terms(two, grad_out, actives, grads, dp_at):
+    count = len(actives)
+    cells, width = two.shape
+    cols = actives[0].shape[1]
+
+    def kernel(at_ref, two_ref, out_ref, *refs):
+        acts, ups, terms = refs[:count], refs[count : 2 * count], refs[-1]
+        for k in range(count):
+
+            @pl.when(pl.program_id(0) == k)
+            def _():
+                terms[0, 0] = lax.dot_general(two_ref[...], ups[k][...], DOWN_ROWS, preferred_element_type=F32).astype(BF)
+                terms[0, 1] = lax.dot_general(out_ref[...], acts[k][...], DOWN_ROWS, preferred_element_type=F32).astype(BF)
+
+    whole = lambda v: pl.BlockSpec(v.shape, lambda k, at: (0, 0))
+    arrays = [two, grad_out, *actives, *grads]
+    return pl.pallas_call(
+        kernel,
+        grid_spec=pltpu.PrefetchScalarGridSpec(
+            num_scalar_prefetch=1,
+            grid=(count,),
+            in_specs=[whole(v) for v in arrays],
+            out_specs=pl.BlockSpec((1, 2, width, cols), lambda k, at: (k ^ at[0], 0, 0, 0)),
+        ),
+        out_shape=jax.ShapeDtypeStruct((count, 2, width, cols), BF),
+        compiler_params=params(32 * 2**20),
+        cost_estimate=LIGHT,
+        name="mlp_terms",
+    )(dp_at.astype(jnp.int32).reshape(1) if count > 1 else jnp.zeros((1,), jnp.int32), *arrays)
+
+
 def lines(*rows):
     width = rows[0].shape[1]
     return jnp.concatenate(list(rows) + [jnp.zeros((8 - len(rows), width), F32)], axis=0)
@@ -716,7 +855,10 @@
 
 
 def wide_rim(v):
-    v = jnp.concatenate([shift(v[:, -3:], "tensor", 1), v, shift(v[:, :3], "tensor", -1)], axis=1)
+    return rows_rim(jnp.concatenate([shift(v[:, -3:], "tensor", 1), v, shift(v[:, :3], "tensor", -1)], axis=1))
+
+
+def rows_rim(v):
     return jnp.concatenate([shift(v[:, :, -EDGE:], "strip", 1), v, shift(v[:, :, :EDGE], "strip", -1)], axis=2)
 
 
@@ -734,11 +876,10 @@
     head_cols = w_qkv.shape[2]
     score_scale = HD**-0.5
 
-    expand_z, reduce_z = gather_conv_weight(w_expand), gather_conv_weight(w_reduce)
+    expand_z, reduce_z = gather_conv_weight(w_expand, 1), gather_conv_weight(w_reduce, 0.5)
     expand_own, reduce_own = expand_z(0), reduce_z(0)
     expand_near = dp_neighbours(expand_own)
     qkv_whole = gather_rows(jnp.swapaxes(w_qkv, 0, 1))
-    mlp_own = gather_mlp_weights(w_up, w_down)
     proj_whole = gather_rows(w_proj)
     count = quarters()
 
@@ -762,14 +903,16 @@
     pool = pool.reshape(items, 3 * grid_rows * grid_cols, map_cols * map_rows).astype(BF)
 
     masked = jnp.swapaxes(map_in, 1, 2) * cell_mask.astype(BF)
+    taps = jnp.pad(dw_kernel.T.reshape(7, 7, channels), ((0, 0), (0, 1), (0, 0)))
     padded = later(wide_rim(masked), expand_own)
-    taps = jnp.pad(dw_kernel.T.reshape(7, 7, channels), ((0, 0), (0, 1), (0, 0)))
     spread = conv7(padded, taps, map_rows, map_cols).reshape(cells, channels)
     reduce_near = dp_neighbours(later(reduce_own, spread))
     normed = norm_rows(spread, conv_gain, conv_bias)
+    if expand_near:
+        normed = later(normed, *expand_near)
     normed_both = jnp.concatenate([normed, core_swap(normed)], axis=0)
     expand_pieces, reduce_pieces, pairs = [expand_own, *expand_near], [reduce_own, *reduce_near], []
-    x = later(normed_both, *expand_near)
+    x = normed_both
     for k in range(count):
         if k == 3:
             expand_pieces.append(expand_z(1, pairs[2][0]))
@@ -777,8 +920,9 @@
         x = later(normed_both, pairs[k][0])
     acts, slopes = zip(*pairs)
     if count > 1:
-        reduce_pieces.append(reduce_z(1, acts[3]))
-    branch_there = core_swap(back_sum(acts, reduce_pieces, cells, cells, BF))
+        reduce_pieces.append(dp_across(reduce_near, reduce_z(1, acts[2]), acts[2]))
+    branch_sent = back_sum(acts, reduce_pieces, cells, cells, BF)
+    branch_there = core_swap(branch_sent)
     branch_here = back_sum(acts, reduce_pieces, 0, cells, F32)
     branch = (branch_here + branch_there.astype(F32)).reshape(masked.shape)
     map_value = cell_mask * (masked.astype(F32) + layer_scale * branch)
@@ -796,6 +940,7 @@
     pooled_low = pooled.astype(BF).reshape(tokens, channels)
     grid_shape = (items, grid_rows, grid_cols, width)
     adapted = jnp.dot(pooled_low, adapt_w, preferred_element_type=F32).reshape(grid_shape)
+    mlp_own = gather_mlp_weights(w_up, w_down, branch)
     adapted_pad = rim(adapted)
     local_mix = depthwise3(adapted_pad, mix_kernel, grid_rows, grid_cols)
     gate = jnp.tanh(gate_logit)
@@ -818,14 +963,11 @@
         "qkv",
     )
     mlp_near = dp_neighbours(mlp_own)
-    if mlp_near:
-        qkv = later(qkv, *mlp_near)
-    qkv = by_source(spread_heads(qkv))
+    qkv = later(by_source(spread_heads(qkv)), mlp_own, *mlp_near)
     mlp_weights = [mlp_own, *mlp_near, *mlp_far(mlp_near)]
     attention_flops = items * 2 * dots(24 * 24, 24 * 24, group)
     heads = by_item(functools.partial(attention_kernel, group), [qkv], group, 2 * attention_flops, "attention")
-    heads = later(heads, *mlp_weights)
-    heads = spread_heads(heads).reshape(2 * zs, tokens, group)
+    heads = later(spread_heads(heads).reshape(2 * zs, tokens, group), *mlp_weights)
     mixed, after_attn, normed_two = whole_call(
         functools.partial(project_kernel, zs, group),
         [shape(BF, tokens, width), shape(F32, tokens, width), shape(BF, tokens, width)],
@@ -852,21 +994,20 @@
         dots(tokens, width, width),
         "norm_back_two",
     )
-    grad_heads = by_source(spread_heads(grad_heads))
-    mlp_there = core_swap(mlp[tokens:].astype(BF))
-    every = lambda v: lax.all_gather(v.astype(BF).reshape(grid_shape), "tensor", axis=0)
-    to_grid = lambda v: jnp.concatenate(list(v), axis=2).astype(F32)
     down_terms = lambda left, rights: [
         lax.dot_general(left, r, DOWN_ROWS, preferred_element_type=F32).astype(BF) for r in rights
     ]
-    grad_down = down_terms(grad_mlp_both, actives)
-    grad_up = down_terms(two_both, grad_ups)
+    four = count > 1
+    mlp_grads = mlp_terms(two_both, grad_mlp_both, actives, grad_ups, dp_at)
+    grad_heads = by_source(spread_heads(grad_heads))
+    mlp_view, mlp_part = mlp_scatter(mlp_grads, dps)
+    mlp_there = core_swap(mlp[tokens:].astype(BF))
+    to_grid = lambda v: jnp.concatenate(list(v), axis=2).astype(F32)
 
     grad_qkv = by_item(
         functools.partial(attention_back_kernel, group), [qkv, grad_heads], 3 * group, 5 * attention_flops, "attention_back"
     )
-    vit_every = every(after_attn + mlp[:tokens] + later(mlp_there, grad_qkv).astype(F32))
-    grad_qkv = later(spread_heads(grad_qkv).reshape(2 * zs, tokens, 3 * group), *grad_down, *grad_up)
+    grad_qkv = later(spread_heads(grad_qkv).reshape(2 * zs, tokens, 3 * group), mlp_grads)
     grad_qkv, grad_joined, sums_one = whole_call(
         functools.partial(norm_back_one_kernel, zs, group),
         [shape(BF, tokens, 3 * width), shape(F32, tokens, width), shape(F32, 8, width)],
@@ -874,7 +1015,6 @@
         dots(tokens, width, 3 * width),
         "norm_back_one",
     )
-    grad_vit_every = every(grad_joined)
 
     grad_grid = grad_joined.reshape(grid_shape)
     over = (0, 1, 2)
@@ -887,6 +1027,8 @@
         for i in range(3)
         for j in range(3)
     ]
+    grad_adapted = later(grad_adapted, mlp_view)
+    grad_pooled = lax.dot_general(grad_adapted, adapt_w, ACROSS, preferred_element_type=F32).astype(BF)
     small_vit = jnp.stack(
         grad_taps
         + [
@@ -898,11 +1040,16 @@
         ],
         axis=0,
     )
-    row_terms = down_terms(normed_one, [grad_qkv]) + down_terms(grad_att, [mixed]) + down_terms(pooled_low, [grad_adapted])
-    grad_pooled = lax.dot_general(grad_adapted, adapt_w, ACROSS, preferred_element_type=F32).astype(BF)
+    small_vit = scatter_steps(scatter_steps(later(small_vit, grad_pooled), "dp"), "strip")
+    row_terms = (
+        down_terms(later(normed_one, grad_pooled), [grad_qkv])
+        + down_terms(later(grad_att, grad_pooled), [mixed])
+        + down_terms(later(pooled_low, grad_pooled), [grad_adapted])
+    )
     grad_pooled = grad_pooled.reshape(items, -1, channels)
+    rows_sums, rows_over_z = rows_scatter(row_terms)
     grad_pooled = jnp.concatenate(
-        [later(shift(grad_pooled, "tensor", 1), *row_terms), grad_pooled, shift(grad_pooled, "tensor", -1)], axis=1
+        [later(shift(grad_pooled, "tensor", 1), *row_terms, small_vit), grad_pooled, shift(grad_pooled, "tensor", -1)], axis=1
     )
     grad_map = lax.dot_general(pool, grad_pooled, (((1,), (1,)), ((0,), (0,))), preferred_element_type=F32)
     grad_map = jnp.swapaxes(d_map, 1, 2).astype(F32) + grad_map.reshape(masked.shape)
@@ -911,43 +1058,40 @@
     grad_scale = jnp.sum(kept * branch, axis=over)
     grad_branch = (kept * layer_scale).astype(BF).reshape(cells, channels)
     grad_branch_both = jnp.concatenate([grad_branch, core_swap(grad_branch)], axis=0)
-    pair = lambda a, b: jnp.stack([a, b], axis=0)
-    own_up, own_down = grad_up[0], grad_down[0]
-    four = count > 1
-    if four:
-        mlp_first = reduce_dp(
-            pair(grad_up[1], grad_up[3]), pair(grad_down[2], grad_down[3]), [own_up, grad_up[2]], [own_down, grad_down[1]]
-        )
-    rows_sums, rows_part = rows_scatter(row_terms)
+    rows_part = rows_over_z(grad_map)
     reduce_terms = conv_terms(grad_branch_both, acts, lambda v: later(v, rows_sums))
     grad_hidden, last = [], [reduce_terms[-1]]
     if four:
-        reduce_first = reduce_dp(*reduce_terms)
+        reduce_first = conv_dp(reduce_terms)
     for k in range(count):
-        if four and k == 2:
-            mlp_sent, mlp_second = mlp_first(last[0])
-            last += [*mlp_sent]
         last = [back_slope(later(grad_branch_both, *last), reduce_pieces[k], slopes[k])]
         grad_hidden += last
-    reduce_halves = jnp.split(reduce_terms[0], 2, axis=0)
+    (both_low,) = whole_call(
+        pair_kernel,
+        [shape(BF, 2, tokens, width)],
+        [after_attn, mlp[:tokens], later(mlp_there, rows_sums), grad_joined],
+        tokens * width,
+        "vit_pair",
+    )
+    both_every = lax.all_gather(both_low.reshape(2, *grid_shape), "tensor", axis=0)
     if four:
-        reduce_sent, reduce_second = reduce_first(last[0])
+        near = tall(later(normed_both, last[0]), grad_hidden[1:], [(0, 2), (1, 2)], "tall_near")
+        keep = tall(later(normed_both, near[0]), grad_hidden[:3], [(0, 2), (0, 1)], "tall_keep")
+        expand_first = conv_dp([*near, *keep])
+        done = keep[0]
+    else:
+        expand_terms = conv_terms(normed_both, grad_hidden, lambda v: later(v, *last))
+        done = expand_terms[0]
+    sent = later(grad_hidden[0], done)
+    normed_sent = back_sum([sent] + grad_hidden[1:], expand_pieces, cells, cells, BF)
+    last = [normed_sent, rows_part]
+    if four:
+        reduce_sent, reduce_second = reduce_first(normed_sent)
         last += [*reduce_sent]
-    expand_terms = conv_terms(normed_both, grad_hidden, lambda v: later(v, *last))
-    expand_halves = jnp.split(expand_terms[0], 2, axis=0)
-    last = [expand_terms[-1], rows_part]
-    if four:
-        expand_first = reduce_dp(*expand_terms)
-        own_up, own_down = mlp_second(expand_terms[-1])
-        last += [own_up, own_down]
-    mlp_part = mlp_scatter([own_up, own_down], dps)
-    sent = later(grad_hidden[0], *last)
-    normed_sent = back_sum([sent] + grad_hidden[1:], expand_pieces, cells, cells, BF)
-    last = [normed_sent]
-    if four:
-        reduce_halves = reduce_second(normed_sent)
-        last += [*reduce_halves]
-    reduce_part = conv_halves(reduce_halves)
+    else:
+        reduce_view, expand_view = (
+            jnp.swapaxes(t[0].reshape(2, zs, -1, t[0].shape[1]), 0, 1) for t in (reduce_terms, expand_terms)
+        )
     normed_there = core_swap(normed_sent)
     kept_here = later(grad_hidden[0], *last)
     normed_here = back_sum([kept_here] + grad_hidden[1:], expand_pieces, 0, cells, F32)
@@ -957,34 +1101,39 @@
         last += [*expand_sent]
     grad_spread, sums_conv = norm_rows_back(later(normed_here, *last), normed_there, spread, conv_gain)
     grad_spread = grad_spread.reshape(masked.shape)
-    mlp_part = later(mlp_part, grad_spread)
-    mlp_turned = jnp.swapaxes(mlp_part, 0, 1)
-    grad_taps = tap_grad(padded, later(grad_spread, mlp_turned), map_rows, map_cols)
+    beside = shift(grad_spread[:, -3:], "tensor", 1), shift(grad_spread[:, :3], "tensor", -1)
+    last = [both_every]
     if four:
-        expand_halves = expand_second(grad_taps)
-    expand_part = conv_halves(expand_halves)
-    out_qkv, out_proj, out_adapt = rows_sum(row_terms, later(rows_part, grad_taps))
-    out_reduce = conv_rows(later(reduce_part, grad_taps))
+        reduce_view = reduce_second(grad_spread)
+        last += [reduce_view]
+    reduce_part = conv_scatter(reduce_view)
+    grad_taps = tap_grad(padded, later(grad_spread, *last), map_rows, map_cols)
+    small_conv = jnp.concatenate([grad_taps.reshape(56, channels), sums_conv[:2], grad_scale[None]], axis=0)
+    rim_spread = jnp.concatenate([later(beside[0], grad_taps), grad_spread, later(beside[1], grad_taps)], axis=1)
+    if four:
+        expand_view = expand_second(rim_spread)
+    expand_part = conv_scatter(expand_view)
+    reduce_both = conv_cores(later(reduce_part, rim_spread))
+    small_conv = scatter_steps(later(small_conv, rim_spread), "strip")
     grad_map_in = conv7(
-        later(wide_rim(grad_spread), *expand_halves, out_reduce, out_qkv), taps[::-1, [6, 5, 4, 3, 2, 1, 0, 7]], map_rows, map_cols
-    )
-    grad_map_in = jnp.swapaxes(cell_mask * (kept + grad_map_in), 1, 2)
-    small_conv = jnp.concatenate(
-        [
-            grad_taps.reshape(56, channels),
-            sums_conv[:2],
-            grad_scale[None],
-        ],
-        axis=0,
-    )
-    out_up, out_down = mlp_rows(later(mlp_turned, grad_map_in), dps)
-    out_adapt = gather_bits(later(out_adapt.astype(BF), grad_map_in)).astype(F32)
-    vit_out = to_grid(later(vit_every, normed_here))
-    grad_vit = to_grid(later(grad_vit_every, grad_taps))
-    out_expand = conv_rows(expand_part)
-    small_vit, small_conv = later(small_vit, grad_map_in), later(small_conv, grad_map_in)
-    small_vit = scatter_small(small_vit, ("dp", "strip"))
-    small_conv = scatter_small(small_conv, ("strip", "tensor"))
+        later(rows_rim(rim_spread), expand_view, reduce_both, small_conv),
+        taps,
+        map_rows,
+        map_cols,
+        True,
+    )
+    out_reduce = conv_rows(reduce_both, grad_map_in)
+    small_conv = sum_dp(small_conv, reduce_both, grad_map_in)
+    out_up, out_down = mlp_rows(jnp.swapaxes(later(mlp_part, grad_map_in), 0, 1), dps)
+    out_qkv, out_proj, out_adapt = rows_sum(row_terms, rows_part, grad_map_in)
+    grad_map_in = jnp.swapaxes(cell_mask * (kept + later(grad_map_in, out_up)), 1, 2)
+    expand_both = conv_cores(later(expand_part, grad_map_in))
+    out_expand = conv_rows(expand_both)
+    both_every = later(both_every, expand_both)
+    vit_out, grad_vit = to_grid(both_every[:, 0]), to_grid(both_every[:, 1])
+    out_adapt = gather_bits(later(out_adapt.astype(BF), expand_both)).astype(F32)
+    small_conv = scatter_steps(later(small_conv, expand_both), "tensor")
+    small_vit = all_sum(later(small_vit, expand_both), ("tensor",))
     conv_share = channels // (2 * zs)
     out_taps = small_conv[:56].reshape(7, 8, conv_share)[:, :7].reshape(49, conv_share).T
     return (

time: 1150 us -> 1030 us (0.90)
  waiting for transfers between devices: 381 us -> 264 us
  blocking collectives: 0 us -> 53 us
  local copies, waits for them, and re-layouts: 192 us -> 148 us
  Pallas kernels: 266 us -> 299 us
  matrix products: 32.5 us -> 12.7 us
  starting transfers between devices: 126 us -> 112 us
    ppermute x20, waiting for transfers between devices: 118 us -> 47.7 us  [shift(): return lax.ppermute(v, axis, pairs)]
    all_to_all x0 -> x2, blocking collectives: none -> 53 us  [shards(): lax.all_to_all(v, ('strip', 'tensor'), 0, 0, tiled=True)]
    unnamed x492 -> x368, local copies, waits for them, and re-layouts: 111 us -> 68.2 us
    all_gather x4, waiting for transfers between devices: 1.14 us -> 42.6 us  [along_z(): whole = lax.all_gather(both[i], 'tensor', axis=0)]
    all_to_all x4 -> x2, waiting for transfers between devices: 52 us -> 11.5 us  [shards(): lax.all_to_all(v, ('strip', 'tensor'), 0, 0, tiled=True)]
    convert_element_type x15 -> x1, other arithmetic: 31.9 us -> 0.97 us  [shards(): gather_bits(later(out_adapt.astype(BF), expand_both)).astype(F32)]
    pallas_call x2 -> x8, Pallas kernels: 45.9 us -> 66.9 us  [the longest x2 45.9 us: conv7(): pl.pallas_call(functools.partial(conv7_kernel, rows, cols, back), grid=(i...]
    ppermute x29 -> x30, waiting for transfers between devices: 145 us -> 125 us  [dp_swap(): lax.ppermute(v, 'dp', [(i, i ^ bit) for i in range(lax.axis_size('dp'))])]
  transfers between devices with their start and end apart: 92 -> 89, of which waited for: 43 -> 37; matrix products, arithmetic and copies ran while one was open for 20% -> 19% of each run, Pallas kernels for 21% -> 27%
where the time goes in v3:
time: 1030 us
  Pallas kernels  299 us (29%)
  waiting for transfers between devices  264 us (26%)
  local copies, waits for them, and re-layouts  148 us (14%)
  other arithmetic  123 us (12%)
  starting transfers between devices  112 us (11%)
  blocking collectives  53 us (5%)
  between operations  16.9 us (2%)
  matrix products  12.7 us (1%)
    ppermute x30, waiting for transfers between devices, dp_swap(): lax.ppermute(v, 'dp', [(i, i ^ bit) for i in range(lax.axis_size('dp'))])  125 us
    unnamed x368, local copies, waits for them, and re-layouts  68.2 us
    pallas_call x4, Pallas kernels, back_sum(): pl.pallas_call(functools.partial(back_sum_kernel, len(parts)), grid=(n //...  66.2 us
    all_to_all x2, blocking collectives, shards(): lax.all_to_all(v, ('strip', 'tensor'), 0, 0, tiled=True)  53 us
    ppermute x20, starting transfers between devices, shift(): return lax.ppermute(v, axis, pairs)  48.9 us
    ppermute x20, waiting for transfers between devices, shift(): return lax.ppermute(v, axis, pairs)  47.7 us
    pallas_call x2, Pallas kernels, conv7(): pl.pallas_call(functools.partial(conv7_kernel, rows, cols, back), grid=(i...  45.9 us
    pallas_call x4, Pallas kernels, tall(): pl.pallas_call(kernel, grid=(2 * steps,), in_specs=[pl.BlockSpec((m, bm),...  44.4 us
  transfers between devices with their start and end apart: 89, of which 37 were waited for; matrix products, arithmetic and copies ran while one was open for 19% of the time, Pallas kernels for 27%

profile of v3, /device:TPU:0, one launch (start us, length us, event | category | flops | bytes accessed | tf_op | source)
XLA Modules:
  0.0 1028.6 jit_solution(12842138363684110168)
XLA Ops:
  40.7 37.9 %all-gather.18.cloned.1.call-done = bf16[8,192,768]{2,1,0:T(8,128)(2,1)} async-done(((bf16[2,192,768]{2,1,0:T(8,128)(2,1)}), bf16[8,192,768]{2,1,0:T(8,128)(2,1)}) %all-gather.18.cloned.1.call-update) | async-done | bytes 2359312 | tf_op jit(solution)/shard_map/all_gather | solution.py:129
  100.4 23.0 %depthwise.2 = f32[3,12,24,1536]{3,2,1,0:T(8,128)S(1)} custom-call(bf16[3,18,40,1536]{3,2,1,0:T(8,128)(2,1)S(1)} %pad_maximum_fusion.x_ref, f32[7,8,1536]{2,1,0:T(8,128)S(1)} %pad.4.k_ref), custom_call_target="tpu_custom_call" | custom-call | flops 1 | bytes 1 | tf_op jit(solution)/shard_map/depthwise/pallas_call | solution.py:389
  127.7 7.7 collective-permute-done.5.w_ref.refs_5_
  144.9 9.5 expand_gelu.4
  157.3 7.7 expand_gelu.5
  168.0 7.7 expand_gelu.6
  178.7 13.6 %collective-permute-done.9.refs_5_.w_ref = bf16[1536,768]{1,0:T(8,128)(2,1)S(1)} collective-permute-done((bf16[1536,768]{1,0:T(8,128)(2,1)S(1)}, bf16[1536,768]{1,0:T(8,128)(2,1)S(1)}, u32[]{:S(2)}, u32[]{:S(2)}) %collective-permute-start.9) | collective-permute-done | bytes 2359328 | tf_op jit(solution)/shard_map/ppermute | solution.py:28
  220.7 15.8 %reduce_sum.126 = bf16[864,1536]{1,0:T(8,128)(2,1)} custom-call(bf16[1728,768]{1,0:T(8,128)(2,1)} %copy-done.27, bf16[1728,768]{1,0:T(8,128)(2,1)} %copy-done.10, bf16[1728,768]{1,0:T(8,128)(2,1)} %copy-done.12, bf16[1728,768]{1,0:T(8,128)(2,1)} %copy-done.29, bf16[1536,768]{1,0:T(8,128)(2,1)} %bitcast.392, bf16[1536,768]{1,0:T(8,128)(2,1)} %copy-done.23, ...), custom_call_target="tpu_custom_call" | custom-call | flops 1 | bytes 1 | tf_op jit(solution)/shard_map/reduce_sum/pallas_call | solution.py:551
  241.9 16.7 %reduce_sum.125 = f32[864,1536]{1,0:T(8,128)} custom-call(bf16[1728,768]{1,0:T(8,128)(2,1)} %copy-done.27, bf16[1728,768]{1,0:T(8,128)(2,1)} %copy-done.10, bf16[1728,768]{1,0:T(8,128)(2,1)} %copy-done.12, bf16[1728,768]{1,0:T(8,128)(2,1)} %copy-done.29, bf16[1536,768]{1,0:T(8,128)(2,1)} %bitcast.393, bf16[1536,768]{1,0:T(8,128)(2,1)} %copy-done.23, ...), custom_call_target="tpu_custom_call" | custom-call | flops 1 | bytes 1 | tf_op jit(solution)/shard_map/reduce_sum/pallas_call | solution.py:551
  300.4 11.9 %collective-permute-done.14 = bf16[3,72,1536]{2,1,0:T(8,128)(2,1)} collective-permute-done((bf16[3,72,1536]{2,1,0:T(8,128)(2,1)}, bf16[3,72,1536]{2,1,0:T(8,128)(2,1)}, u32[]{:S(2)}, u32[]{:S(2)}) %collective-permute-start.14) | collective-permute-done | bytes 663584 | tf_op jit(solution)/shard_map/ppermute | solution.py:34
  328.0 7.2 collective-permute-start.18
  369.3 25.0 %collective-permute-done.20.refs_1_ = bf16[2,1024,512]{2,1,0:T(8,128)(2,1)} collective-permute-done((bf16[2,1024,512]{2,1,0:T(8,128)(2,1)}, bf16[2,1024,512]{2,1,0:T(8,128)(2,1)}, u32[]{:S(2)}, u32[]{:S(2)}) %collective-permute-start.20) | collective-permute-done | bytes 2097184 | tf_op jit(solution)/shard_map/ppermute | solution.py:28
  419.7 9.7 all-to-all-done.1
  435.0 11.5 %mlp.1 = (f32[432,1024]{1,0:T(8,128)S(1)}, f32[432,1024]{1,0:T(8,128)S(1)}, bf16[432,512]{1,0:T(8,128)(2,1)S(1)}, bf16[432,512]{1,0:T(8,128)(2,1)S(1)}, bf16[432...) custom-call(bf16[432,1024]{1,0:T(8,128)(2,1)S(1)} %constant_dynamic-, ...), custom_call_target="tpu_custom_call" | custom-call | flops 1 | bytes 1 | tf_op jit(solution)/shard_map/mlp/pallas_call | solution.py:624
  462.7 18.0 %all_to_all.25 = bf16[8,216,128]{2,1,0:T(8,128)(2,1)S(1)} all-to-all(bf16[8,216,128]{2,1,0:T(8,128)(2,1)S(1)} %get-tuple-element.152), channel_id=1, replica_groups=mesh['dp'=4,'strip'=2,'tensor'=4] {'strip','tensor'}, dimensions={0} | all-to-all | bytes 884736 | tf_op jit(solution)/shard_map/all_to_all | solution.py:956
  480.7 10.9 %attention_back.1 = bf16[8,3,72,384]{3,2,1,0:T(8,128)(2,1)S(1)} custom-call(bf16[8,3,72,384]{3,2,1,0:T(8,128)(2,1)} %bitcast.50.qkv_ref, bf16[8,3,72,128]{3,2,1,0:T(8,128)(2,1)S(1)} %bitcast.411), custom_call_target="tpu_custom_call" | custom-call | flops 1 | bytes 1 | tf_op jit(solution)/shard_map/attention_back/pallas_call | solution.py:706
  491.6 35.0 %all_to_all.26 = bf16[8,3,72,384]{3,2,1,0:T(8,128)(2,1)S(1)} all-to-all(bf16[8,3,72,384]{3,2,1,0:T(8,128)(2,1)S(1)} %attention_back.1), channel_id=1, replica_groups=mesh['dp'=4,'strip'=2,'tensor'=4] {'strip','tensor'}, dimensions={0} | all-to-all | bytes 2654208 | tf_op jit(solution)/shard_map/all_to_all | solution.py:956
  604.2 7.0 add_convert_fusion
  628.8 11.8 %tall_near.2 = (bf16[2,768,768]{2,1,0:T(8,128)(2,1)}, bf16[2,768,768]{2,1,0:T(8,128)(2,1)}) custom-call(bf16[1728,1536]{1,0:T(8,128)(2,1)S(1)} %pad_maximum_fusion.4.a_ref, bf16[1728,768]{1,0:T(8,128)(2,1)S(1)} %copy-done.11, bf16[1728,768]{1,0:T(8,128)(2,1)S(1)} %copy-done.13, bf16[1728,768]{1,0:T(8,128)(2,1)S(1)} %copy-done.30), custom_call_target="tpu_custom_call" | custom-call | flops 1 | bytes 1 | tf_op jit(solution)/shard_map/tall_near/pallas_call | solution.py:584
  642.6 10.7 %tall_keep.2 = (bf16[2,768,768]{2,1,0:T(8,128)(2,1)S(1)}, bf16[2,768,768]{2,1,0:T(8,128)(2,1)S(1)}) custom-call(bf16[1728,1536]{1,0:T(8,128)(2,1)S(1)} %pad_maximum_fusion.4.a_ref, bf16[1728,768]{1,0:T(8,128)(2,1)S(1)} %copy-done.28, bf16[1728,768]{1,0:T(8,128)(2,1)S(1)} %copy-done.11, bf16[1728,768]{1,0:T(8,128)(2,1)S(1)} %copy-done.13), custom_call_target="tpu_custom_call" | custom-call | flops 1 | bytes 1 | tf_op jit(solution)/shard_map/tall_keep/pallas_call | solution.py:584
  673.0 10.7 %tall_near.3 = (bf16[2,768,768]{2,1,0:T(8,128)(2,1)S(1)}, bf16[2,768,768]{2,1,0:T(8,128)(2,1)S(1)}) custom-call(bf16[1728,1536]{1,0:T(8,128)(2,1)S(1)} %bitcast.383, bf16[1728,768]{1,0:T(8,128)(2,1)S(1)} %back_slope.5.refs_0_.refs_1_, bf16[1728,768]{1,0:T(8,128)(2,1)S(1)} %back_slope.6.refs_1_.refs_2_, bf16[1728,768]{1,0:T(8,128)(2,1)S(1)} %back_slope.7.refs_2_.refs_3_), custom_call_target="tpu_custom_call" | custom-call | flops 1 | bytes 1 | tf_op jit(solution)/shard_map/tall_near/pallas_call | solution.py:584
  685.2 11.2 %tall_keep.3 = (bf16[2,768,768]{2,1,0:T(8,128)(2,1)S(1)}, bf16[2,768,768]{2,1,0:T(8,128)(2,1)S(1)}) custom-call(bf16[1728,1536]{1,0:T(8,128)(2,1)S(1)} %bitcast.383, bf16[1728,768]{1,0:T(8,128)(2,1)S(1)} %back_slope.4.refs_0_, bf16[1728,768]{1,0:T(8,128)(2,1)S(1)} %back_slope.5.refs_0_.refs_1_, bf16[1728,768]{1,0:T(8,128)(2,1)S(1)} %back_slope.6.refs_1_.refs_2_), custom_call_target="tpu_custom_call" | custom-call | flops 1 | bytes 1 | tf_op jit(solution)/shard_map/tall_keep/pallas_call | solution.py:584
  697.9 16.7 %reduce_sum.127 = bf16[864,1536]{1,0:T(8,128)(2,1)} custom-call(bf16[1728,768]{1,0:T(8,128)(2,1)} %copy-done.14, bf16[1728,768]{1,0:T(8,128)(2,1)} %copy-done.4, bf16[1728,768]{1,0:T(8,128)(2,1)} %copy-done.5, bf16[1728,768]{1,0:T(8,128)(2,1)} %copy-done.15, bf16[1536,768]{1,0:T(8,128)(2,1)} %bitcast.6.w_ref.refs_4_, ...), custom_call_target="tpu_custom_call" | custom-call | flops 1 | bytes 1 | tf_op jit(solution)/shard_map/reduce_sum/pallas_call | solution.py:551
  722.9 17.0 %reduce_sum.128.here_ref = f32[864,1536]{1,0:T(8,128)} custom-call(bf16[1728,768]{1,0:T(8,128)(2,1)} %copy-done.14, bf16[1728,768]{1,0:T(8,128)(2,1)} %copy-done.4, bf16[1728,768]{1,0:T(8,128)(2,1)} %copy-done.5, bf16[1728,768]{1,0:T(8,128)(2,1)} %copy-done.15, bf16[1536,768]{1,0:T(8,128)(2,1)} %bitcast.6.w_ref.refs_4_, ...), custom_call_target="tpu_custom_call" | custom-call | flops 1 | bytes 1 | tf_op jit(solution)/shard_map/reduce_sum/pallas_call | solution.py:551
  739.8 29.1 %collective-permute-done.42.refs_3_.refs_4_ = bf16[2,768,768]{2,1,0:T(8,128)(2,1)S(1)} collective-permute-done((bf16[2,768,768]{2,1,0:T(8,128)(2,1)}, bf16[2,768,768]{2,1,0:T(8,128)(2,1)S(1)}, u32[]{:S(2)}, u32[]{:S(2)}) %collective-permute-start.42) | collective-permute-done | bytes 2359328 | tf_op jit(solution)/shard_map/ppermute | solution.py:28
  782.0 12.3 %collective-permute-done.47.refs_5_ = bf16[768,768]{1,0:T(8,128)(2,1)} collective-permute-done((bf16[768,768]{1,0:T(8,128)(2,1)}, bf16[768,768]{1,0:T(8,128)(2,1)}, u32[]{:S(2)}, u32[]{:S(2)}) %collective-permute-start.47) | collective-permute-done | bytes 1179680 | tf_op jit(solution)/shard_map/ppermute | solution.py:28
  810.0 24.0 %tap_grad.1 = f32[7,8,1536]{2,1,0:T(8,128)S(1)} custom-call(bf16[3,18,40,1536]{3,2,1,0:T(8,128)(2,1)S(1)} %copy-done.7, bf16[3,12,24,1536]{3,2,1,0:T(8,128)(2,1)S(1)} %bitcast.400), custom_call_target="tpu_custom_call" | custom-call | flops 1 | bytes 1 | tf_op jit(solution)/shard_map/tap_grad/pallas_call | solution.py:431
  834.1 19.7 %collective-permute-done.48 = bf16[3,3,24,1536]{3,2,1,0:T(8,128)(2,1)} collective-permute-done((bf16[3,3,24,1536]{3,2,1,0:T(8,128)(2,1)}, bf16[3,3,24,1536]{3,2,1,0:T(8,128)(2,1)}, u32[]{:S(2)}, u32[]{:S(2)}) %collective-permute-start.48) | collective-permute-done | bytes 663584 | tf_op jit(solution)/shard_map/ppermute | solution.py:34
  869.2 19.5 %collective-permute-done.49.refs_5_ = bf16[768,768]{1,0:T(8,128)(2,1)} collective-permute-done((bf16[768,768]{1,0:T(8,128)(2,1)}, bf16[768,768]{1,0:T(8,128)(2,1)}, u32[]{:S(2)}, u32[]{:S(2)}) %collective-permute-start.49) | collective-permute-done | bytes 1179680 | tf_op jit(solution)/shard_map/ppermute | solution.py:28
  908.5 22.9 %depthwise.3 = f32[3,12,24,1536]{3,2,1,0:T(8,128)S(1)} custom-call(bf16[3,18,40,1536]{3,2,1,0:T(8,128)(2,1)S(1)} %pad_maximum_fusion.1.x_ref, f32[7,8,1536]{2,1,0:T(8,128)S(1)} %copy-done.61), custom_call_target="tpu_custom_call" | custom-call | flops 1 | bytes 1 | tf_op jit(solution)/shard_map/depthwise/pallas_call | solution.py:389
  953.1 7.8 multiply_bitcast_fusion
  962.9 13.2 %collective-permute-done.63 = bf16[2,192,768]{2,1,0:T(8,128)(2,1)S(1)} collective-permute-done((bf16[2,192,768]{2,1,0:T(8,128)(2,1)}, bf16[2,192,768]{2,1,0:T(8,128)(2,1)S(1)}, u32[]{:S(2)}, u32[]{:S(2)}) %collective-permute-start.63) | collective-permute-done | bytes 589856 | tf_op jit(solution)/shard_map/ppermute | solution.py:28
  (733 shorter events, 509.4 us)
Async XLA Ops:
  7.2 71.3 %all-gather.18.cloned.1.call-start = ((), (), s32[]{:S(2)}) async-start(), calls=%async_computation.16 | async-start | bytes 2949120 | tf_op jit(solution)/shard_map/all_gather | solution.py:129
  14.9 121.8 %all-gather.22.cloned.1.call-start = ((), (), s32[]{:S(2)}) async-start(), calls=%async_computation.18 | async-start | bytes 2949120 | tf_op jit(solution)/shard_map/all_gather | solution.py:129
  21.6 175.4 %all-gather.20.cloned.1.call-start = ((), (), s32[]{:S(2)}) async-start(), calls=%async_computation.17 | async-start | bytes 2949120 | tf_op jit(solution)/shard_map/all_gather | solution.py:129
  23.6 192.9 %all-gather.24.cloned.1.call-start = ((), (), s32[]{:S(2)}) async-start(), calls=%async_computation.19 | async-start | bytes 1474560 | tf_op jit(solution)/shard_map/all_gather | solution.py:129
  25.5 268.8 %all-gather.26.cloned.1.call-start = ((), (), s32[]{:S(2)}) async-start(), calls=%async_computation.20 | async-start | bytes 6488064 | tf_op jit(solution)/shard_map/all_gather | solution.py:284
  27.2 313.5 %all-gather.28.cloned.1.call-start = ((), (), s32[]{:S(2)}) async-start(), calls=%async_computation.21 | async-start | bytes 2621440 | tf_op jit(solution)/shard_map/all_gather | solution.py:185
  33.7 51.4 %collective-permute-start = (bf16[3,3,24,1536]{3,2,1,0:T(8,128)(2,1)}, bf16[3,3,24,1536]{3,2,1,0:T(8,128)(2,1)}, u32[]{:S(2)}, u32[]{:S(2)}) collective-permute-start(bf16[3,3,24,1536]{3,2,1,0:T(8,128)(2,1)} %get-tuple-element.439), channel_id=1, source_target_pairs={{0,1},{1,2},{2,3},{4,5},{5,6},{6,7},{8,9},{9,10},{10,11},{12,13},{... | collective-permute-start | bytes 1990664 | tf_op jit(solution)/shard_map/ppermute | solution.py:34
  39.4 45.8 %collective-permute-start.1 = (bf16[3,3,24,1536]{3,2,1,0:T(8,128)(2,1)}, bf16[3,3,24,1536]{3,2,1,0:T(8,128)(2,1)}, u32[]{:S(2)}, u32[]{:S(2)}) collective-permute-start(bf16[3,3,24,1536]{3,2,1,0:T(8,128)(2,1)} %get-tuple-element.440), channel_id=1, source_target_pairs={{1,0},{2,1},{3,2},{5,4},{6,5},{7,6},{9,8},{10,9},{11,10},{13,12},{... | collective-permute-start | bytes 1990664 | tf_op jit(solution)/shard_map/ppermute | solution.py:34
  82.0 53.5 %collective-permute-start.5 = (bf16[1536,768]{1,0:T(8,128)(2,1)}, bf16[1536,768]{1,0:T(8,128)(2,1)}, u32[]{:S(2)}, u32[]{:S(2)}) collective-permute-start(bf16[1536,768]{1,0:T(8,128)(2,1)} %bitcast.6.w_ref.refs_4_), channel_id=1, source_target_pairs={{0,8},{8,0},{16,24},{24,16},{1,9},{9,1},{17,25},{25,17},{2,10},{10... | collective-permute-start | bytes 7077896 | tf_op jit(solution)/shard_map/ppermute | solution.py:28
  83.7 53.0 %collective-permute-start.6 = (bf16[1536,768]{1,0:T(8,128)(2,1)}, bf16[1536,768]{1,0:T(8,128)(2,1)}, u32[]{:S(2)}, u32[]{:S(2)}) collective-permute-start(bf16[1536,768]{1,0:T(8,128)(2,1)} %bitcast.6.w_ref.refs_4_), channel_id=1, source_target_pairs={{0,16},{8,24},{16,0},{24,8},{1,17},{9,25},{17,1},{25,9},{2,18},{10... | collective-permute-start | bytes 7077896 | tf_op jit(solution)/shard_map/ppermute | solution.py:28
  138.6 53.7 %collective-permute-start.9 = (bf16[1536,768]{1,0:T(8,128)(2,1)S(1)}, bf16[1536,768]{1,0:T(8,128)(2,1)S(1)}, u32[]{:S(2)}, u32[]{:S(2)}) collective-permute-start(bf16[1536,768]{1,0:T(8,128)(2,1)S(1)} %bitcast.390), channel_id=1, source_target_pairs={{0,8},{8,0},{16,24},{24,16},{1,9},{9,1},{17,25},{25,17},{2,10},{10... | collective-permute-start | bytes 7077896 | tf_op jit(solution)/shard_map/ppermute | solution.py:28
  139.1 55.6 %collective-permute-start.10 = (bf16[1536,768]{1,0:T(8,128)(2,1)S(1)}, bf16[1536,768]{1,0:T(8,128)(2,1)S(1)}, u32[]{:S(2)}, u32[]{:S(2)}) collective-permute-start(bf16[1536,768]{1,0:T(8,128)(2,1)S(1)} %bitcast.391), channel_id=1, source_target_pairs={{0,16},{8,24},{16,0},{24,8},{1,17},{9,25},{17,1},{25,9},{2,18},{10... | collective-permute-start | bytes 7077896 | tf_op jit(solution)/shard_map/ppermute | solution.py:28
  265.4 164.0 %all-gather.30.cloned.1.call-start = ((), (), s32[]{:S(2)}) async-start(), calls=%async_computation.22 | async-start | bytes 2162688 | tf_op jit(solution)/shard_map/all_gather | solution.py:284
  343.9 50.3 %collective-permute-start.20 = (bf16[2,1024,512]{2,1,0:T(8,128)(2,1)}, bf16[2,1024,512]{2,1,0:T(8,128)(2,1)}, u32[]{:S(2)}, u32[]{:S(2)}) collective-permute-start(bf16[2,1024,512]{2,1,0:T(8,128)(2,1)} %pad_maximum_fusion.6.refs_0_), channel_id=1, source_target_pairs={{0,8},{8,0},{16,24},{24,16},{1,9},{9,1},{17,25},{25,17},{2,10},{10... | collective-permute-start | bytes 6291464 | tf_op jit(solution)/shard_map/ppermute | solution.py:28
  347.9 50.2 %collective-permute-start.21 = (bf16[2,1024,512]{2,1,0:T(8,128)(2,1)}, bf16[2,1024,512]{2,1,0:T(8,128)(2,1)}, u32[]{:S(2)}, u32[]{:S(2)}) collective-permute-start(bf16[2,1024,512]{2,1,0:T(8,128)(2,1)} %pad_maximum_fusion.6.refs_0_), channel_id=1, source_target_pairs={{0,16},{8,24},{16,0},{24,8},{1,17},{9,25},{17,1},{25,9},{2,18},{10... | collective-permute-start | bytes 6291464 | tf_op jit(solution)/shard_map/ppermute | solution.py:28
  416.2 141.9 %reduce-scatter.6.cloned.1.call-start = ((), (), s32[]{:S(2)}) async-start(), calls=%async_computation.10 | async-start | bytes 10485760 | tf_op jit(solution)/shard_map/reduce_scatter | solution.py:196
  455.3 267.6 %reduce-scatter.8.cloned.1.call-start = ((), (), s32[]{:S(2)}) async-start(), calls=%async_computation.12 | async-start | bytes 7208960 | tf_op jit(solution)/shard_map/reduce_scatter | solution.py:243
  611.3 195.9 %all-gather.16.cloned.1.call-start = ((), (), s32[]{:S(2)}) async-start(), calls=%async_computation.11 | async-start | bytes 4423680 | tf_op jit(solution)/shard_map/all_gather | solution.py:1076
  623.7 276.1 %reduce-scatter.12.cloned.1.call-start = ((), (), s32[]{:S(2)}) async-start(), calls=%async_computation.14 | async-start | bytes 2949120 | tf_op jit(solution)/shard_map/reduce_scatter | solution.py:163
  640.6 76.2 %collective-permute-start.41 = (bf16[2,768,768]{2,1,0:T(8,128)(2,1)}, bf16[2,768,768]{2,1,0:T(8,128)(2,1)}, u32[]{:S(2)}, u32[]{:S(2)}) collective-permute-start(bf16[2,768,768]{2,1,0:T(8,128)(2,1)} %get-tuple-element.196), channel_id=1, source_target_pairs={{0,16},{8,24},{16,0},{24,8},{1,17},{9,25},{17,1},{25,9},{2,18},{10... | collective-permute-start | bytes 7077896 | tf_op jit(solution)/shard_map/ppermute | solution.py:28
  642.3 74.5 %collective-permute-start.40 = (bf16[2,768,768]{2,1,0:T(8,128)(2,1)}, bf16[2,768,768]{2,1,0:T(8,128)(2,1)}, u32[]{:S(2)}, u32[]{:S(2)}) collective-permute-start(bf16[2,768,768]{2,1,0:T(8,128)(2,1)} %get-tuple-element.177), channel_id=1, source_target_pairs={{0,8},{8,0},{16,24},{24,16},{1,9},{9,1},{17,25},{25,17},{2,10},{10... | collective-permute-start | bytes 7077896 | tf_op jit(solution)/shard_map/ppermute | solution.py:28
  714.6 59.6 %collective-permute-start.44 = (bf16[864,1536]{1,0:T(8,128)(2,1)}, bf16[864,1536]{1,0:T(8,128)(2,1)}, u32[]{:S(2)}, u32[]{:S(2)}) collective-permute-start(bf16[864,1536]{1,0:T(8,128)(2,1)} %reduce_sum.127), channel_id=1, source_target_pairs={{0,4},{4,0},{1,5},{5,1},{2,6},{6,2},{3,7},{7,3},{8,12},{12,8},{9,1... | collective-permute-start | bytes 7962632 | tf_op jit(solution)/shard_map/ppermute | solution.py:24
  714.6 54.3 %collective-permute-start.42 = (bf16[2,768,768]{2,1,0:T(8,128)(2,1)}, bf16[2,768,768]{2,1,0:T(8,128)(2,1)S(1)}, u32[]{:S(2)}, u32[]{:S(2)}) collective-permute-start(bf16[2,768,768]{2,1,0:T(8,128)(2,1)} %copy-done.88), channel_id=1, source_target_pairs={{0,16},{8,24},{16,0},{24,8},{1,17},{9,25},{17,1},{25,9},{2,18},{10... | collective-permute-start | bytes 7077896 | tf_op jit(solution)/shard_map/ppermute | solution.py:28
  715.3 54.4 %collective-permute-start.39 = (bf16[2,768,768]{2,1,0:T(8,128)(2,1)}, bf16[2,768,768]{2,1,0:T(8,128)(2,1)}, u32[]{:S(2)}, u32[]{:S(2)}) collective-permute-start(bf16[2,768,768]{2,1,0:T(8,128)(2,1)} %copy-done.87), channel_id=1, source_target_pairs={{0,8},{8,0},{16,24},{24,16},{1,9},{9,1},{17,25},{25,17},{2,10},{10... | collective-permute-start | bytes 7077896 | tf_op jit(solution)/shard_map/ppermute | solution.py:28
  720.9 73.3 %collective-permute-start.47 = (bf16[768,768]{1,0:T(8,128)(2,1)}, bf16[768,768]{1,0:T(8,128)(2,1)}, u32[]{:S(2)}, u32[]{:S(2)}) collective-permute-start(bf16[768,768]{1,0:T(8,128)(2,1)} %get-tuple-element.199), channel_id=1, source_target_pairs={{0,8},{8,0},{16,24},{24,16},{1,9},{9,1},{17,25},{25,17},{2,10},{10... | collective-permute-start | bytes 3538952 | tf_op jit(solution)/shard_map/ppermute | solution.py:28
  721.5 72.8 %collective-permute-start.46 = (bf16[768,768]{1,0:T(8,128)(2,1)}, bf16[768,768]{1,0:T(8,128)(2,1)}, u32[]{:S(2)}, u32[]{:S(2)}) collective-permute-start(bf16[768,768]{1,0:T(8,128)(2,1)} %get-tuple-element.198), channel_id=1, source_target_pairs={{0,16},{8,24},{16,0},{24,8},{1,17},{9,25},{17,1},{25,9},{2,18},{10... | collective-permute-start | bytes 3538952 | tf_op jit(solution)/shard_map/ppermute | solution.py:28
  799.1 136.5 %reduce-scatter.14.cloned.1.call-start = ((), (), s32[]{:S(2)}) async-start(), calls=%async_computation.15 | async-start | bytes 2621440 | tf_op jit(solution)/shard_map/reduce_scatter | solution.py:200
  799.6 179.0 %reduce-scatter.10.cloned.1.call-start = ((), (), s32[]{:S(2)}) async-start(), calls=%async_computation.13 | async-start | bytes 2949120 | tf_op jit(solution)/shard_map/reduce_scatter | solution.py:163
  805.8 47.9 %collective-permute-start.48 = (bf16[3,3,24,1536]{3,2,1,0:T(8,128)(2,1)}, bf16[3,3,24,1536]{3,2,1,0:T(8,128)(2,1)}, u32[]{:S(2)}, u32[]{:S(2)}) collective-permute-start(bf16[3,3,24,1536]{3,2,1,0:T(8,128)(2,1)} %get-tuple-element.438), channel_id=1, source_target_pairs={{1,0},{2,1},{3,2},{5,4},{6,5},{7,6},{9,8},{10,9},{11,10},{13,12},{... | collective-permute-start | bytes 1990664 | tf_op jit(solution)/shard_map/ppermute | solution.py:34
  868.0 65.9 %collective-permute-start.66 = (bf16[704,256]{1,0:T(8,128)(2,1)}, bf16[704,256]{1,0:T(8,128)(2,1)}, u32[]{:S(2)}, u32[]{:S(2)}) collective-permute-start(bf16[704,256]{1,0:T(8,128)(2,1)} %get-tuple-element.467), channel_id=1, source_target_pairs={{0,8},{8,0},{16,24},{24,16},{1,9},{9,1},{17,25},{25,17},{2,10},{10... | collective-permute-start | bytes 1081352 | tf_op jit(solution)/shard_map/ppermute | solution.py:28
  888.7 46.8 %collective-permute-start.67 = (bf16[704,256]{1,0:T(8,128)(2,1)}, bf16[704,256]{1,0:T(8,128)(2,1)S(1)}, u32[]{:S(2)}, u32[]{:S(2)}) collective-permute-start(bf16[704,256]{1,0:T(8,128)(2,1)} %get-tuple-element.469), channel_id=1, source_target_pairs={{0,16},{8,24},{16,0},{24,8},{1,17},{9,25},{17,1},{25,9},{2,18},{10... | collective-permute-start | bytes 1081352 | tf_op jit(solution)/shard_map/ppermute | solution.py:28
  890.7 44.8 %collective-permute-start.68 = (bf16[704,256]{1,0:T(8,128)(2,1)}, bf16[704,256]{1,0:T(8,128)(2,1)}, u32[]{:S(2)}, u32[]{:S(2)}) collective-permute-start(bf16[704,256]{1,0:T(8,128)(2,1)} %get-tuple-element.468), channel_id=1, source_target_pairs={{0,24},{8,16},{16,8},{24,0},{1,25},{9,17},{17,9},{25,1},{2,26},{10... | collective-permute-start | bytes 1081352 | tf_op jit(solution)/shard_map/ppermute | solution.py:28
  (225 other events, 2790.8 us)
Sparse Core Ops, SparseCore 0:
  15.1 63.4 all-gather.17
  80.7 52.9 all-gather.21
  135.8 49.2 all-gather.19
  187.1 29.2 all-gather.23
  219.1 68.6 all-gather.25
  289.8 50.7 all-gather.27
  343.5 75.4 all-gather.29
  455.4 86.6 reduce-scatter.5
  611.4 100.0 reduce-scatter.7
  713.0 70.4 all-gather.15
  799.2 60.7 reduce-scatter.11
  862.3 43.4 reduce-scatter.13
  908.7 47.3 reduce-scatter.9

commit v4 on v3

--- a/solution.py
+++ b/solution.py
@@ -178,12 +178,12 @@
     return jnp.concatenate([every[d, c] for c in range(2) for d in range(4)], axis=1).astype(F32)
 
 
-def gather_mlp_weights(up, down, *waits):
+def gather_mlp_weights(up, down):
     q = quarters()
     strip_at, dp_at = lax.axis_index("strip"), lax.axis_index("dp") if q > 1 else 0
-    mine = later(jnp.concatenate([hidden_share(w, strip_at, dp_at, q) for w in (up, down)], axis=0), *waits)
+    mine = jnp.concatenate([hidden_share(w, strip_at, dp_at, q) for w in (up, down)], axis=0)
     whole = lax.all_gather(mine, "tensor", axis=0)
-    return jnp.concatenate(list(whole), axis=1).reshape(2, up.shape[0], -1)
+    return jnp.concatenate(list(whole), axis=1).reshape(2, up.shape[0], -1), whole
 
 
 def mlp_far(near):
@@ -197,8 +197,12 @@
     terms = terms.reshape(2, width, cols)
     view = sum_cols([(terms, 0)], [(terms, 1)])
     cols = view.shape[3]
-    part = lax.psum_scatter(view.reshape(-1, cols), "tensor", scatter_dimension=0, tiled=True)
-    return view, part.reshape(2, dps * 2, -1, cols)
+
+    def over_z(*waits):
+        part = lax.psum_scatter(later(view, *waits).reshape(-1, cols), "tensor", scatter_dimension=0, tiled=True)
+        return part.reshape(2, dps * 2, -1, cols)
+
+    return view, over_z
 
 
 def mlp_rows(part, dps):
@@ -275,14 +279,16 @@
     return v
 
 
-def gather_rows(block):
-    width, cols = block.shape[-2:]
+def gather_rows(block, *waits):
+    _, width, cols = block.shape
     dps, zs = lax.axis_size("dp"), lax.axis_size("tensor")
     rows = width // (2 * dps)
     at = lax.axis_index("dp") * 2 + lax.axis_index("strip")
-    mine = lax.dynamic_slice_in_dim(block.reshape(-1, width, cols), at * rows, rows, 1)
-    whole = lax.all_gather(mine, ("tensor", "dp", "strip"), axis=0).reshape(zs, 2 * dps, -1, rows, cols)
-    return jnp.concatenate([whole[:, :, a].reshape(zs, width, cols) for a in range(whole.shape[2])], axis=2)
+    mine = lax.dynamic_slice_in_dim(block, at * rows, rows, 1)
+    if waits:
+        mine = later(mine, *waits)
+    whole = lax.all_gather(mine, ("tensor", "dp", "strip"), axis=0)
+    return whole.reshape(zs, 2 * dps, -1, rows, cols)
 
 
 def params(limit=VMEM):
@@ -444,6 +450,28 @@
     )(padded, grad)
 
 
+def map_kernel(here_ref, there_ref, masked_ref, mask_ref, scale_ref, branch_ref, value_ref):
+    branch = here_ref[...] + there_ref[...].astype(F32)
+    branch_ref[...] = branch.astype(BF)
+    value_ref[...] = (mask_ref[...] * (masked_ref[...].astype(F32) + scale_ref[...] * branch)).astype(BF)
+
+
+def map_value_rows(here, there, masked, mask, scale):
+    rows, width = here.shape
+    block = row_block(rows, 144)
+    tile, line = pl.BlockSpec((block, width), lambda i: (i, 0)), pl.BlockSpec((1, width), lambda i: (0, 0))
+    return pl.pallas_call(
+        map_kernel,
+        grid=(rows // block,),
+        in_specs=[tile, tile, tile, pl.BlockSpec((block, 1), lambda i: (i, 0)), line],
+        out_specs=[tile, tile],
+        out_shape=[jax.ShapeDtypeStruct((rows, width), BF)] * 2,
+        compiler_params=params(20 * 2**20),
+        cost_estimate=LIGHT,
+        name="map_value",
+    )(here, there, masked, mask, scale.reshape(1, width))
+
+
 def norm_kernel(v_ref, gain_ref, bias_ref, out_ref):
     unit, _ = normalise(v_ref[...])
     out_ref[...] = (unit * gain_ref[...] + bias_ref[...]).astype(BF)
@@ -636,16 +664,20 @@
     return jax.ShapeDtypeStruct(dims, dtype)
 
 
+def shares(w_ref, z, a):
+    _, count, _, rows, cols = w_ref.shape
+    return w_ref[z, :, a].reshape(count * rows, cols)
+
+
 def qkv_kernel(zs, group, joined_ref, gain_ref, bias_ref, w_ref, normed_ref, out_ref):
     unit, _ = normalise(joined_ref[...])
     normed = (unit * gain_ref[...] + bias_ref[...]).astype(BF)
     normed_ref[...] = normed
     for z in range(zs):
-        part = jnp.dot(normed, w_ref[z], preferred_element_type=F32).astype(BF)
         for a in range(3):
+            part = jnp.dot(normed, shares(w_ref, z, a), preferred_element_type=F32).astype(BF)
             for core in range(2):
-                at = (2 * a + core) * group
-                out_ref[core * zs + z, :, a * group : (a + 1) * group] = part[:, at : at + group]
+                out_ref[core * zs + z, :, a * group : (a + 1) * group] = part[:, core * group : (core + 1) * group]
 
 
 def tokens_of(ref):
@@ -808,11 +840,11 @@
 def norm_back_one_kernel(zs, group, g_ref, w_ref, joined_ref, after_ref, gain_ref, all_ref, grad_ref, sums_ref):
     grad_one = jnp.zeros(joined_ref.shape, F32)
     for z in range(zs):
-        part = jnp.concatenate(
-            [g_ref[core * zs + z, :, a * group : (a + 1) * group] for a in range(3) for core in range(2)], axis=1
-        )
-        all_ref[:, z * 6 * group : (z + 1) * 6 * group] = part
-        grad_one = grad_one + lax.dot_general(part, w_ref[z], ACROSS, preferred_element_type=F32)
+        for a in range(3):
+            part = jnp.concatenate([g_ref[core * zs + z, :, a * group : (a + 1) * group] for core in range(2)], axis=1)
+            at = (3 * z + a) * 2 * group
+            all_ref[:, at : at + 2 * group] = part
+            grad_one = grad_one + lax.dot_general(part, shares(w_ref, z, a), ACROSS, preferred_element_type=F32)
     unit, scale = normalise(joined_ref[...])
     sums_ref[...] = lines(jnp.sum(grad_one * unit, axis=0, keepdims=True), jnp.sum(grad_one, axis=0, keepdims=True))
     grad_ref[...] = after_ref[...] + normalise_back(grad_one, unit, scale, gain_ref[...])
@@ -852,10 +884,6 @@
 def rim(v):
     v = jnp.concatenate([shift(v[:, -1:], "strip", 1), v, shift(v[:, :1], "strip", -1)], axis=1)
     return jnp.concatenate([shift(v[:, :, -1:], "tensor", 1), v, shift(v[:, :, :1], "tensor", -1)], axis=2)
-
-
-def wide_rim(v):
-    return rows_rim(jnp.concatenate([shift(v[:, -3:], "tensor", 1), v, shift(v[:, :3], "tensor", -1)], axis=1))
 
 
 def rows_rim(v):
@@ -879,8 +907,9 @@
     expand_z, reduce_z = gather_conv_weight(w_expand, 1), gather_conv_weight(w_reduce, 0.5)
     expand_own, reduce_own = expand_z(0), reduce_z(0)
     expand_near = dp_neighbours(expand_own)
-    qkv_whole = gather_rows(jnp.swapaxes(w_qkv, 0, 1))
-    proj_whole = gather_rows(w_proj)
+    mlp_own, mlp_gathered = gather_mlp_weights(w_up, w_down)
+    qkv_whole = gather_rows(jnp.swapaxes(w_qkv, 0, 1), mlp_gathered)
+    proj_whole = gather_rows(w_proj[None]).reshape(zs, width, head_cols)
     count = quarters()
 
     side = res_code // 32
@@ -904,7 +933,8 @@
 
     masked = jnp.swapaxes(map_in, 1, 2) * cell_mask.astype(BF)
     taps = jnp.pad(dw_kernel.T.reshape(7, 7, channels), ((0, 0), (0, 1), (0, 0)))
-    padded = later(wide_rim(masked), expand_own)
+    edges = [later(shift(e, "tensor", step), pool, expand_own) for e, step in ((masked[:, -3:], 1), (masked[:, :3], -1))]
+    padded = rows_rim(jnp.concatenate([edges[0], masked, edges[1]], axis=1))
     spread = conv7(padded, taps, map_rows, map_cols).reshape(cells, channels)
     reduce_near = dp_neighbours(later(reduce_own, spread))
     normed = norm_rows(spread, conv_gain, conv_bias)
@@ -924,9 +954,10 @@
     branch_sent = back_sum(acts, reduce_pieces, cells, cells, BF)
     branch_there = core_swap(branch_sent)
     branch_here = back_sum(acts, reduce_pieces, 0, cells, F32)
-    branch = (branch_here + branch_there.astype(F32)).reshape(masked.shape)
-    map_value = cell_mask * (masked.astype(F32) + layer_scale * branch)
-    map_low = map_value.astype(BF)
+    branch, map_low = map_value_rows(
+        branch_here, branch_there, masked.reshape(cells, channels), cell_mask.reshape(cells, 1), layer_scale
+    )
+    branch, map_low = branch.reshape(masked.shape), map_low.reshape(masked.shape)
     map_out = jnp.swapaxes(map_low, 1, 2)
 
     pooled3 = lax.dot_general(
@@ -940,7 +971,6 @@
     pooled_low = pooled.astype(BF).reshape(tokens, channels)
     grid_shape = (items, grid_rows, grid_cols, width)
     adapted = jnp.dot(pooled_low, adapt_w, preferred_element_type=F32).reshape(grid_shape)
-    mlp_own = gather_mlp_weights(w_up, w_down, branch)
     adapted_pad = rim(adapted)
     local_mix = depthwise3(adapted_pad, mix_kernel, grid_rows, grid_cols)
     gate = jnp.tanh(gate_logit)
@@ -998,9 +1028,9 @@
         lax.dot_general(left, r, DOWN_ROWS, preferred_element_type=F32).astype(BF) for r in rights
     ]
     four = count > 1
-    mlp_grads = mlp_terms(two_both, grad_mlp_both, actives, grad_ups, dp_at)
-    grad_heads = by_source(spread_heads(grad_heads))
-    mlp_view, mlp_part = mlp_scatter(mlp_grads, dps)
+    mlp_grads = mlp_terms(later(two_both, grad_heads), grad_mlp_both, actives, grad_ups, dp_at)
+    grad_heads = later(by_source(spread_heads(grad_heads)), mlp_grads)
+    mlp_view, mlp_over_z = mlp_scatter(mlp_grads, dps)
     mlp_there = core_swap(mlp[tokens:].astype(BF))
     to_grid = lambda v: jnp.concatenate(list(v), axis=2).astype(F32)
 
@@ -1018,17 +1048,18 @@
 
     grad_grid = grad_joined.reshape(grid_shape)
     over = (0, 1, 2)
-    grad_gate = jnp.sum(grad_grid * local_mix, axis=over) * (1.0 - gate * gate)
     grad_mix = grad_grid * gate
     grad_adapted = depthwise3(rim(grad_mix), mix_kernel[:, ::-1], grid_rows, grid_cols)
     grad_adapted = grad_adapted.astype(BF).reshape(tokens, width)
+    grad_adapted = later(grad_adapted, mlp_view)
+    grad_pooled = lax.dot_general(grad_adapted, adapt_w, ACROSS, preferred_element_type=F32).astype(BF)
+    grad_late = later(grad_grid, grad_pooled)
+    grad_gate = jnp.sum(grad_late * local_mix, axis=over) * (1.0 - gate * gate)
     grad_taps = [
-        jnp.sum(adapted_pad[:, i : i + grid_rows, j : j + grid_cols] * grad_mix, axis=over)
+        jnp.sum(adapted_pad[:, i : i + grid_rows, j : j + grid_cols] * (grad_late * gate), axis=over)
         for i in range(3)
         for j in range(3)
     ]
-    grad_adapted = later(grad_adapted, mlp_view)
-    grad_pooled = lax.dot_general(grad_adapted, adapt_w, ACROSS, preferred_element_type=F32).astype(BF)
     small_vit = jnp.stack(
         grad_taps
         + [
@@ -1055,7 +1086,7 @@
     grad_map = jnp.swapaxes(d_map, 1, 2).astype(F32) + grad_map.reshape(masked.shape)
 
     kept = cell_mask * grad_map
-    grad_scale = jnp.sum(kept * branch, axis=over)
+    grad_scale = jnp.sum(kept * branch.astype(F32), axis=over)
     grad_branch = (kept * layer_scale).astype(BF).reshape(cells, channels)
     grad_branch_both = jnp.concatenate([grad_branch, core_swap(grad_branch)], axis=0)
     rows_part = rows_over_z(grad_map)
@@ -1082,41 +1113,45 @@
     else:
         expand_terms = conv_terms(normed_both, grad_hidden, lambda v: later(v, *last))
         done = expand_terms[0]
-    sent = later(grad_hidden[0], done)
+    last = [done]
+    if four:
+        reduce_sent, reduce_second = reduce_first(done)
+        last += [*reduce_sent]
+    sent = later(grad_hidden[0], *last)
     normed_sent = back_sum([sent] + grad_hidden[1:], expand_pieces, cells, cells, BF)
-    last = [normed_sent, rows_part]
+    normed_there = core_swap(normed_sent)
+    kept_here = later(grad_hidden[0], normed_sent)
+    normed_here = back_sum([kept_here] + grad_hidden[1:], expand_pieces, 0, cells, F32)
+    last = [normed_here, rows_part]
     if four:
-        reduce_sent, reduce_second = reduce_first(normed_sent)
-        last += [*reduce_sent]
+        reduce_view = reduce_second(normed_here)
+        last += [reduce_view]
     else:
         reduce_view, expand_view = (
             jnp.swapaxes(t[0].reshape(2, zs, -1, t[0].shape[1]), 0, 1) for t in (reduce_terms, expand_terms)
         )
-    normed_there = core_swap(normed_sent)
-    kept_here = later(grad_hidden[0], *last)
-    normed_here = back_sum([kept_here] + grad_hidden[1:], expand_pieces, 0, cells, F32)
-    last = [normed_here]
-    if four:
-        expand_sent, expand_second = expand_first(normed_here)
-        last += [*expand_sent]
+    reduce_part = conv_scatter(reduce_view)
     grad_spread, sums_conv = norm_rows_back(later(normed_here, *last), normed_there, spread, conv_gain)
     grad_spread = grad_spread.reshape(masked.shape)
     beside = shift(grad_spread[:, -3:], "tensor", 1), shift(grad_spread[:, :3], "tensor", -1)
     last = [both_every]
     if four:
-        reduce_view = reduce_second(grad_spread)
-        last += [reduce_view]
-    reduce_part = conv_scatter(reduce_view)
+        expand_sent, expand_second = expand_first(grad_spread)
+        last += [*expand_sent]
     grad_taps = tap_grad(padded, later(grad_spread, *last), map_rows, map_cols)
+    last = [grad_taps]
+    if four:
+        expand_view = expand_second(grad_taps)
+        last += [expand_view]
     small_conv = jnp.concatenate([grad_taps.reshape(56, channels), sums_conv[:2], grad_scale[None]], axis=0)
-    rim_spread = jnp.concatenate([later(beside[0], grad_taps), grad_spread, later(beside[1], grad_taps)], axis=1)
-    if four:
-        expand_view = expand_second(rim_spread)
+    rim_spread = jnp.concatenate([later(beside[0], *last), grad_spread, later(beside[1], *last)], axis=1)
     expand_part = conv_scatter(expand_view)
     reduce_both = conv_cores(later(reduce_part, rim_spread))
     small_conv = scatter_steps(later(small_conv, rim_spread), "strip")
+    wide_spread = rows_rim(rim_spread)
+    mlp_part = mlp_over_z(wide_spread)
     grad_map_in = conv7(
-        later(rows_rim(rim_spread), expand_view, reduce_both, small_conv),
+        later(wide_spread, reduce_both, small_conv),
         taps,
         map_rows,
         map_cols,
@@ -1124,11 +1159,11 @@
     )
     out_reduce = conv_rows(reduce_both, grad_map_in)
     small_conv = sum_dp(small_conv, reduce_both, grad_map_in)
-    out_up, out_down = mlp_rows(jnp.swapaxes(later(mlp_part, grad_map_in), 0, 1), dps)
     out_qkv, out_proj, out_adapt = rows_sum(row_terms, rows_part, grad_map_in)
-    grad_map_in = jnp.swapaxes(cell_mask * (kept + later(grad_map_in, out_up)), 1, 2)
+    grad_map_in = jnp.swapaxes(cell_mask * (kept + grad_map_in), 1, 2)
     expand_both = conv_cores(later(expand_part, grad_map_in))
     out_expand = conv_rows(expand_both)
+    out_up, out_down = mlp_rows(jnp.swapaxes(later(mlp_part, expand_both), 0, 1), dps)
     both_every = later(both_every, expand_both)
     vit_out, grad_vit = to_grid(both_every[:, 0]), to_grid(both_every[:, 1])
     out_adapt = gather_bits(later(out_adapt.astype(BF), expand_both)).astype(F32)

time: 1030 us -> 983 us (0.954)
  waiting for transfers between devices: 264 us -> 213 us
  other arithmetic: 123 us -> 107 us
  local copies, waits for them, and re-layouts: 148 us -> 159 us
    ppermute x30, waiting for transfers between devices: 125 us -> 75.7 us  [dp_swap(): lax.ppermute(v, 'dp', [(i, i ^ bit) for i in range(lax.axis_size('dp'))])]
    unnamed x368 -> x366, local copies, waits for them, and re-layouts: 68.2 us -> 82.9 us
    all_gather x4, waiting for transfers between devices: 42.6 us -> 29.8 us  [along_z(): whole = lax.all_gather(both[i], 'tensor', axis=0)]
  transfers between devices with their start and end apart: 89 -> 89, of which waited for: 37 -> 37; matrix products, arithmetic and copies ran while one was open for 19% -> 18% of each run, Pallas kernels for 27% -> 29%
where the time goes in v4:
time: 983 us; the launch traced here: 975 us
  Pallas kernels  304 us (31%)
  waiting for transfers between devices  213 us (22%)
  local copies, waits for them, and re-layouts  159 us (16%)
  starting transfers between devices  107 us (11%)
  other arithmetic  107 us (11%)
  blocking collectives  50.8 us (5%)
  between operations  17.3 us (2%)
  matrix products  16.9 us (2%)
    unnamed x366, local copies, waits for them, and re-layouts  82.9 us
    ppermute x30, waiting for transfers between devices, dp_swap(): lax.ppermute(v, 'dp', [(i, i ^ bit) for i in range(lax.axis_size('dp'))])  75.7 us
    pallas_call x4, Pallas kernels, back_sum(): pl.pallas_call(functools.partial(back_sum_kernel, len(parts)), grid=(n //...  65.4 us
    all_to_all x2, blocking collectives, shards(): lax.all_to_all(v, ('strip', 'tensor'), 0, 0, tiled=True)  50.8 us
    ppermute x20, waiting for transfers between devices, shift(): return lax.ppermute(v, axis, pairs)  49.8 us
    ppermute x20, starting transfers between devices, shift(): return lax.ppermute(v, axis, pairs)  46.2 us
    pallas_call x2, Pallas kernels, conv7(): pl.pallas_call(functools.partial(conv7_kernel, rows, cols, back), grid=(i...  45.9 us
    pallas_call x4, Pallas kernels, tall(): pl.pallas_call(kernel, grid=(2 * steps,), in_specs=[pl.BlockSpec((m, bm),...  43.9 us
  transfers between devices with their start and end apart: 89, of which 37 were waited for; matrix products, arithmetic and copies ran while one was open for 18% of the time, Pallas kernels for 29%

profile of v4, /device:TPU:0, one launch (start us, length us, event | category | flops | bytes accessed | tf_op | source)
XLA Modules:
  0.0 974.9 jit_solution(15519278597585050489)
XLA Ops:
  52.2 26.3 %all-gather.18.cloned.1.call-done = bf16[8,192,768]{2,1,0:T(8,128)(2,1)} async-done(((bf16[2,192,768]{2,1,0:T(8,128)(2,1)}), bf16[8,192,768]{2,1,0:T(8,128)(2,1)}) %all-gather.18.cloned.1.call-update) | async-done | bytes 2359312 | tf_op jit(solution)/shard_map/all_gather | solution.py:129
  99.5 23.0 %depthwise.2 = f32[3,12,24,1536]{3,2,1,0:T(8,128)S(1)} custom-call(bf16[3,18,40,1536]{3,2,1,0:T(8,128)(2,1)S(1)} %pad_maximum_fusion.x_ref, f32[7,8,1536]{2,1,0:T(8,128)S(1)} %pad.4.k_ref), custom_call_target="tpu_custom_call" | custom-call | flops 1 | bytes 1 | tf_op jit(solution)/shard_map/depthwise/pallas_call | solution.py:395
  126.9 8.5 collective-permute-done.5.w_ref.refs_5_
  144.7 9.5 expand_gelu.4
  157.2 7.7 expand_gelu.5
  167.8 7.7 expand_gelu.6
  178.6 13.7 %collective-permute-done.9.refs_5_.w_ref = bf16[1536,768]{1,0:T(8,128)(2,1)S(1)} collective-permute-done((bf16[1536,768]{1,0:T(8,128)(2,1)S(1)}, bf16[1536,768]{1,0:T(8,128)(2,1)S(1)}, u32[]{:S(2)}, u32[]{:S(2)}) %collective-permute-start.9) | collective-permute-done | bytes 2359328 | tf_op jit(solution)/shard_map/ppermute | solution.py:28
  201.2 6.0 expand_gelu.7
  219.5 15.9 %reduce_sum.126 = bf16[864,1536]{1,0:T(8,128)(2,1)} custom-call(bf16[1728,768]{1,0:T(8,128)(2,1)} %copy-done.34, bf16[1728,768]{1,0:T(8,128)(2,1)} %copy-done.13, bf16[1728,768]{1,0:T(8,128)(2,1)} %copy-done.15, bf16[1728,768]{1,0:T(8,128)(2,1)} %copy-done.36, bf16[1536,768]{1,0:T(8,128)(2,1)} %bitcast.382, bf16[1536,768]{1,0:T(8,128)(2,1)} %copy-done.30, ...), custom_call_target="tpu_custom_call" | custom-call | flops 1 | bytes 1 | tf_op jit(solution)/shard_map/reduce_sum/pallas_call | solution.py:579
  237.1 16.8 %reduce_sum.125.here_ref = f32[864,1536]{1,0:T(8,128)} custom-call(bf16[1728,768]{1,0:T(8,128)(2,1)} %copy-done.34, bf16[1728,768]{1,0:T(8,128)(2,1)} %copy-done.13, bf16[1728,768]{1,0:T(8,128)(2,1)} %copy-done.15, bf16[1728,768]{1,0:T(8,128)(2,1)} %copy-done.36, bf16[1536,768]{1,0:T(8,128)(2,1)} %bitcast.383, bf16[1536,768]{1,0:T(8,128)(2,1)} %copy-done.30, ...), custom_call_target="tpu_custom_call" | custom-call | flops 1 | bytes 1 | tf_op jit(solution)/shard_map/reduce_sum/pallas_call | solution.py:579
  279.5 13.3 %collective-permute-done.14 = bf16[3,72,1536]{2,1,0:T(8,128)(2,1)} collective-permute-done((bf16[3,72,1536]{2,1,0:T(8,128)(2,1)}, bf16[3,72,1536]{2,1,0:T(8,128)(2,1)}, u32[]{:S(2)}, u32[]{:S(2)}) %collective-permute-start.14) | collective-permute-done | bytes 663584 | tf_op jit(solution)/shard_map/ppermute | solution.py:34
  349.9 19.4 %collective-permute-done.20.refs_1_ = bf16[2,1024,512]{2,1,0:T(8,128)(2,1)} collective-permute-done((bf16[2,1024,512]{2,1,0:T(8,128)(2,1)}, bf16[2,1024,512]{2,1,0:T(8,128)(2,1)}, u32[]{:S(2)}, u32[]{:S(2)}) %collective-permute-start.20) | collective-permute-done | bytes 2097184 | tf_op jit(solution)/shard_map/ppermute | solution.py:28
  375.9 9.1 all-to-all-done
  384.9 7.0 attention.1
  406.0 7.3 all-to-all-done.1
  420.4 11.6 %mlp.1 = (f32[432,1024]{1,0:T(8,128)S(1)}, f32[432,1024]{1,0:T(8,128)S(1)}, bf16[432,512]{1,0:T(8,128)(2,1)S(1)}, bf16[432,512]{1,0:T(8,128)(2,1)S(1)}, bf16[432...) custom-call(bf16[432,1024]{1,0:T(8,128)(2,1)S(1)} %constant_dynamic-, ...), custom_call_target="tpu_custom_call" | custom-call | flops 1 | bytes 1 | tf_op jit(solution)/shard_map/mlp/pallas_call | solution.py:652
  447.8 15.7 %all_to_all.25 = bf16[8,216,128]{2,1,0:T(8,128)(2,1)S(1)} all-to-all(bf16[8,216,128]{2,1,0:T(8,128)(2,1)S(1)} %copy-done.91), channel_id=1, replica_groups=mesh['dp'=4,'strip'=2,'tensor'=4] {'strip','tensor'}, dimensions={0} | all-to-all | bytes 884736 | tf_op jit(solution)/shard_map/all_to_all | solution.py:986
  463.6 10.9 %attention_back.1 = bf16[8,3,72,384]{3,2,1,0:T(8,128)(2,1)S(1)} custom-call(bf16[8,3,72,384]{3,2,1,0:T(8,128)(2,1)} %bitcast.47.qkv_ref, bf16[8,3,72,128]{3,2,1,0:T(8,128)(2,1)S(1)} %bitcast.403), custom_call_target="tpu_custom_call" | custom-call | flops 1 | bytes 1 | tf_op jit(solution)/shard_map/attention_back/pallas_call | solution.py:738
  474.6 35.1 %all_to_all.26 = bf16[8,3,72,384]{3,2,1,0:T(8,128)(2,1)S(1)} all-to-all(bf16[8,3,72,384]{3,2,1,0:T(8,128)(2,1)S(1)} %attention_back.1), channel_id=1, replica_groups=mesh['dp'=4,'strip'=2,'tensor'=4] {'strip','tensor'}, dimensions={0} | all-to-all | bytes 2654208 | tf_op jit(solution)/shard_map/all_to_all | solution.py:986
  589.7 6.8 add_convert_fusion
  614.9 11.7 %tall_near.2 = (bf16[2,768,768]{2,1,0:T(8,128)(2,1)}, bf16[2,768,768]{2,1,0:T(8,128)(2,1)}) custom-call(bf16[1728,1536]{1,0:T(8,128)(2,1)S(1)} %pad_maximum_fusion.3.a_ref, bf16[1728,768]{1,0:T(8,128)(2,1)S(1)} %copy-done.14, bf16[1728,768]{1,0:T(8,128)(2,1)S(1)} %copy-done.16, bf16[1728,768]{1,0:T(8,128)(2,1)S(1)} %copy-done.37), custom_call_target="tpu_custom_call" | custom-call | flops 1 | bytes 1 | tf_op jit(solution)/shard_map/tall_near/pallas_call | solution.py:612
  630.0 10.7 %tall_keep.2 = (bf16[2,768,768]{2,1,0:T(8,128)(2,1)S(1)}, bf16[2,768,768]{2,1,0:T(8,128)(2,1)S(1)}) custom-call(bf16[1728,1536]{1,0:T(8,128)(2,1)S(1)} %pad_maximum_fusion.3.a_ref, bf16[1728,768]{1,0:T(8,128)(2,1)S(1)} %copy-done.35, bf16[1728,768]{1,0:T(8,128)(2,1)S(1)} %copy-done.14, bf16[1728,768]{1,0:T(8,128)(2,1)S(1)} %copy-done.16), custom_call_target="tpu_custom_call" | custom-call | flops 1 | bytes 1 | tf_op jit(solution)/shard_map/tall_keep/pallas_call | solution.py:612
  660.3 10.7 %tall_near.3 = (bf16[2,768,768]{2,1,0:T(8,128)(2,1)S(1)}, bf16[2,768,768]{2,1,0:T(8,128)(2,1)S(1)}) custom-call(bf16[1728,1536]{1,0:T(8,128)(2,1)S(1)} %bitcast.376, bf16[1728,768]{1,0:T(8,128)(2,1)S(1)} %back_slope.5.refs_0_.refs_1_, bf16[1728,768]{1,0:T(8,128)(2,1)S(1)} %back_slope.6.refs_1_.refs_2_, bf16[1728,768]{1,0:T(8,128)(2,1)S(1)} %back_slope.7.refs_2_.refs_3_), custom_call_target="tpu_custom_call" | custom-call | flops 1 | bytes 1 | tf_op jit(solution)/shard_map/tall_near/pallas_call | solution.py:612
  673.8 10.9 %tall_keep.3 = (bf16[2,768,768]{2,1,0:T(8,128)(2,1)S(1)}, bf16[2,768,768]{2,1,0:T(8,128)(2,1)S(1)}) custom-call(bf16[1728,1536]{1,0:T(8,128)(2,1)S(1)} %bitcast.376, bf16[1728,768]{1,0:T(8,128)(2,1)S(1)} %back_slope.4.refs_0_, bf16[1728,768]{1,0:T(8,128)(2,1)S(1)} %back_slope.5.refs_0_.refs_1_, bf16[1728,768]{1,0:T(8,128)(2,1)S(1)} %back_slope.6.refs_1_.refs_2_), custom_call_target="tpu_custom_call" | custom-call | flops 1 | bytes 1 | tf_op jit(solution)/shard_map/tall_keep/pallas_call | solution.py:612
  688.1 15.9 %reduce_sum.127 = bf16[864,1536]{1,0:T(8,128)(2,1)} custom-call(bf16[1728,768]{1,0:T(8,128)(2,1)} %copy-done.17, bf16[1728,768]{1,0:T(8,128)(2,1)} %copy-done.4, bf16[1728,768]{1,0:T(8,128)(2,1)} %copy-done.5, bf16[1728,768]{1,0:T(8,128)(2,1)} %copy-done.18, bf16[1536,768]{1,0:T(8,128)(2,1)} %bitcast.6.w_ref.refs_4_, ...), custom_call_target="tpu_custom_call" | custom-call | flops 1 | bytes 1 | tf_op jit(solution)/shard_map/reduce_sum/pallas_call | solution.py:579
  707.5 16.9 %reduce_sum.128.here_ref = f32[864,1536]{1,0:T(8,128)} custom-call(bf16[1728,768]{1,0:T(8,128)(2,1)} %copy-done.17, bf16[1728,768]{1,0:T(8,128)(2,1)} %copy-done.4, bf16[1728,768]{1,0:T(8,128)(2,1)} %copy-done.5, bf16[1728,768]{1,0:T(8,128)(2,1)} %copy-done.18, bf16[1536,768]{1,0:T(8,128)(2,1)} %bitcast.6.w_ref.refs_4_, ...), custom_call_target="tpu_custom_call" | custom-call | flops 1 | bytes 1 | tf_op jit(solution)/shard_map/reduce_sum/pallas_call | solution.py:579
  736.5 6.2 norm_back.1
  743.3 22.6 %collective-permute-done.45.refs_3_.refs_4_ = bf16[2,768,768]{2,1,0:T(8,128)(2,1)} collective-permute-done((bf16[2,768,768]{2,1,0:T(8,128)(2,1)}, bf16[2,768,768]{2,1,0:T(8,128)(2,1)}, u32[]{:S(2)}, u32[]{:S(2)}) %collective-permute-start.45) | collective-permute-done | bytes 2359328 | tf_op jit(solution)/shard_map/ppermute | solution.py:28
  781.8 24.0 %tap_grad.1 = f32[7,8,1536]{2,1,0:T(8,128)S(1)} custom-call(bf16[3,18,40,1536]{3,2,1,0:T(8,128)(2,1)S(1)} %copy-done.7, bf16[3,12,24,1536]{3,2,1,0:T(8,128)(2,1)S(1)} %bitcast.390), custom_call_target="tpu_custom_call" | custom-call | flops 1 | bytes 1 | tf_op jit(solution)/shard_map/tap_grad/pallas_call | solution.py:437
  810.2 15.1 %collective-permute-done.49 = bf16[3,3,24,1536]{3,2,1,0:T(8,128)(2,1)} collective-permute-done((bf16[3,3,24,1536]{3,2,1,0:T(8,128)(2,1)}, bf16[3,3,24,1536]{3,2,1,0:T(8,128)(2,1)}, u32[]{:S(2)}, u32[]{:S(2)}) %collective-permute-start.49) | collective-permute-done | bytes 663584 | tf_op jit(solution)/shard_map/ppermute | solution.py:34
  855.3 23.0 %depthwise.3 = f32[3,12,24,1536]{3,2,1,0:T(8,128)S(1)} custom-call(bf16[3,18,40,1536]{3,2,1,0:T(8,128)(2,1)S(1)} %pad_maximum_fusion.1.x_ref, f32[7,8,1536]{2,1,0:T(8,128)S(1)} %copy-done.64), custom_call_target="tpu_custom_call" | custom-call | flops 1 | bytes 1 | tf_op jit(solution)/shard_map/depthwise/pallas_call | solution.py:395
  922.9 9.1 collective-permute-done.58
  (729 shorter events, 509.6 us)
Async XLA Ops:
  7.2 71.3 %all-gather.18.cloned.1.call-start = ((), (), s32[]{:S(2)}) async-start(), calls=%async_computation.16 | async-start | bytes 2949120 | tf_op jit(solution)/shard_map/all_gather | solution.py:129
  14.9 121.8 %all-gather.22.cloned.1.call-start = ((), (), s32[]{:S(2)}) async-start(), calls=%async_computation.18 | async-start | bytes 2949120 | tf_op jit(solution)/shard_map/all_gather | solution.py:129
  21.6 175.3 %all-gather.20.cloned.1.call-start = ((), (), s32[]{:S(2)}) async-start(), calls=%async_computation.17 | async-start | bytes 2949120 | tf_op jit(solution)/shard_map/all_gather | solution.py:129
  23.5 191.7 %all-gather.24.cloned.1.call-start = ((), (), s32[]{:S(2)}) async-start(), calls=%async_computation.19 | async-start | bytes 1474560 | tf_op jit(solution)/shard_map/all_gather | solution.py:129
  25.5 282.6 %all-gather.26.cloned.1.call-start = ((), (), s32[]{:S(2)}) async-start(), calls=%async_computation.20 | async-start | bytes 2621440 | tf_op jit(solution)/shard_map/all_gather | solution.py:185
  27.5 310.0 %all-gather.28.cloned.1.call-start = ((), (), s32[]{:S(2)}) async-start(), calls=%async_computation.21 | async-start | bytes 6488064 | tf_op jit(solution)/shard_map/all_gather | solution.py:290
  33.7 51.4 %collective-permute-start = (bf16[3,3,24,1536]{3,2,1,0:T(8,128)(2,1)}, bf16[3,3,24,1536]{3,2,1,0:T(8,128)(2,1)}, u32[]{:S(2)}, u32[]{:S(2)}) collective-permute-start(bf16[3,3,24,1536]{3,2,1,0:T(8,128)(2,1)} %get-tuple-element.448), channel_id=1, source_target_pairs={{0,1},{1,2},{2,3},{4,5},{5,6},{6,7},{8,9},{9,10},{10,11},{12,13},{... | collective-permute-start | bytes 1990664 | tf_op jit(solution)/shard_map/ppermute | solution.py:34
  39.4 45.7 %collective-permute-start.2 = (bf16[3,3,24,1536]{3,2,1,0:T(8,128)(2,1)}, bf16[3,3,24,1536]{3,2,1,0:T(8,128)(2,1)}, u32[]{:S(2)}, u32[]{:S(2)}) collective-permute-start(bf16[3,3,24,1536]{3,2,1,0:T(8,128)(2,1)} %get-tuple-element.449), channel_id=1, source_target_pairs={{1,0},{2,1},{3,2},{5,4},{6,5},{7,6},{9,8},{10,9},{11,10},{13,12},{... | collective-permute-start | bytes 1990664 | tf_op jit(solution)/shard_map/ppermute | solution.py:34
  42.4 372.4 %all-gather.30.cloned.1.call-start = ((), (), s32[]{:S(2)}) async-start(), calls=%async_computation.22 | async-start | bytes 2162688 | tf_op jit(solution)/shard_map/all_gather | solution.py:290
  82.0 53.5 %collective-permute-start.5 = (bf16[1536,768]{1,0:T(8,128)(2,1)}, bf16[1536,768]{1,0:T(8,128)(2,1)}, u32[]{:S(2)}, u32[]{:S(2)}) collective-permute-start(bf16[1536,768]{1,0:T(8,128)(2,1)} %bitcast.6.w_ref.refs_4_), channel_id=1, source_target_pairs={{0,8},{8,0},{16,24},{24,16},{1,9},{9,1},{17,25},{25,17},{2,10},{10... | collective-permute-start | bytes 7077896 | tf_op jit(solution)/shard_map/ppermute | solution.py:28
  83.7 53.0 %collective-permute-start.6 = (bf16[1536,768]{1,0:T(8,128)(2,1)}, bf16[1536,768]{1,0:T(8,128)(2,1)}, u32[]{:S(2)}, u32[]{:S(2)}) collective-permute-start(bf16[1536,768]{1,0:T(8,128)(2,1)} %bitcast.6.w_ref.refs_4_), channel_id=1, source_target_pairs={{0,16},{8,24},{16,0},{24,8},{1,17},{9,25},{17,1},{25,9},{2,18},{10... | collective-permute-start | bytes 7077896 | tf_op jit(solution)/shard_map/ppermute | solution.py:28
  138.5 53.7 %collective-permute-start.9 = (bf16[1536,768]{1,0:T(8,128)(2,1)S(1)}, bf16[1536,768]{1,0:T(8,128)(2,1)S(1)}, u32[]{:S(2)}, u32[]{:S(2)}) collective-permute-start(bf16[1536,768]{1,0:T(8,128)(2,1)S(1)} %bitcast.380), channel_id=1, source_target_pairs={{0,8},{8,0},{16,24},{24,16},{1,9},{9,1},{17,25},{25,17},{2,10},{10... | collective-permute-start | bytes 7077896 | tf_op jit(solution)/shard_map/ppermute | solution.py:28
  139.1 55.6 %collective-permute-start.10 = (bf16[1536,768]{1,0:T(8,128)(2,1)S(1)}, bf16[1536,768]{1,0:T(8,128)(2,1)S(1)}, u32[]{:S(2)}, u32[]{:S(2)}) collective-permute-start(bf16[1536,768]{1,0:T(8,128)(2,1)S(1)} %bitcast.381), channel_id=1, source_target_pairs={{0,16},{8,24},{16,0},{24,8},{1,17},{9,25},{17,1},{25,9},{2,18},{10... | collective-permute-start | bytes 7077896 | tf_op jit(solution)/shard_map/ppermute | solution.py:28
  318.9 50.5 %collective-permute-start.20 = (bf16[2,1024,512]{2,1,0:T(8,128)(2,1)}, bf16[2,1024,512]{2,1,0:T(8,128)(2,1)}, u32[]{:S(2)}, u32[]{:S(2)}) collective-permute-start(bf16[2,1024,512]{2,1,0:T(8,128)(2,1)} %pad_maximum_fusion.5.refs_0_), channel_id=1, source_target_pairs={{0,8},{8,0},{16,24},{24,16},{1,9},{9,1},{17,25},{25,17},{2,10},{10... | collective-permute-start | bytes 6291464 | tf_op jit(solution)/shard_map/ppermute | solution.py:28
  320.4 52.7 %collective-permute-start.21 = (bf16[2,1024,512]{2,1,0:T(8,128)(2,1)}, bf16[2,1024,512]{2,1,0:T(8,128)(2,1)}, u32[]{:S(2)}, u32[]{:S(2)}) collective-permute-start(bf16[2,1024,512]{2,1,0:T(8,128)(2,1)} %pad_maximum_fusion.5.refs_0_), channel_id=1, source_target_pairs={{0,16},{8,24},{16,0},{24,8},{1,17},{9,25},{17,1},{25,9},{2,18},{10... | collective-permute-start | bytes 6291464 | tf_op jit(solution)/shard_map/ppermute | solution.py:28
  345.1 39.8 %all-to-all-start = ((bf16[8,216,384]{2,1,0:T(8,128)(2,1)}), bf16[8,216,384]{2,1,0:T(8,128)(2,1)}, u32[]{:S(2)}, u32[]{:S(2)}) async-start(bf16[8,216,384]{2,1,0:T(8,128)(2,1)} %copy-done.81), calls=%async_computation | async-start | bytes 2654208 | tf_op jit(solution)/shard_map/all_to_all | solution.py:986
  396.8 141.5 %reduce-scatter.6.cloned.1.call-start = ((), (), s32[]{:S(2)}) async-start(), calls=%async_computation.10 | async-start | bytes 10485760 | tf_op jit(solution)/shard_map/reduce_scatter | solution.py:196
  446.9 283.9 %reduce-scatter.8.cloned.1.call-start = ((), (), s32[]{:S(2)}) async-start(), calls=%async_computation.12 | async-start | bytes 7208960 | tf_op jit(solution)/shard_map/reduce_scatter | solution.py:247
  596.6 180.5 %all-gather.16.cloned.1.call-start = ((), (), s32[]{:S(2)}) async-start(), calls=%async_computation.11 | async-start | bytes 4423680 | tf_op jit(solution)/shard_map/all_gather | solution.py:1107
  609.7 225.7 %reduce-scatter.12.cloned.1.call-start = ((), (), s32[]{:S(2)}) async-start(), calls=%async_computation.14 | async-start | bytes 2949120 | tf_op jit(solution)/shard_map/reduce_scatter | solution.py:163
  626.6 58.1 %collective-permute-start.41 = (bf16[2,768,768]{2,1,0:T(8,128)(2,1)}, bf16[2,768,768]{2,1,0:T(8,128)(2,1)S(1)}, u32[]{:S(2)}, u32[]{:S(2)}) collective-permute-start(bf16[2,768,768]{2,1,0:T(8,128)(2,1)} %get-tuple-element.205), channel_id=1, source_target_pairs={{0,16},{8,24},{16,0},{24,8},{1,17},{9,25},{17,1},{25,9},{2,18},{10... | collective-permute-start | bytes 7077896 | tf_op jit(solution)/shard_map/ppermute | solution.py:28
  627.9 56.8 %collective-permute-start.40 = (bf16[2,768,768]{2,1,0:T(8,128)(2,1)}, bf16[2,768,768]{2,1,0:T(8,128)(2,1)S(1)}, u32[]{:S(2)}, u32[]{:S(2)}) collective-permute-start(bf16[2,768,768]{2,1,0:T(8,128)(2,1)} %get-tuple-element.188), channel_id=1, source_target_pairs={{0,8},{8,0},{16,24},{24,16},{1,9},{9,1},{17,25},{25,17},{2,10},{10... | collective-permute-start | bytes 7077896 | tf_op jit(solution)/shard_map/ppermute | solution.py:28
  704.0 61.8 %collective-permute-start.45 = (bf16[2,768,768]{2,1,0:T(8,128)(2,1)}, bf16[2,768,768]{2,1,0:T(8,128)(2,1)}, u32[]{:S(2)}, u32[]{:S(2)}) collective-permute-start(bf16[2,768,768]{2,1,0:T(8,128)(2,1)} %copy-done.106), channel_id=1, source_target_pairs={{0,16},{8,24},{16,0},{24,8},{1,17},{9,25},{17,1},{25,9},{2,18},{10... | collective-permute-start | bytes 7077896 | tf_op jit(solution)/shard_map/ppermute | solution.py:28
  705.5 60.3 %collective-permute-start.39 = (bf16[2,768,768]{2,1,0:T(8,128)(2,1)}, bf16[2,768,768]{2,1,0:T(8,128)(2,1)}, u32[]{:S(2)}, u32[]{:S(2)}) collective-permute-start(bf16[2,768,768]{2,1,0:T(8,128)(2,1)} %copy-done.105), channel_id=1, source_target_pairs={{0,8},{8,0},{16,24},{24,16},{1,9},{9,1},{17,25},{25,17},{2,10},{10... | collective-permute-start | bytes 7077896 | tf_op jit(solution)/shard_map/ppermute | solution.py:28
  730.7 159.5 %reduce-scatter.10.cloned.1.call-start = ((), (), s32[]{:S(2)}) async-start(), calls=%async_computation.13 | async-start | bytes 2949120 | tf_op jit(solution)/shard_map/reduce_scatter | solution.py:163
  775.8 49.5 %collective-permute-start.49 = (bf16[3,3,24,1536]{3,2,1,0:T(8,128)(2,1)}, bf16[3,3,24,1536]{3,2,1,0:T(8,128)(2,1)}, u32[]{:S(2)}, u32[]{:S(2)}) collective-permute-start(bf16[3,3,24,1536]{3,2,1,0:T(8,128)(2,1)} %get-tuple-element.447), channel_id=1, source_target_pairs={{1,0},{2,1},{3,2},{5,4},{6,5},{7,6},{9,8},{10,9},{11,10},{13,12},{... | collective-permute-start | bytes 1990664 | tf_op jit(solution)/shard_map/ppermute | solution.py:34
  836.6 107.4 %reduce-scatter.14.cloned.1.call-start = ((), (), s32[]{:S(2)}) async-start(), calls=%async_computation.15 | async-start | bytes 2621440 | tf_op jit(solution)/shard_map/reduce_scatter | solution.py:202
  836.9 41.4 %collective-permute-start.67 = (bf16[704,256]{1,0:T(8,128)(2,1)S(1)}, bf16[704,256]{1,0:T(8,128)(2,1)S(1)}, u32[]{:S(2)}, u32[]{:S(2)}) collective-permute-start(bf16[704,256]{1,0:T(8,128)(2,1)S(1)} %get-tuple-element.478), channel_id=1, source_target_pairs={{0,16},{8,24},{16,0},{24,8},{1,17},{9,25},{17,1},{25,9},{2,18},{10... | collective-permute-start | bytes 1081352 | tf_op jit(solution)/shard_map/ppermute | solution.py:28
  840.0 38.4 %collective-permute-start.68 = (bf16[704,256]{1,0:T(8,128)(2,1)S(1)}, bf16[704,256]{1,0:T(8,128)(2,1)S(1)}, u32[]{:S(2)}, u32[]{:S(2)}) collective-permute-start(bf16[704,256]{1,0:T(8,128)(2,1)S(1)} %get-tuple-element.477), channel_id=1, source_target_pairs={{0,24},{8,16},{16,8},{24,0},{1,25},{9,17},{17,9},{25,1},{2,26},{10... | collective-permute-start | bytes 1081352 | tf_op jit(solution)/shard_map/ppermute | solution.py:28
  902.8 47.2 %collective-permute-start.60 = (bf16[2,192,768]{2,1,0:T(8,128)(2,1)}, bf16[2,192,768]{2,1,0:T(8,128)(2,1)}, u32[]{:S(2)}, u32[]{:S(2)}) collective-permute-start(bf16[2,192,768]{2,1,0:T(8,128)(2,1)} %pad_maximum_fusion.21), channel_id=1, source_target_pairs={{0,24},{8,16},{16,8},{24,0},{1,25},{9,17},{17,9},{25,1},{2,26},{10... | collective-permute-start | bytes 1769480 | tf_op jit(solution)/shard_map/ppermute | solution.py:28
  904.7 45.3 %collective-permute-start.61 = (bf16[2,192,768]{2,1,0:T(8,128)(2,1)}, bf16[2,192,768]{2,1,0:T(8,128)(2,1)}, u32[]{:S(2)}, u32[]{:S(2)}) collective-permute-start(bf16[2,192,768]{2,1,0:T(8,128)(2,1)} %pad_maximum_fusion.21), channel_id=1, source_target_pairs={{0,16},{8,24},{16,0},{24,8},{1,17},{9,25},{17,1},{25,9},{2,18},{10... | collective-permute-start | bytes 1769480 | tf_op jit(solution)/shard_map/ppermute | solution.py:28
  904.9 45.2 %collective-permute-start.62 = (bf16[2,192,768]{2,1,0:T(8,128)(2,1)}, bf16[2,192,768]{2,1,0:T(8,128)(2,1)}, u32[]{:S(2)}, u32[]{:S(2)}) collective-permute-start(bf16[2,192,768]{2,1,0:T(8,128)(2,1)} %pad_maximum_fusion.21), channel_id=1, source_target_pairs={{0,8},{8,0},{16,24},{24,16},{1,9},{9,1},{17,25},{25,17},{2,10},{10... | collective-permute-start | bytes 1769480 | tf_op jit(solution)/shard_map/ppermute | solution.py:28
  (224 other events, 2623.5 us)
Sparse Core Ops, SparseCore 0:
  15.1 63.4 all-gather.17
  80.7 52.9 all-gather.21
  135.2 49.2 all-gather.19
  186.0 29.2 all-gather.23
  217.3 45.0 all-gather.25
  265.1 71.0 all-gather.27
  339.0 75.7 all-gather.29
  447.0 84.8 reduce-scatter.5
  596.7 100.8 reduce-scatter.7
  699.1 70.5 all-gather.15
  772.6 58.6 reduce-scatter.11
  836.8 45.2 reduce-scatter.9
  887.1 46.1 reduce-scatter.13

commit v5 on v4

--- a/solution.py
+++ b/solution.py
@@ -570,11 +570,10 @@
     out_ref[...] = total.astype(out_ref.dtype)
 
 
-def back_sum(parts, weights, first, rows, dtype):
+def back_sum(parts, weights, first, rows, dtype, bn=512, most=432):
     n = weights[0].shape[0]
     ks = [w.shape[1] for w in weights]
-    bm = row_block(rows, 432)
-    bn = 512
+    bm = row_block(rows, most)
     skip = first // bm
     return pl.pallas_call(
         functools.partial(back_sum_kernel, len(parts)),
@@ -951,9 +950,9 @@
     acts, slopes = zip(*pairs)
     if count > 1:
         reduce_pieces.append(dp_across(reduce_near, reduce_z(1, acts[2]), acts[2]))
-    branch_sent = back_sum(acts, reduce_pieces, cells, cells, BF)
+    branch_sent = back_sum(acts, reduce_pieces, cells, cells, BF, 256, cells)
     branch_there = core_swap(branch_sent)
-    branch_here = back_sum(acts, reduce_pieces, 0, cells, F32)
+    branch_here = back_sum(acts, reduce_pieces, 0, cells, F32, 256, cells)
     branch, map_low = map_value_rows(
         branch_here, branch_there, masked.reshape(cells, channels), cell_mask.reshape(cells, 1), layer_scale
     )

time: 983 us -> 989 us (level)
  waiting for transfers between devices: 213 us -> 224 us
  transfers between devices with their start and end apart: 89 -> 89, of which waited for: 37 -> 37; matrix products, arithmetic and copies ran while one was open for 18% -> 18% of each run, Pallas kernels for 29% -> 28%
where the time goes in v5:
time: 989 us; the launch traced here: 980 us
  Pallas kernels  298 us (30%)
  waiting for transfers between devices  224 us (23%)
  local copies, waits for them, and re-layouts  158 us (16%)
  other arithmetic  107 us (11%)
  starting transfers between devices  106 us (11%)
  blocking collectives  51.8 us (5%)
  between operations  17.3 us (2%)
  matrix products  16.9 us (2%)
    unnamed x366, local copies, waits for them, and re-layouts  82.8 us
    ppermute x30, waiting for transfers between devices, dp_swap(): lax.ppermute(v, 'dp', [(i, i ^ bit) for i in range(lax.axis_size('dp'))])  68.5 us
    pallas_call x4, Pallas kernels, back_sum(): pl.pallas_call(functools.partial(back_sum_kernel, len(parts)), grid=(n //...  60.2 us
    ppermute x20, waiting for transfers between devices, shift(): return lax.ppermute(v, axis, pairs)  53 us
    all_to_all x2, blocking collectives, shards(): lax.all_to_all(v, ('strip', 'tensor'), 0, 0, tiled=True)  51.8 us
    ppermute x20, starting transfers between devices, shift(): return lax.ppermute(v, axis, pairs)  46.7 us
    pallas_call x2, Pallas kernels, conv7(): pl.pallas_call(functools.partial(conv7_kernel, rows, cols, back), grid=(i...  45.9 us
    pallas_call x4, Pallas kernels, tall(): pl.pallas_call(kernel, grid=(2 * steps,), in_specs=[pl.BlockSpec((m, bm),...  43.9 us
  transfers between devices with their start and end apart: 89, of which 37 were waited for; matrix products, arithmetic and copies ran while one was open for 18% of the time, Pallas kernels for 28%

profile of v5, /device:TPU:0, one launch (start us, length us, event | category | flops | bytes accessed | tf_op | source)
XLA Modules:
  0.0 979.8 jit_solution(15620781605928408500)
XLA Ops:
  52.2 26.3 %all-gather.18.cloned.1.call-done = bf16[8,192,768]{2,1,0:T(8,128)(2,1)} async-done(((bf16[2,192,768]{2,1,0:T(8,128)(2,1)}), bf16[8,192,768]{2,1,0:T(8,128)(2,1)}) %all-gather.18.cloned.1.call-update) | async-done | bytes 2359312 | tf_op jit(solution)/shard_map/all_gather | solution.py:129
  99.5 23.0 %depthwise.2 = f32[3,12,24,1536]{3,2,1,0:T(8,128)S(1)} custom-call(bf16[3,18,40,1536]{3,2,1,0:T(8,128)(2,1)S(1)} %pad_maximum_fusion.x_ref, f32[7,8,1536]{2,1,0:T(8,128)S(1)} %pad.4.k_ref), custom_call_target="tpu_custom_call" | custom-call | flops 1 | bytes 1 | tf_op jit(solution)/shard_map/depthwise/pallas_call | solution.py:395
  126.9 8.5 collective-permute-done.5.w_ref.refs_5_
  144.7 9.5 expand_gelu.4
  157.2 7.7 expand_gelu.5
  167.8 7.7 expand_gelu.6
  178.6 13.7 %collective-permute-done.9.refs_5_.w_ref = bf16[1536,768]{1,0:T(8,128)(2,1)S(1)} collective-permute-done((bf16[1536,768]{1,0:T(8,128)(2,1)S(1)}, bf16[1536,768]{1,0:T(8,128)(2,1)S(1)}, u32[]{:S(2)}, u32[]{:S(2)}) %collective-permute-start.9) | collective-permute-done | bytes 2359328 | tf_op jit(solution)/shard_map/ppermute | solution.py:28
  219.5 13.5 %reduce_sum.126 = bf16[864,1536]{1,0:T(8,128)(2,1)} custom-call(bf16[1728,768]{1,0:T(8,128)(2,1)} %copy-done.34, bf16[1728,768]{1,0:T(8,128)(2,1)} %copy-done.13, bf16[1728,768]{1,0:T(8,128)(2,1)} %copy-done.15, bf16[1728,768]{1,0:T(8,128)(2,1)} %copy-done.36, bf16[1536,768]{1,0:T(8,128)(2,1)} %bitcast.382, bf16[1536,768]{1,0:T(8,128)(2,1)} %copy-done.30, ...), custom_call_target="tpu_custom_call" | custom-call | flops 1 | bytes 1 | tf_op jit(solution)/shard_map/reduce_sum/pallas_call | solution.py:578
  234.8 14.0 %reduce_sum.125.here_ref = f32[864,1536]{1,0:T(8,128)} custom-call(bf16[1728,768]{1,0:T(8,128)(2,1)} %copy-done.34, bf16[1728,768]{1,0:T(8,128)(2,1)} %copy-done.13, bf16[1728,768]{1,0:T(8,128)(2,1)} %copy-done.15, bf16[1728,768]{1,0:T(8,128)(2,1)} %copy-done.36, bf16[1536,768]{1,0:T(8,128)(2,1)} %bitcast.383, bf16[1536,768]{1,0:T(8,128)(2,1)} %copy-done.30, ...), custom_call_target="tpu_custom_call" | custom-call | flops 1 | bytes 1 | tf_op jit(solution)/shard_map/reduce_sum/pallas_call | solution.py:578
  274.4 13.3 %collective-permute-done.14 = bf16[3,72,1536]{2,1,0:T(8,128)(2,1)} collective-permute-done((bf16[3,72,1536]{2,1,0:T(8,128)(2,1)}, bf16[3,72,1536]{2,1,0:T(8,128)(2,1)}, u32[]{:S(2)}, u32[]{:S(2)}) %collective-permute-start.14) | collective-permute-done | bytes 663584 | tf_op jit(solution)/shard_map/ppermute | solution.py:34
  318.3 8.0 collective-permute-done.19
  353.0 16.6 %collective-permute-done.20.refs_1_ = bf16[2,1024,512]{2,1,0:T(8,128)(2,1)} collective-permute-done((bf16[2,1024,512]{2,1,0:T(8,128)(2,1)}, bf16[2,1024,512]{2,1,0:T(8,128)(2,1)}, u32[]{:S(2)}, u32[]{:S(2)}) %collective-permute-start.20) | collective-permute-done | bytes 2097184 | tf_op jit(solution)/shard_map/ppermute | solution.py:28
  376.1 10.4 %all-to-all-done = bf16[8,216,384]{2,1,0:T(8,128)(2,1)} async-done(((bf16[8,216,384]{2,1,0:T(8,128)(2,1)}), bf16[8,216,384]{2,1,0:T(8,128)(2,1)}, u32[]{:S(2)}, u32[]{:S(2)}) %all-to-all-start) | async-done | bytes 1327136 | tf_op jit(solution)/shard_map/all_to_all | solution.py:985
  386.5 7.0 attention.1
  403.1 13.6 %all-to-all-done.1 = bf16[8,3,72,128]{3,2,1,0:T(8,128)(2,1)} async-done(((bf16[8,3,72,128]{3,2,1,0:T(8,128)(2,1)}), bf16[8,3,72,128]{3,2,1,0:T(8,128)(2,1)}, u32[]{:S(2)}, u32[]{:S(2)}) %all-to-all-start.1) | async-done | bytes 442400 | tf_op jit(solution)/shard_map/all_to_all | solution.py:985
  424.8 11.6 %mlp.1 = (f32[432,1024]{1,0:T(8,128)S(1)}, f32[432,1024]{1,0:T(8,128)S(1)}, bf16[432,512]{1,0:T(8,128)(2,1)S(1)}, bf16[432,512]{1,0:T(8,128)(2,1)S(1)}, bf16[432...) custom-call(bf16[432,1024]{1,0:T(8,128)(2,1)S(1)} %constant_dynamic-, ...), custom_call_target="tpu_custom_call" | custom-call | flops 1 | bytes 1 | tf_op jit(solution)/shard_map/mlp/pallas_call | solution.py:651
  452.3 16.7 %all_to_all.25 = bf16[8,216,128]{2,1,0:T(8,128)(2,1)S(1)} all-to-all(bf16[8,216,128]{2,1,0:T(8,128)(2,1)S(1)} %copy-done.91), channel_id=1, replica_groups=mesh['dp'=4,'strip'=2,'tensor'=4] {'strip','tensor'}, dimensions={0} | all-to-all | bytes 884736 | tf_op jit(solution)/shard_map/all_to_all | solution.py:985
  468.9 10.9 %attention_back.1 = bf16[8,3,72,384]{3,2,1,0:T(8,128)(2,1)S(1)} custom-call(bf16[8,3,72,384]{3,2,1,0:T(8,128)(2,1)} %bitcast.47.qkv_ref, bf16[8,3,72,128]{3,2,1,0:T(8,128)(2,1)S(1)} %bitcast.403), custom_call_target="tpu_custom_call" | custom-call | flops 1 | bytes 1 | tf_op jit(solution)/shard_map/attention_back/pallas_call | solution.py:737
  479.9 35.1 %all_to_all.26 = bf16[8,3,72,384]{3,2,1,0:T(8,128)(2,1)S(1)} all-to-all(bf16[8,3,72,384]{3,2,1,0:T(8,128)(2,1)S(1)} %attention_back.1), channel_id=1, replica_groups=mesh['dp'=4,'strip'=2,'tensor'=4] {'strip','tensor'}, dimensions={0} | all-to-all | bytes 2654208 | tf_op jit(solution)/shard_map/all_to_all | solution.py:985
  595.1 6.8 add_convert_fusion
  620.0 11.7 %tall_near.2 = (bf16[2,768,768]{2,1,0:T(8,128)(2,1)}, bf16[2,768,768]{2,1,0:T(8,128)(2,1)}) custom-call(bf16[1728,1536]{1,0:T(8,128)(2,1)S(1)} %pad_maximum_fusion.3.a_ref, bf16[1728,768]{1,0:T(8,128)(2,1)S(1)} %copy-done.14, bf16[1728,768]{1,0:T(8,128)(2,1)S(1)} %copy-done.16, bf16[1728,768]{1,0:T(8,128)(2,1)S(1)} %copy-done.37), custom_call_target="tpu_custom_call" | custom-call | flops 1 | bytes 1 | tf_op jit(solution)/shard_map/tall_near/pallas_call | solution.py:611
  634.6 10.7 %tall_keep.2 = (bf16[2,768,768]{2,1,0:T(8,128)(2,1)S(1)}, bf16[2,768,768]{2,1,0:T(8,128)(2,1)S(1)}) custom-call(bf16[1728,1536]{1,0:T(8,128)(2,1)S(1)} %pad_maximum_fusion.3.a_ref, bf16[1728,768]{1,0:T(8,128)(2,1)S(1)} %copy-done.35, bf16[1728,768]{1,0:T(8,128)(2,1)S(1)} %copy-done.14, bf16[1728,768]{1,0:T(8,128)(2,1)S(1)} %copy-done.16), custom_call_target="tpu_custom_call" | custom-call | flops 1 | bytes 1 | tf_op jit(solution)/shard_map/tall_keep/pallas_call | solution.py:611
  664.9 10.7 %tall_near.3 = (bf16[2,768,768]{2,1,0:T(8,128)(2,1)S(1)}, bf16[2,768,768]{2,1,0:T(8,128)(2,1)S(1)}) custom-call(bf16[1728,1536]{1,0:T(8,128)(2,1)S(1)} %bitcast.376, bf16[1728,768]{1,0:T(8,128)(2,1)S(1)} %back_slope.5.refs_0_.refs_1_, bf16[1728,768]{1,0:T(8,128)(2,1)S(1)} %back_slope.6.refs_1_.refs_2_, bf16[1728,768]{1,0:T(8,128)(2,1)S(1)} %back_slope.7.refs_2_.refs_3_), custom_call_target="tpu_custom_call" | custom-call | flops 1 | bytes 1 | tf_op jit(solution)/shard_map/tall_near/pallas_call | solution.py:611
  678.4 10.9 %tall_keep.3 = (bf16[2,768,768]{2,1,0:T(8,128)(2,1)S(1)}, bf16[2,768,768]{2,1,0:T(8,128)(2,1)S(1)}) custom-call(bf16[1728,1536]{1,0:T(8,128)(2,1)S(1)} %bitcast.376, bf16[1728,768]{1,0:T(8,128)(2,1)S(1)} %back_slope.4.refs_0_, bf16[1728,768]{1,0:T(8,128)(2,1)S(1)} %back_slope.5.refs_0_.refs_1_, bf16[1728,768]{1,0:T(8,128)(2,1)S(1)} %back_slope.6.refs_1_.refs_2_), custom_call_target="tpu_custom_call" | custom-call | flops 1 | bytes 1 | tf_op jit(solution)/shard_map/tall_keep/pallas_call | solution.py:611
  693.3 15.9 %reduce_sum.127 = bf16[864,1536]{1,0:T(8,128)(2,1)} custom-call(bf16[1728,768]{1,0:T(8,128)(2,1)} %copy-done.17, bf16[1728,768]{1,0:T(8,128)(2,1)} %copy-done.4, bf16[1728,768]{1,0:T(8,128)(2,1)} %copy-done.5, bf16[1728,768]{1,0:T(8,128)(2,1)} %copy-done.18, bf16[1536,768]{1,0:T(8,128)(2,1)} %bitcast.6.w_ref.refs_4_, ...), custom_call_target="tpu_custom_call" | custom-call | flops 1 | bytes 1 | tf_op jit(solution)/shard_map/reduce_sum/pallas_call | solution.py:578
  712.1 16.9 %reduce_sum.128.here_ref = f32[864,1536]{1,0:T(8,128)} custom-call(bf16[1728,768]{1,0:T(8,128)(2,1)} %copy-done.17, bf16[1728,768]{1,0:T(8,128)(2,1)} %copy-done.4, bf16[1728,768]{1,0:T(8,128)(2,1)} %copy-done.5, bf16[1728,768]{1,0:T(8,128)(2,1)} %copy-done.18, bf16[1536,768]{1,0:T(8,128)(2,1)} %bitcast.6.w_ref.refs_4_, ...), custom_call_target="tpu_custom_call" | custom-call | flops 1 | bytes 1 | tf_op jit(solution)/shard_map/reduce_sum/pallas_call | solution.py:578
  741.0 6.2 norm_back.1
  747.9 23.0 %collective-permute-done.45.refs_3_.refs_4_ = bf16[2,768,768]{2,1,0:T(8,128)(2,1)} collective-permute-done((bf16[2,768,768]{2,1,0:T(8,128)(2,1)}, bf16[2,768,768]{2,1,0:T(8,128)(2,1)}, u32[]{:S(2)}, u32[]{:S(2)}) %collective-permute-start.45) | collective-permute-done | bytes 2359328 | tf_op jit(solution)/shard_map/ppermute | solution.py:28
  786.8 24.0 %tap_grad.1 = f32[7,8,1536]{2,1,0:T(8,128)S(1)} custom-call(bf16[3,18,40,1536]{3,2,1,0:T(8,128)(2,1)S(1)} %copy-done.7, bf16[3,12,24,1536]{3,2,1,0:T(8,128)(2,1)S(1)} %bitcast.390), custom_call_target="tpu_custom_call" | custom-call | flops 1 | bytes 1 | tf_op jit(solution)/shard_map/tap_grad/pallas_call | solution.py:437
  815.1 15.3 %collective-permute-done.49 = bf16[3,3,24,1536]{3,2,1,0:T(8,128)(2,1)} collective-permute-done((bf16[3,3,24,1536]{3,2,1,0:T(8,128)(2,1)}, bf16[3,3,24,1536]{3,2,1,0:T(8,128)(2,1)}, u32[]{:S(2)}, u32[]{:S(2)}) %collective-permute-start.49) | collective-permute-done | bytes 663584 | tf_op jit(solution)/shard_map/ppermute | solution.py:34
  860.4 23.0 %depthwise.3 = f32[3,12,24,1536]{3,2,1,0:T(8,128)S(1)} custom-call(bf16[3,18,40,1536]{3,2,1,0:T(8,128)(2,1)S(1)} %pad_maximum_fusion.1.x_ref, f32[7,8,1536]{2,1,0:T(8,128)S(1)} %copy-done.64), custom_call_target="tpu_custom_call" | custom-call | flops 1 | bytes 1 | tf_op jit(solution)/shard_map/depthwise/pallas_call | solution.py:395
  927.9 9.1 collective-permute-done.58
  (729 shorter events, 511.5 us)
Async XLA Ops:
  7.2 71.3 %all-gather.18.cloned.1.call-start = ((), (), s32[]{:S(2)}) async-start(), calls=%async_computation.16 | async-start | bytes 2949120 | tf_op jit(solution)/shard_map/all_gather | solution.py:129
  14.9 121.8 %all-gather.22.cloned.1.call-start = ((), (), s32[]{:S(2)}) async-start(), calls=%async_computation.18 | async-start | bytes 2949120 | tf_op jit(solution)/shard_map/all_gather | solution.py:129
  21.6 175.3 %all-gather.20.cloned.1.call-start = ((), (), s32[]{:S(2)}) async-start(), calls=%async_computation.17 | async-start | bytes 2949120 | tf_op jit(solution)/shard_map/all_gather | solution.py:129
  23.5 191.7 %all-gather.24.cloned.1.call-start = ((), (), s32[]{:S(2)}) async-start(), calls=%async_computation.19 | async-start | bytes 1474560 | tf_op jit(solution)/shard_map/all_gather | solution.py:129
  25.5 277.0 %all-gather.26.cloned.1.call-start = ((), (), s32[]{:S(2)}) async-start(), calls=%async_computation.20 | async-start | bytes 2621440 | tf_op jit(solution)/shard_map/all_gather | solution.py:185
  27.5 313.6 %all-gather.28.cloned.1.call-start = ((), (), s32[]{:S(2)}) async-start(), calls=%async_computation.21 | async-start | bytes 6488064 | tf_op jit(solution)/shard_map/all_gather | solution.py:290
  33.7 51.4 %collective-permute-start = (bf16[3,3,24,1536]{3,2,1,0:T(8,128)(2,1)}, bf16[3,3,24,1536]{3,2,1,0:T(8,128)(2,1)}, u32[]{:S(2)}, u32[]{:S(2)}) collective-permute-start(bf16[3,3,24,1536]{3,2,1,0:T(8,128)(2,1)} %get-tuple-element.448), channel_id=1, source_target_pairs={{0,1},{1,2},{2,3},{4,5},{5,6},{6,7},{8,9},{9,10},{10,11},{12,13},{... | collective-permute-start | bytes 1990664 | tf_op jit(solution)/shard_map/ppermute | solution.py:34
  39.4 45.7 %collective-permute-start.2 = (bf16[3,3,24,1536]{3,2,1,0:T(8,128)(2,1)}, bf16[3,3,24,1536]{3,2,1,0:T(8,128)(2,1)}, u32[]{:S(2)}, u32[]{:S(2)}) collective-permute-start(bf16[3,3,24,1536]{3,2,1,0:T(8,128)(2,1)} %get-tuple-element.449), channel_id=1, source_target_pairs={{1,0},{2,1},{3,2},{5,4},{6,5},{7,6},{9,8},{10,9},{11,10},{13,12},{... | collective-permute-start | bytes 1990664 | tf_op jit(solution)/shard_map/ppermute | solution.py:34
  42.4 376.8 %all-gather.30.cloned.1.call-start = ((), (), s32[]{:S(2)}) async-start(), calls=%async_computation.22 | async-start | bytes 2162688 | tf_op jit(solution)/shard_map/all_gather | solution.py:290
  82.0 53.5 %collective-permute-start.5 = (bf16[1536,768]{1,0:T(8,128)(2,1)}, bf16[1536,768]{1,0:T(8,128)(2,1)}, u32[]{:S(2)}, u32[]{:S(2)}) collective-permute-start(bf16[1536,768]{1,0:T(8,128)(2,1)} %bitcast.6.w_ref.refs_4_), channel_id=1, source_target_pairs={{0,8},{8,0},{16,24},{24,16},{1,9},{9,1},{17,25},{25,17},{2,10},{10... | collective-permute-start | bytes 7077896 | tf_op jit(solution)/shard_map/ppermute | solution.py:28
  83.7 53.0 %collective-permute-start.6 = (bf16[1536,768]{1,0:T(8,128)(2,1)}, bf16[1536,768]{1,0:T(8,128)(2,1)}, u32[]{:S(2)}, u32[]{:S(2)}) collective-permute-start(bf16[1536,768]{1,0:T(8,128)(2,1)} %bitcast.6.w_ref.refs_4_), channel_id=1, source_target_pairs={{0,16},{8,24},{16,0},{24,8},{1,17},{9,25},{17,1},{25,9},{2,18},{10... | collective-permute-start | bytes 7077896 | tf_op jit(solution)/shard_map/ppermute | solution.py:28
  138.5 53.7 %collective-permute-start.9 = (bf16[1536,768]{1,0:T(8,128)(2,1)S(1)}, bf16[1536,768]{1,0:T(8,128)(2,1)S(1)}, u32[]{:S(2)}, u32[]{:S(2)}) collective-permute-start(bf16[1536,768]{1,0:T(8,128)(2,1)S(1)} %bitcast.380), channel_id=1, source_target_pairs={{0,8},{8,0},{16,24},{24,16},{1,9},{9,1},{17,25},{25,17},{2,10},{10... | collective-permute-start | bytes 7077896 | tf_op jit(solution)/shard_map/ppermute | solution.py:28
  139.1 55.6 %collective-permute-start.10 = (bf16[1536,768]{1,0:T(8,128)(2,1)S(1)}, bf16[1536,768]{1,0:T(8,128)(2,1)S(1)}, u32[]{:S(2)}, u32[]{:S(2)}) collective-permute-start(bf16[1536,768]{1,0:T(8,128)(2,1)S(1)} %bitcast.381), channel_id=1, source_target_pairs={{0,16},{8,24},{16,0},{24,8},{1,17},{9,25},{17,1},{25,9},{2,18},{10... | collective-permute-start | bytes 7077896 | tf_op jit(solution)/shard_map/ppermute | solution.py:28
  313.3 56.3 %collective-permute-start.20 = (bf16[2,1024,512]{2,1,0:T(8,128)(2,1)}, bf16[2,1024,512]{2,1,0:T(8,128)(2,1)}, u32[]{:S(2)}, u32[]{:S(2)}) collective-permute-start(bf16[2,1024,512]{2,1,0:T(8,128)(2,1)} %pad_maximum_fusion.5.refs_0_), channel_id=1, source_target_pairs={{0,8},{8,0},{16,24},{24,16},{1,9},{9,1},{17,25},{25,17},{2,10},{10... | collective-permute-start | bytes 6291464 | tf_op jit(solution)/shard_map/ppermute | solution.py:28
  314.8 58.5 %collective-permute-start.21 = (bf16[2,1024,512]{2,1,0:T(8,128)(2,1)}, bf16[2,1024,512]{2,1,0:T(8,128)(2,1)}, u32[]{:S(2)}, u32[]{:S(2)}) collective-permute-start(bf16[2,1024,512]{2,1,0:T(8,128)(2,1)} %pad_maximum_fusion.5.refs_0_), channel_id=1, source_target_pairs={{0,16},{8,24},{16,0},{24,8},{1,17},{9,25},{17,1},{25,9},{2,18},{10... | collective-permute-start | bytes 6291464 | tf_op jit(solution)/shard_map/ppermute | solution.py:28
  348.7 37.8 %all-to-all-start = ((bf16[8,216,384]{2,1,0:T(8,128)(2,1)}), bf16[8,216,384]{2,1,0:T(8,128)(2,1)}, u32[]{:S(2)}, u32[]{:S(2)}) async-start(bf16[8,216,384]{2,1,0:T(8,128)(2,1)} %copy-done.81), calls=%async_computation | async-start | bytes 2654208 | tf_op jit(solution)/shard_map/all_to_all | solution.py:985
  398.3 145.3 %reduce-scatter.6.cloned.1.call-start = ((), (), s32[]{:S(2)}) async-start(), calls=%async_computation.10 | async-start | bytes 10485760 | tf_op jit(solution)/shard_map/reduce_scatter | solution.py:196
  451.3 284.1 %reduce-scatter.8.cloned.1.call-start = ((), (), s32[]{:S(2)}) async-start(), calls=%async_computation.12 | async-start | bytes 7208960 | tf_op jit(solution)/shard_map/reduce_scatter | solution.py:247
  602.0 180.1 %all-gather.16.cloned.1.call-start = ((), (), s32[]{:S(2)}) async-start(), calls=%async_computation.11 | async-start | bytes 4423680 | tf_op jit(solution)/shard_map/all_gather | solution.py:1106
  614.9 225.6 %reduce-scatter.12.cloned.1.call-start = ((), (), s32[]{:S(2)}) async-start(), calls=%async_computation.14 | async-start | bytes 2949120 | tf_op jit(solution)/shard_map/reduce_scatter | solution.py:163
  631.7 57.6 %collective-permute-start.41 = (bf16[2,768,768]{2,1,0:T(8,128)(2,1)}, bf16[2,768,768]{2,1,0:T(8,128)(2,1)S(1)}, u32[]{:S(2)}, u32[]{:S(2)}) collective-permute-start(bf16[2,768,768]{2,1,0:T(8,128)(2,1)} %get-tuple-element.205), channel_id=1, source_target_pairs={{0,16},{8,24},{16,0},{24,8},{1,17},{9,25},{17,1},{25,9},{2,18},{10... | collective-permute-start | bytes 7077896 | tf_op jit(solution)/shard_map/ppermute | solution.py:28
  633.3 56.0 %collective-permute-start.40 = (bf16[2,768,768]{2,1,0:T(8,128)(2,1)}, bf16[2,768,768]{2,1,0:T(8,128)(2,1)S(1)}, u32[]{:S(2)}, u32[]{:S(2)}) collective-permute-start(bf16[2,768,768]{2,1,0:T(8,128)(2,1)} %get-tuple-element.188), channel_id=1, source_target_pairs={{0,8},{8,0},{16,24},{24,16},{1,9},{9,1},{17,25},{25,17},{2,10},{10... | collective-permute-start | bytes 7077896 | tf_op jit(solution)/shard_map/ppermute | solution.py:28
  709.1 61.7 %collective-permute-start.45 = (bf16[2,768,768]{2,1,0:T(8,128)(2,1)}, bf16[2,768,768]{2,1,0:T(8,128)(2,1)}, u32[]{:S(2)}, u32[]{:S(2)}) collective-permute-start(bf16[2,768,768]{2,1,0:T(8,128)(2,1)} %copy-done.106), channel_id=1, source_target_pairs={{0,16},{8,24},{16,0},{24,8},{1,17},{9,25},{17,1},{25,9},{2,18},{10... | collective-permute-start | bytes 7077896 | tf_op jit(solution)/shard_map/ppermute | solution.py:28
  710.8 60.1 %collective-permute-start.39 = (bf16[2,768,768]{2,1,0:T(8,128)(2,1)}, bf16[2,768,768]{2,1,0:T(8,128)(2,1)}, u32[]{:S(2)}, u32[]{:S(2)}) collective-permute-start(bf16[2,768,768]{2,1,0:T(8,128)(2,1)} %copy-done.105), channel_id=1, source_target_pairs={{0,8},{8,0},{16,24},{24,16},{1,9},{9,1},{17,25},{25,17},{2,10},{10... | collective-permute-start | bytes 7077896 | tf_op jit(solution)/shard_map/ppermute | solution.py:28
  735.3 160.1 %reduce-scatter.10.cloned.1.call-start = ((), (), s32[]{:S(2)}) async-start(), calls=%async_computation.13 | async-start | bytes 2949120 | tf_op jit(solution)/shard_map/reduce_scatter | solution.py:163
  780.8 49.6 %collective-permute-start.49 = (bf16[3,3,24,1536]{3,2,1,0:T(8,128)(2,1)}, bf16[3,3,24,1536]{3,2,1,0:T(8,128)(2,1)}, u32[]{:S(2)}, u32[]{:S(2)}) collective-permute-start(bf16[3,3,24,1536]{3,2,1,0:T(8,128)(2,1)} %get-tuple-element.447), channel_id=1, source_target_pairs={{1,0},{2,1},{3,2},{5,4},{6,5},{7,6},{9,8},{10,9},{11,10},{13,12},{... | collective-permute-start | bytes 1990664 | tf_op jit(solution)/shard_map/ppermute | solution.py:34
  841.7 107.3 %reduce-scatter.14.cloned.1.call-start = ((), (), s32[]{:S(2)}) async-start(), calls=%async_computation.15 | async-start | bytes 2621440 | tf_op jit(solution)/shard_map/reduce_scatter | solution.py:202
  842.8 40.6 %collective-permute-start.67 = (bf16[704,256]{1,0:T(8,128)(2,1)S(1)}, bf16[704,256]{1,0:T(8,128)(2,1)S(1)}, u32[]{:S(2)}, u32[]{:S(2)}) collective-permute-start(bf16[704,256]{1,0:T(8,128)(2,1)S(1)} %get-tuple-element.478), channel_id=1, source_target_pairs={{0,16},{8,24},{16,0},{24,8},{1,17},{9,25},{17,1},{25,9},{2,18},{10... | collective-permute-start | bytes 1081352 | tf_op jit(solution)/shard_map/ppermute | solution.py:28
  845.9 38.4 %collective-permute-start.68 = (bf16[704,256]{1,0:T(8,128)(2,1)S(1)}, bf16[704,256]{1,0:T(8,128)(2,1)S(1)}, u32[]{:S(2)}, u32[]{:S(2)}) collective-permute-start(bf16[704,256]{1,0:T(8,128)(2,1)S(1)} %get-tuple-element.477), channel_id=1, source_target_pairs={{0,24},{8,16},{16,8},{24,0},{1,25},{9,17},{17,9},{25,1},{2,26},{10... | collective-permute-start | bytes 1081352 | tf_op jit(solution)/shard_map/ppermute | solution.py:28
  908.0 47.0 %collective-permute-start.60 = (bf16[2,192,768]{2,1,0:T(8,128)(2,1)}, bf16[2,192,768]{2,1,0:T(8,128)(2,1)}, u32[]{:S(2)}, u32[]{:S(2)}) collective-permute-start(bf16[2,192,768]{2,1,0:T(8,128)(2,1)} %pad_maximum_fusion.21), channel_id=1, source_target_pairs={{0,24},{8,16},{16,8},{24,0},{1,25},{9,17},{17,9},{25,1},{2,26},{10... | collective-permute-start | bytes 1769480 | tf_op jit(solution)/shard_map/ppermute | solution.py:28
  909.7 45.3 %collective-permute-start.61 = (bf16[2,192,768]{2,1,0:T(8,128)(2,1)}, bf16[2,192,768]{2,1,0:T(8,128)(2,1)}, u32[]{:S(2)}, u32[]{:S(2)}) collective-permute-start(bf16[2,192,768]{2,1,0:T(8,128)(2,1)} %pad_maximum_fusion.21), channel_id=1, source_target_pairs={{0,16},{8,24},{16,0},{24,8},{1,17},{9,25},{17,1},{25,9},{2,18},{10... | collective-permute-start | bytes 1769480 | tf_op jit(solution)/shard_map/ppermute | solution.py:28
  910.1 45.0 %collective-permute-start.62 = (bf16[2,192,768]{2,1,0:T(8,128)(2,1)}, bf16[2,192,768]{2,1,0:T(8,128)(2,1)}, u32[]{:S(2)}, u32[]{:S(2)}) collective-permute-start(bf16[2,192,768]{2,1,0:T(8,128)(2,1)} %pad_maximum_fusion.21), channel_id=1, source_target_pairs={{0,8},{8,0},{16,24},{24,16},{1,9},{9,1},{17,25},{25,17},{2,10},{10... | collective-permute-start | bytes 1769480 | tf_op jit(solution)/shard_map/ppermute | solution.py:28
  (224 other events, 2668.7 us)
Sparse Core Ops, SparseCore 0:
  15.1 63.4 all-gather.17
  80.7 52.9 all-gather.21
  135.2 49.2 all-gather.19
  186.0 29.2 all-gather.23
  217.3 45.0 all-gather.25
  265.1 75.9 all-gather.27
  343.9 75.2 all-gather.29
  451.4 86.1 reduce-scatter.5
  602.1 100.0 reduce-scatter.7
  703.7 70.5 all-gather.15
  777.2 59.0 reduce-scatter.11
  841.8 45.4 reduce-scatter.9
  892.2 45.9 reduce-scatter.13
